TPU v7x, 32 devices: a whole 2x2x4 slice. The times are simulated.
32 devices in a mesh: gx: 4 (over z), gy: 4 (over y, core), gz: 2 (over x).
Axes of the slice: x: 2, y: 2, z: 4, core: 2. Of those that a mesh axis runs over, the one named last changes fastest.
Arguments:
- patch_state: float32 [4, 2, 32, 5, 1024], P('gx', 'gz', 'gy'), as said below
- coarse_boxes: float32 [8, 5, 4096], P(('gx', 'gz')), as said below
- new_owner: int32 [4, 2, 32, 1], P('gx', 'gz'), may hold values from 0 to 3; in each aligned block of 8 rows (0 to 7, 8 to 15, ..., all dimensions but the last counted through in order) at most 4 rows name the same one
- neighbors: int32 [4, 2, 32, 4], P('gx', 'gz'), may hold values from -1 to 31, as said below
- coarse_box: int32 [4, 2, 32, 4], P('gx', 'gz'), may hold values from 0 to 7
- coarse_start: int32 [4, 2, 32, 4], P('gx', 'gz'), may hold values from 0 to 3135
Outputs:
- advanced: float32 [4, 2, 64, 5, 1024], P('gx', 'gz', 'gy')
Inputs may be any that keep to these rules, and one draw needn't show every extreme that they name: `new_owner`: no device hands more than 4 of its patches to one new owner. `neighbors`: a patch of the same group by its number before redistribution, or -1 where the side borders the coarse level. `patch_state`: density and pressure positive. `coarse_boxes`: density and pressure positive.
All inputs are finite; a program needn't handle non-finite values.
Results may differ from a plain program's by a relative error of at most 0.0003.
Values sent between devices are 32-bit elements; how exact they have to be, the bound alone decides.
No kernel may reach another device: no remote copies, remote signals or barrier semaphores. Data moves between devices by JAX's collectives and lax.ppermute only.
A program may use at most 64 MiB of HBM per device.

v0:
```python
import functools

import jax
import jax.numpy as jnp
from jax import lax
from jax.experimental import pallas as pl
from jax.experimental.pallas import tpu as pltpu
from jax.sharding import PartitionSpec as P

FIELDS = 5
PX = 32
BOX = 64
SUB = 8
LANE = 128
HALF = PX // 2
STRIDE = BOX - HALF + 1
BOX_ROWS = BOX * BOX // LANE
ROWS = FIELDS * SUB
VX, PRESSURE, WAVE_X, VY, WAVE_Y = range(FIELDS, FIELDS + 5)
X_PLANES = WAVE_X + 1
PLANES = WAVE_Y + 1
FULL = PLANES * SUB
SIDE = X_PLANES * SUB
heat_ratio = 1.4
courant = 0.3
WEST, EAST, SOUTH, NORTH = range(4)
BATCH = 8


def power_of_two(n):
    return n & (n - 1) == 0


def masks_of(n):
    return [n >> (i + 1) for i in range(n.bit_length() - 1)]


def primitive(u):
    inverse = 1.0 / u[0]
    vx, vy, vz = u[1] * inverse, u[2] * inverse, u[3] * inverse
    kinetic = u[1] * (0.5 * vx) + u[2] * (0.5 * vy) + u[3] * (0.5 * vz)
    pressure = (heat_ratio - 1.0) * (u[4] - kinetic)
    sound = jnp.sqrt(heat_ratio * pressure * inverse)
    return vx, vy, pressure, sound


def with_primitives(u):
    vx, vy, pressure, sound = primitive(u)
    return u + [vx, pressure, 0.5 * (jnp.abs(vx) + sound), vy, 0.5 * (jnp.abs(vy) + sound)]


def half_flux(u, moving, pressure, normal):
    half = 0.5 * moving
    flux = [u[f] * half for f in range(FIELDS)]
    flux[normal] = flux[normal] + 0.5 * pressure
    flux[4] = flux[4] + pressure * half
    return flux


def lane_of():
    return lax.broadcasted_iota(jnp.int32, (SUB, LANE), 1)


def sub_of():
    return lax.broadcasted_iota(jnp.int32, (SUB, LANE), 0)


def take_lanes(x, lanes):
    return jnp.take_along_axis(x, lanes, axis=1, mode="promise_in_bounds")


def below(x, low_lanes):
    turned = pltpu.roll(x, PX, 1)
    return jnp.where(low_lanes, pltpu.roll(turned, 1, 0), turned)


def above(x, high_lanes):
    turned = pltpu.roll(x, LANE - PX, 1)
    return jnp.where(high_lanes, pltpu.roll(turned, SUB - 1, 0), turned)


def x_part(own, west, east):
    lane = lane_of()
    col = lane & (PX - 1)
    first, last = col == 0, col == PX - 1
    swap = lane + (PX - 1) - 2 * col
    ghost = [take_lanes(jnp.where(last, w, e), swap) for w, e in zip(west, east)]
    u, wave = own[:FIELDS], own[WAVE_X]
    flux = half_flux(u, own[VX], own[PRESSURE], 1)
    gflux = half_flux(ghost[:FIELDS], ghost[VX], ghost[PRESSURE], 1)
    gwave = ghost[WAVE_X]
    face = jnp.maximum(jnp.where(first, gwave, pltpu.roll(wave, 1, 1)), wave)
    border = jnp.maximum(gwave, wave)
    part = []
    for f in range(FIELDS):
        left_u = jnp.where(first, ghost[f], pltpu.roll(u[f], 1, 1))
        left_flux = jnp.where(first, gflux[f], pltpu.roll(flux[f], 1, 1))
        west_flux = left_flux + flux[f] - face * (u[f] - left_u)
        east_flux = flux[f] + gflux[f] - border * (ghost[f] - u[f])
        part.append(west_flux - jnp.where(last, east_flux, pltpu.roll(west_flux, LANE - 1, 1)))
    return part


def y_border(row0, row31, south, north):
    lane, sub = lane_of(), sub_of()
    low = lane < LANE // 2
    cell = [jnp.where(low, a, b) for a, b in zip(row0, row31)]
    ghost = [take_lanes(jnp.where(low, n, s), lane ^ (LANE - PX)) for s, n in zip(south, north)]

    def flux(u, moving, pressure):
        half = 0.5 * moving
        return u * half + pressure * jnp.where(sub == 2, 0.5, jnp.where(sub == 4, half, 0.0))

    both = flux(*ghost[:3]) + flux(*cell[:3])
    spread = jnp.maximum(ghost[3], cell[3]) * (cell[0] - ghost[0])
    return both - jnp.where(low, spread, -spread)


def y_part(own, border):
    lane, sub = lane_of(), sub_of()
    low, high = lane < PX, lane >= LANE - PX
    first, last = low & (sub == 0), high & (sub == SUB - 1)
    u, wave = own[:FIELDS], own[WAVE_Y]
    flux = half_flux(u, own[VY], own[PRESSURE], 2)
    face = jnp.maximum(below(wave, low), wave)
    part = []
    for f in range(FIELDS):
        south_flux = below(flux[f], low) + flux[f] - face * (u[f] - below(u[f], low))
        edge = jnp.broadcast_to(border[f : f + 1, :], (SUB, LANE))
        south_flux = jnp.where(first, edge, south_flux)
        part.append(south_flux - jnp.where(last, edge, above(south_flux, high)))
    return part


def pack_kernel(
    count, tiles, rows, patches, mesh_sizes, patch_ref, box_ref, which_ref, start_ref, state_ref, pay_ref, meta_ref, scr
):
    n_gx, n_gz = mesh_sizes
    for f in range(FIELDS):
        for s in range(SUB):
            at = (f * SUB + s) * count
            scr[at : at + count, :] = patch_ref[0, 0, f, :, s * LANE : (s + 1) * LANE]
    top = None
    for p in range(count):
        u = []
        for f in range(FIELDS):
            plane = scr[pl.ds(f * SUB * count + p, SUB, stride=count), :]
            state_ref[p * ROWS + f * SUB : p * ROWS + (f + 1) * SUB, :] = plane
            u.append(plane)
        vx, vy, pressure, sound = primitive(u)
        wave = jnp.maximum(jnp.abs(vx), jnp.abs(vy)) + sound
        top = wave if top is None else jnp.maximum(top, wave)
    me = lax.axis_index("gy")
    pieces = [box_ref[pl.ds(f * BOX_ROWS + me * tiles, tiles), :] for f in range(FIELDS)]
    for k in range(n_gx * n_gz):
        for f in range(FIELDS):
            at = k * rows + f * tiles
            pay_ref[at : at + tiles, :] = pieces[f]
        pay_ref[(k + 1) * rows - SUB : (k + 1) * rows, :] = top

    start = start_ref[0, 0]
    row = lax.shift_right_logical(start * 2675, 17)
    offset = BOX * (row & 1) + start - row * STRIDE
    tile = lax.shift_right_logical(row, 1)
    which = which_ref[0, 0]
    near = tile - me * tiles
    mine = (near >= 0) & (near < tiles)
    patch = lax.broadcasted_iota(jnp.int32, start.shape, 1)
    meta_ref[0:4, 0:patches] = which * rows + jnp.where(mine, near, 0)
    meta_ref[4:8, 0:patches] = (HALF * (patch & (SUB - 1)) - offset) & (LANE - 1)
    meta_ref[8:12, 0:patches] = jnp.where(mine, patch & (SUB - 1), -1)


def strip_kernel(parts, group, rows, tiles, patches, meta_ref, pay_ref, out_ref):
    top = None
    for k in range(parts):
        wave = pay_ref[(k + 1) * rows - SUB : (k + 1) * rows, :]
        top = wave if top is None else jnp.maximum(top, wave)
    block = lane_of() // HALF
    lines = 4 * patches // SUB
    total = FIELDS * lines + SUB
    for v in range(lines):
        side, first = v * SUB // patches, v * SUB % patches
        acc = jnp.zeros((SUB, LANE), jnp.float32)
        for m in range(SUB):
            p = first + m
            at, shift, fills = meta_ref[side, p], meta_ref[4 + side, p], meta_ref[8 + side, p]
            strip = pay_ref[pl.ds(at, FIELDS, stride=tiles), :]
            strip = jnp.concatenate([strip, jnp.zeros((SUB - FIELDS, LANE), jnp.float32)], axis=0)
            acc = jnp.where(block == fills, pltpu.roll(strip, shift, 1), acc)
        for k in range(group):
            out_ref[pl.ds(k * total + v, FIELDS, stride=lines), :] = acc[:FIELDS, :]
    for k in range(group):
        out_ref[(k + 1) * total - SUB : (k + 1) * total, :] = top


def step_kernel(sources, count, patches, slots, around_ref, owner_ref, *refs):
    group = len(sources)
    state_refs, strip_ref, out_ref = refs[:group], refs[group], refs[group + 1]
    cells, cells_one, strips, placed, own_patch, own_slot = refs[group + 2 :]
    me = lax.axis_index("gy")
    lines = 4 * patches // SUB
    capacity = slots // group
    side_base = patches * FULL
    row_base = side_base + 2 * patches * SIDE

    held = jnp.int32(0)
    for i in range(BATCH):
        own_patch[slots + i] = 0
    for source in range(group):
        rank = jnp.int32(0)
        for i in range(count):
            hit = owner_ref[0, 0, 0, source * count + i] == me
            own_patch[held] = source * count + i
            own_slot[held] = source * capacity + rank
            step = jnp.where(hit, 1, 0)
            held, rank = held + step, rank + step

    def prepare(k):
        for i in range(count):
            u = [state_refs[k][i * ROWS + f * SUB : i * ROWS + (f + 1) * SUB, :] for f in range(FIELDS)]
            first = pl.multiple_of((sources[k](me) * count + i) * FULL, SUB)
            for q, plane in enumerate(with_primitives(u)):
                cells[pl.ds(first + q * SUB, SUB), :] = plane

    for k in range(group):
        prepare(k)

    length = FIELDS * lines + SUB

    def joined(at, join):
        return functools.reduce(join, [strip_ref[k * length + at : k * length + at + SUB, :] for k in range(group)])

    for h in range(lines // SUB):
        u = [joined(f * lines + h * SUB, jnp.add) for f in range(FIELDS)]
        planes = with_primitives(u)
        for q in range(PLANES):
            strips[q * lines + h * SUB : q * lines + (h + 1) * SUB, :] = planes[q]
    time_step = courant / jnp.max(joined(FIELDS * lines, jnp.maximum))
    lane, sub = lane_of(), sub_of()
    down = 2 * sub + lane // (2 * PX)
    along = HALF * sub + (lane & (PX - 1)) // 2

    def wide(q, v, pick):
        row = jnp.broadcast_to(strips[pl.ds(q * lines + v, 1), :], (SUB, LANE))
        return take_lanes(row, pick)

    def coarse_sides(v, carry):
        for m in range(SUB):
            first = pl.multiple_of(side_base + (v * SUB + m) * SIDE, SUB)
            made = [wide(q, v, HALF * m + down) for q in range(X_PLANES)]
            for q in range(X_PLANES):
                cells[pl.ds(first + q * SUB, SUB), :] = made[q]
                cells_one[pl.ds(first + q * SUB, SUB), :] = made[q]
        return carry

    lax.fori_loop(0, lines // 2, coarse_sides, 0)

    def coarse_rows(v, carry):
        first = pl.multiple_of(row_base + v * FULL, SUB)
        made = [wide(q, lines // 2 + v, along) for q in range(PLANES)]
        for q in range(PLANES):
            cells[pl.ds(first + q * SUB, SUB), :] = made[q]
            cells_one[pl.ds(first + q * SUB, SUB), :] = made[q]
        return carry

    lax.fori_loop(0, lines // 2, coarse_rows, 0)

    def tendencies(ref, ps):
        loaded = []
        for p in ps:
            near = [around_ref[0, 0, side, p] for side in range(4)]
            first = p * FULL
            bases = [
                pl.multiple_of(
                    jnp.where(near[side] >= 0, near[side] * FULL, side_base + (side * patches + p) * SIDE), SUB
                )
                for side in (WEST, EAST)
            ]

            def facing(side, row):
                line = (side - SOUTH) * patches + p
                at_coarse = row_base + line // SUB * FULL + line % SUB
                return jnp.where(near[side] >= 0, near[side] * FULL + row, at_coarse)

            def rows_at(at):
                return [ref[pl.ds(at, SUB, stride=SUB), :]] + [
                    jnp.broadcast_to(ref[pl.ds(at + q * SUB, 1), :], (SUB, LANE)) for q in (VY, PRESSURE, WAVE_Y)
                ]

            own = [ref[pl.ds(pl.multiple_of(first + q * SUB, SUB), SUB), :] for q in range(PLANES)]
            west, east = [
                [ref[pl.ds(pl.multiple_of(base + q * SUB, SUB), SUB), :] for q in range(X_PLANES)] for base in bases
            ]
            border = [
                rows_at(at)
                for at in (first, first + SUB - 1, facing(SOUTH, SUB - 1), facing(NORTH, 0))
            ]
            loaded.append((own, west, east, border))
        out = []
        for own, west, east, border in loaded:
            across = x_part(own, west, east)
            along = y_part(own, y_border(*border))
            out.append((own, [a + b for a, b in zip(across, along)]))
        return out

    def first_section(i, carry):
        ps = [i * BATCH + b for b in range(BATCH)]
        made = []
        for own, change in tendencies(cells, ps):
            made.append(with_primitives([own[f] + time_step * change[f] for f in range(FIELDS)]))
        for p, planes in zip(ps, made):
            first = pl.multiple_of(p * FULL, SUB)
            for q in range(PLANES):
                cells_one[pl.ds(first + q * SUB, SUB), :] = planes[q]
        return carry

    lax.fori_loop(0, patches // BATCH, first_section, 0)

    placed[...] = jnp.zeros_like(placed)

    def second_section(i, carry):
        ps = [own_patch[i * BATCH + b] for b in range(BATCH)]
        ps = [jnp.where(i * BATCH + b < held, p, 0) for b, p in enumerate(ps)]
        made = []
        for p, (own, change) in zip(ps, tendencies(cells_one, ps)):
            first = pl.multiple_of(p * FULL, SUB)
            old = [cells[pl.ds(first + f * SUB, SUB), :] for f in range(FIELDS)]
            made.append([0.5 * old[f] + 0.5 * (own[f] + time_step * change[f]) for f in range(FIELDS)])
        for b in range(BATCH):
            slot = jnp.where(i * BATCH + b < held, own_slot[i * BATCH + b], slots)
            for f in range(FIELDS):
                at = (f * (slots // SUB + 1) + slot // SUB) * (SUB * SUB) + slot % SUB
                placed[pl.ds(at, SUB, stride=SUB), :] = made[b][f]
        return carry

    lax.fori_loop(0, (held + BATCH - 1) // BATCH, second_section, 0)
    for f in range(FIELDS):
        for t in range(slots // SUB):
            for s in range(SUB):
                at = ((f * (slots // SUB + 1) + t) * SUB + s) * SUB
                out_ref[0, 0, f, t * SUB : (t + 1) * SUB, s * LANE : (s + 1) * LANE] = placed[at : at + SUB, :]


def per_device(patch_state, coarse_boxes, new_owner, neighbors, coarse_box, coarse_start):
    count = patch_state.shape[2]
    n_gx, n_gz, group = lax.axis_size("gx"), lax.axis_size("gz"), lax.axis_size("gy")
    parts = n_gx * n_gz
    patches = count * group
    lines = 4 * patches // SUB
    slots = group * max(2, 2 * count // group)
    tiles = BOX_ROWS // group
    rows = -(-tiles * FIELDS // SUB) * SUB + SUB
    vmem = pl.BlockSpec(memory_space=pltpu.VMEM)
    smem = pl.BlockSpec(memory_space=pltpu.SMEM)
    f32 = jnp.float32

    def sides_first(x):
        return jnp.swapaxes(x, 2, 3)

    state, payload, meta = pl.pallas_call(
        functools.partial(pack_kernel, count, tiles, rows, patches, (n_gx, n_gz)),
        out_shape=(
            jax.ShapeDtypeStruct((count * ROWS, LANE), f32),
            jax.ShapeDtypeStruct((parts * rows, LANE), f32),
            jax.ShapeDtypeStruct((16, max(LANE, patches)), jnp.int32),
        ),
        in_specs=[vmem] * 4,
        out_specs=(vmem,) * 3,
        scratch_shapes=[pltpu.VMEM((FIELDS * SUB * count, LANE), f32)],
        name="pack",
    )(
        sides_first(patch_state),
        coarse_boxes.reshape(FIELDS * BOX_ROWS, LANE),
        sides_first(coarse_box),
        sides_first(coarse_start),
    )

    payload = lax.all_to_all(payload, ("gx", "gz"), split_axis=0, concat_axis=0, tiled=True)

    states, sources = [state], [lambda me: me]
    for mask in masks_of(group):
        perm = [(i, i ^ mask) for i in range(group)]
        states = states + [lax.ppermute(x, "gy", perm) for x in states]
        sources = sources + [lambda me, f=f, mask=mask: f(me) ^ mask for f in sources]

    strip = pl.pallas_call(
        functools.partial(strip_kernel, parts, group, rows, tiles, patches),
        out_shape=jax.ShapeDtypeStruct((group * (FIELDS * lines + SUB), LANE), f32),
        in_specs=[smem, vmem],
        out_specs=vmem,
        name="strips",
    )(meta, payload)

    strip = lax.all_to_all(strip, "gy", split_axis=0, concat_axis=0, tiled=True)

    place_rows = patches * FULL + 2 * patches * SIDE + lines // 2 * FULL
    out = pl.pallas_call(
        functools.partial(step_kernel, sources, count, patches, slots),
        out_shape=jax.ShapeDtypeStruct((1, 1, FIELDS, slots, SUB * LANE), f32),
        in_specs=[smem, smem] + [vmem] * (group + 1),
        out_specs=vmem,
        scratch_shapes=[
            pltpu.VMEM((place_rows, LANE), f32),
            pltpu.VMEM((place_rows, LANE), f32),
            pltpu.VMEM((PLANES * lines, LANE), f32),
            pltpu.VMEM((FIELDS * (slots // SUB + 1) * SUB * SUB, LANE), f32),
            pltpu.SMEM((slots + BATCH,), jnp.int32),
            pltpu.SMEM((slots + BATCH,), jnp.int32),
        ],
        compiler_params=pltpu.CompilerParams(vmem_limit_bytes=56 * 1024 * 1024),
        name="step",
    )(sides_first(neighbors), sides_first(new_owner), *states, strip)
    return sides_first(out)


def solution(mesh):
    in_specs = (
        P("gx", "gz", "gy", None, None),
        P(("gx", "gz"), None, None),
        P("gx", "gz", None, None),
        P("gx", "gz", None, None),
        P("gx", "gz", None, None),
        P("gx", "gz", None, None),
    )
    out_specs = P("gx", "gz", "gy", None, None)
    return jax.shard_map(
        per_device, mesh=mesh, in_specs=in_specs, out_specs=out_specs, check_vma=False
    )
```

profile of v0, /device:TPU:4, one launch (start us, length us, event | category | flops | bytes accessed | tf_op | source)
XLA Modules:
  0.0 52.0 jit_solution(9933177376484698033)
XLA Ops:
  0.0 1.7 %pack.1 = (f32[320,128]{1,0:T(8,128)}, f32[384,128]{1,0:T(8,128)}, s32[16,128]{1,0:T(8,128)}) custom-call(f32[1,1,5,8,1024]{4,3,2,1,0:T(8,128)} %bitcast.15, f32[160,128]{1,0:T(8,128)} %bitcast.16, s32[1,1,4,32]{3,2,1,0:T(4,128)} %bitcast.17, s32[1,1,4,32]{3,2,1,0:T(4,128)} %bitcast.18), custom_call_target="tpu_custom_call" | custom-call | tf_op jit(solution)/shard_map/pack/pallas_call | solution.py:361
  1.7 0.0 copy-start.2
  1.7 5.9 %all-to-all-start = ((f32[8,48,128]{2,1,0:T(8,128)}), f32[8,48,128]{2,1,0:T(8,128)S(1)}, u32[]{:S(2)}, u32[]{:S(2)}) async-start(f32[8,48,128]{2,1,0:T(8,128)} %bitcast.14), calls=%async_computation | async-start | bytes 393216 | tf_op jit(solution)/shard_map/all_to_all | solution.py:379
  7.7 0.0 copy-done.2
  7.7 0.6 %collective-permute-start = (f32[320,128]{1,0:T(8,128)S(1)}, f32[320,128]{1,0:T(8,128)S(1)}, u32[]{:S(2)}, u32[]{:S(2)}) collective-permute-start(f32[320,128]{1,0:T(8,128)S(1)} %copy-done.2), channel_id=1, source_target_pairs={{0,4},{2,6},{4,0},{6,2},{1,5},{3,7},{5,1},{7,3},{8,12},{10,14},{12... | collective-permute-start | bytes 491528 | tf_op jit(solution)/shard_map/ppermute | solution.py:384
  8.3 0.0 collective-permute-start.1
  8.3 5.1 %collective-permute-done.refs_1_ = f32[320,128]{1,0:T(8,128)S(1)} collective-permute-done((f32[320,128]{1,0:T(8,128)S(1)}, f32[320,128]{1,0:T(8,128)S(1)}, u32[]{:S(2)}, u32[]{:S(2)}) %collective-permute-start) | collective-permute-done | bytes 163872 | tf_op jit(solution)/shard_map/ppermute | solution.py:384
  13.4 0.0 copy-start.3
  13.4 0.0 collective-permute-start.2
  13.4 2.2 %all-to-all-done = f32[8,48,128]{2,1,0:T(8,128)S(1)} async-done(((f32[8,48,128]{2,1,0:T(8,128)}), f32[8,48,128]{2,1,0:T(8,128)S(1)}, u32[]{:S(2)}, u32[]{:S(2)}) %all-to-all-start) | async-done | bytes 196640 | tf_op jit(solution)/shard_map/all_to_all | solution.py:379
  15.6 0.0 copy-start
  15.6 0.7 %copy-done = f32[8,48,128]{2,1,0:T(8,128)} copy-done((f32[8,48,128]{2,1,0:T(8,128)}, f32[8,48,128]{2,1,0:T(8,128)S(1)}, u32[]{:S(2)}) %copy-start) | copy-done | bytes 196632
  16.3 1.9 %strips.1 = f32[352,128]{1,0:T(8,128)} custom-call(s32[16,128]{1,0:T(8,128)} %get-tuple-element.9.meta_ref, f32[384,128]{1,0:T(8,128)} %bitcast.11), custom_call_target="tpu_custom_call" | custom-call | tf_op jit(solution)/shard_map/strips/pallas_call | solution.py:387
  18.2 3.8 %all-to-all-start.1 = ((f32[4,88,128]{2,1,0:T(8,128)}), f32[4,88,128]{2,1,0:T(8,128)S(1)}, u32[]{:S(2)}, u32[]{:S(2)}) async-start(f32[4,88,128]{2,1,0:T(8,128)} %bitcast.12), calls=%async_computation.1 | async-start | bytes 360448 | tf_op jit(solution)/shard_map/all_to_all | solution.py:395
  22.0 0.0 collective-permute-done.1.refs_2_
  22.0 0.0 copy-start.4
  22.0 0.0 collective-permute-done.2.refs_3_
  22.0 0.0 copy-start.5
  22.0 3.5 %all-to-all-done.1 = f32[4,88,128]{2,1,0:T(8,128)S(1)} async-done(((f32[4,88,128]{2,1,0:T(8,128)}), f32[4,88,128]{2,1,0:T(8,128)S(1)}, u32[]{:S(2)}, u32[]{:S(2)}) %all-to-all-start.1) | async-done | bytes 180256 | tf_op jit(solution)/shard_map/all_to_all | solution.py:395
  25.5 0.0 copy-start.1
  25.5 0.0 copy-done.3
  25.5 0.0 copy-done.4
  25.5 0.0 copy-done.5
  25.5 0.7 %copy-done.1 = f32[4,88,128]{2,1,0:T(8,128)} copy-done((f32[4,88,128]{2,1,0:T(8,128)}, f32[4,88,128]{2,1,0:T(8,128)S(1)}, u32[]{:S(2)}) %copy-start.1) | copy-done | bytes 180248
  26.2 25.8 %step.1 = f32[1,1,5,16,1024]{4,3,2,1,0:T(8,128)} custom-call(s32[1,1,4,32]{3,2,1,0:T(4,128)} %bitcast.19, s32[1,1,1,32]{3,2,1,0:T(1,128)} %bitcast.20, f32[320,128]{1,0:T(8,128)} %get-tuple-element.8.refs_0_, f32[320,128]{1,0:T(8,128)} %copy-done.3, f32[320,128]{1,0:T(8,128)} %copy-done.4, f32[320,128]{1,0:T(8,128)} %copy-done.5, f32[352,128]{1,0:T(8,128)} %bitcast.13), custom_call_target="tpu_custom_call" | custom-call | tf_op jit(solution)/shard_map/step/pallas_call | solution.py:398
Async XLA Ops:
  1.7 5.9 %copy-start.2 = (f32[320,128]{1,0:T(8,128)S(1)}, f32[320,128]{1,0:T(8,128)}, u32[]{:S(2)}) copy-start(f32[320,128]{1,0:T(8,128)} %get-tuple-element.8.refs_0_) | copy-start | bytes 491524
  1.7 13.9 %all-to-all-start = ((f32[8,48,128]{2,1,0:T(8,128)}), f32[8,48,128]{2,1,0:T(8,128)S(1)}, u32[]{:S(2)}, u32[]{:S(2)}) async-start(f32[8,48,128]{2,1,0:T(8,128)} %bitcast.14), calls=%async_computation | async-start | bytes 393216 | tf_op jit(solution)/shard_map/all_to_all | solution.py:379
  7.7 5.7 %collective-permute-start = (f32[320,128]{1,0:T(8,128)S(1)}, f32[320,128]{1,0:T(8,128)S(1)}, u32[]{:S(2)}, u32[]{:S(2)}) collective-permute-start(f32[320,128]{1,0:T(8,128)S(1)} %copy-done.2), channel_id=1, source_target_pairs={{0,4},{2,6},{4,0},{6,2},{1,5},{3,7},{5,1},{7,3},{8,12},{10,14},{12... | collective-permute-start | bytes 491528 | tf_op jit(solution)/shard_map/ppermute | solution.py:384
  8.3 13.7 %collective-permute-start.1 = (f32[320,128]{1,0:T(8,128)S(1)}, f32[320,128]{1,0:T(8,128)S(1)}, u32[]{:S(2)}, u32[]{:S(2)}) collective-permute-start(f32[320,128]{1,0:T(8,128)S(1)} %copy-done.2), channel_id=1, source_target_pairs={{0,2},{2,0},{4,6},{6,4},{1,3},{3,1},{5,7},{7,5},{8,10},{10,8},{12,... | collective-permute-start | bytes 491528 | tf_op jit(solution)/shard_map/ppermute | solution.py:384
  13.4 12.1 %copy-start.3 = (f32[320,128]{1,0:T(8,128)}, f32[320,128]{1,0:T(8,128)S(1)}, u32[]{:S(2)}) copy-start(f32[320,128]{1,0:T(8,128)S(1)} %collective-permute-done.refs_1_) | copy-start | bytes 491524
  13.4 8.6 %collective-permute-start.2 = (f32[320,128]{1,0:T(8,128)S(1)}, f32[320,128]{1,0:T(8,128)S(1)}, u32[]{:S(2)}, u32[]{:S(2)}) collective-permute-start(f32[320,128]{1,0:T(8,128)S(1)} %collective-permute-done.refs_1_), channel_id=1, source_target_pairs={{0,2},{2,0},{4,6},{6,4},{1,3},{3,1},{5,7},{7,5},{8,10},{10,8},{12,... | collective-permute-start | bytes 491528 | tf_op jit(solution)/shard_map/ppermute | solution.py:384
  15.6 0.7 %copy-start = (f32[8,48,128]{2,1,0:T(8,128)}, f32[8,48,128]{2,1,0:T(8,128)S(1)}, u32[]{:S(2)}) copy-start(f32[8,48,128]{2,1,0:T(8,128)S(1)} %all-to-all-done) | copy-start | bytes 589828
  18.2 7.3 %all-to-all-start.1 = ((f32[4,88,128]{2,1,0:T(8,128)}), f32[4,88,128]{2,1,0:T(8,128)S(1)}, u32[]{:S(2)}, u32[]{:S(2)}) async-start(f32[4,88,128]{2,1,0:T(8,128)} %bitcast.12), calls=%async_computation.1 | async-start | bytes 360448 | tf_op jit(solution)/shard_map/all_to_all | solution.py:395
  22.0 3.5 %copy-start.4 = (f32[320,128]{1,0:T(8,128)}, f32[320,128]{1,0:T(8,128)S(1)}, u32[]{:S(2)}) copy-start(f32[320,128]{1,0:T(8,128)S(1)} %collective-permute-done.1.refs_2_) | copy-start | bytes 491524
  22.0 3.5 %copy-start.5 = (f32[320,128]{1,0:T(8,128)}, f32[320,128]{1,0:T(8,128)S(1)}, u32[]{:S(2)}) copy-start(f32[320,128]{1,0:T(8,128)S(1)} %collective-permute-done.2.refs_3_) | copy-start | bytes 491524
  25.5 0.7 %copy-start.1 = (f32[4,88,128]{2,1,0:T(8,128)}, f32[4,88,128]{2,1,0:T(8,128)S(1)}, u32[]{:S(2)}) copy-start(f32[4,88,128]{2,1,0:T(8,128)S(1)} %all-to-all-done.1) | copy-start | bytes 540676
where the time goes:
time: 52.3 us; the launch traced here: 52 us
  Pallas kernels  29.4 us (56%)
  waiting for transfers between devices  10.8 us (21%)
  starting transfers between devices  10.3 us (20%)
  local copies, waits for them, and re-layouts  1.35 us (3%)
    pallas_call x1, Pallas kernels, per_device(): pl.pallas_call(functools.partial(step_kernel, sources, count, patches, sl...  25.8 us
    all_to_all x1, starting transfers between devices, per_device(): lax.all_to_all(payload, ('gx', 'gz'), split_axis=0, concat_axis=0, tiled=...  5.94 us
    ppermute x3, waiting for transfers between devices, per_device(): states = states + [lax.ppermute(x, 'gy', perm) for x in states]  5.15 us
    all_to_all x1, starting transfers between devices, per_device(): strip = lax.all_to_all(strip, 'gy', split_axis=0, concat_axis=0, tiled=True)  3.83 us
    all_to_all x1, waiting for transfers between devices, per_device(): strip = lax.all_to_all(strip, 'gy', split_axis=0, concat_axis=0, tiled=True)  3.47 us
    all_to_all x1, waiting for transfers between devices, per_device(): lax.all_to_all(payload, ('gx', 'gz'), split_axis=0, concat_axis=0, tiled=...  2.22 us
    pallas_call x1, Pallas kernels, per_device(): pl.pallas_call(functools.partial(strip_kernel, parts, group, rows, tiles,...  1.86 us
    pallas_call x1, Pallas kernels, per_device(): pl.pallas_call(functools.partial(pack_kernel, count, tiles, rows, patches...  1.74 us
  transfers between devices with their start and end apart: 5, of which 3 were waited for; matrix products, arithmetic and copies ran while one was open for 0% of the time, Pallas kernels for 4%

commit v1 on v0

v1 whole, which is shorter than its diff:
```python
import functools

import jax
import jax.numpy as jnp
from jax import lax
from jax.experimental import pallas as pl
from jax.experimental.pallas import tpu as pltpu
from jax.sharding import PartitionSpec as P

FIELDS = 5
PX = 32
BOX = 64
SUB = 8
LANE = 128
HALF = PX // 2
STRIDE = BOX - HALF + 1
BOX_ROWS = BOX * BOX // LANE
ROWS = FIELDS * SUB
VX, PRESSURE, WAVE_X, VY, WAVE_Y = range(FIELDS, FIELDS + 5)
X_PLANES = WAVE_X + 1
PLANES = WAVE_Y + 1
FULL = PLANES * SUB
SIDE = X_PLANES * SUB
heat_ratio = 1.4
courant = 0.3
WEST, EAST, SOUTH, NORTH = range(4)
BATCH = 4


def masks_of(n):
    return [n >> (i + 1) for i in range(n.bit_length() - 1)]


def primitive(u):
    inverse = 1.0 / u[0]
    vx, vy, vz = u[1] * inverse, u[2] * inverse, u[3] * inverse
    kinetic = u[1] * (0.5 * vx) + u[2] * (0.5 * vy) + u[3] * (0.5 * vz)
    pressure = (heat_ratio - 1.0) * (u[4] - kinetic)
    sound = jnp.sqrt(heat_ratio * pressure * inverse)
    return vx, vy, pressure, sound


def with_primitives(u):
    vx, vy, pressure, sound = primitive(u)
    return u + [vx, pressure, 0.5 * (jnp.abs(vx) + sound), vy, 0.5 * (jnp.abs(vy) + sound)]


def half_flux(u, moving, pressure, normal):
    half = 0.5 * moving
    flux = [u[f] * half for f in range(FIELDS)]
    flux[normal] = flux[normal] + 0.5 * pressure
    flux[4] = flux[4] + pressure * half
    return flux


def lane_of():
    return lax.broadcasted_iota(jnp.int32, (SUB, LANE), 1)


def sub_of():
    return lax.broadcasted_iota(jnp.int32, (SUB, LANE), 0)


def take_lanes(x, lanes):
    return jnp.take_along_axis(x, lanes, axis=1, mode="promise_in_bounds")


def below(x, low_lanes):
    turned = pltpu.roll(x, PX, 1)
    return jnp.where(low_lanes, pltpu.roll(turned, 1, 0), turned)


def above(x, high_lanes):
    turned = pltpu.roll(x, LANE - PX, 1)
    return jnp.where(high_lanes, pltpu.roll(turned, SUB - 1, 0), turned)


def x_part(own, west, east):
    lane = lane_of()
    col = lane & (PX - 1)
    first, last = col == 0, col == PX - 1
    swap = lane + (PX - 1) - 2 * col
    ghost = [take_lanes(jnp.where(last, w, e), swap) for w, e in zip(west, east)]
    u, wave = own[:FIELDS], own[WAVE_X]
    flux = half_flux(u, own[VX], own[PRESSURE], 1)
    gflux = half_flux(ghost[:FIELDS], ghost[VX], ghost[PRESSURE], 1)
    gwave = ghost[WAVE_X]
    face = jnp.maximum(jnp.where(first, gwave, pltpu.roll(wave, 1, 1)), wave)
    border = jnp.maximum(gwave, wave)
    part = []
    for f in range(FIELDS):
        left_u = jnp.where(first, ghost[f], pltpu.roll(u[f], 1, 1))
        left_flux = jnp.where(first, gflux[f], pltpu.roll(flux[f], 1, 1))
        west_flux = left_flux + flux[f] - face * (u[f] - left_u)
        east_flux = flux[f] + gflux[f] - border * (ghost[f] - u[f])
        part.append(west_flux - jnp.where(last, east_flux, pltpu.roll(west_flux, LANE - 1, 1)))
    return part


def y_border(row0, row31, south, north):
    lane, sub = lane_of(), sub_of()
    low = lane < LANE // 2
    cell = [jnp.where(low, a, b) for a, b in zip(row0, row31)]
    ghost = [take_lanes(jnp.where(low, n, s), lane ^ (LANE - PX)) for s, n in zip(south, north)]

    def flux(u, moving, pressure):
        half = 0.5 * moving
        return u * half + pressure * jnp.where(sub == 2, 0.5, jnp.where(sub == 4, half, 0.0))

    both = flux(*ghost[:3]) + flux(*cell[:3])
    spread = jnp.maximum(ghost[3], cell[3]) * (cell[0] - ghost[0])
    return both - jnp.where(low, spread, -spread)


def y_part(own, border):
    lane, sub = lane_of(), sub_of()
    low, high = lane < PX, lane >= LANE - PX
    first, last = low & (sub == 0), high & (sub == SUB - 1)
    u, wave = own[:FIELDS], own[WAVE_Y]
    flux = half_flux(u, own[VY], own[PRESSURE], 2)
    face = jnp.maximum(below(wave, low), wave)
    part = []
    for f in range(FIELDS):
        south_flux = below(flux[f], low) + flux[f] - face * (u[f] - below(u[f], low))
        edge = jnp.broadcast_to(border[f : f + 1, :], (SUB, LANE))
        south_flux = jnp.where(first, edge, south_flux)
        part.append(south_flux - jnp.where(last, edge, above(south_flux, high)))
    return part


def top_speed(u):
    vx, vy, _, sound = primitive(u)
    return jnp.maximum(jnp.abs(vx), jnp.abs(vy)) + sound


def pack_kernel(parts, tiles, rows, patches, patch_ref, box_ref, which_ref, start_ref, pay_ref, meta_ref):
    me = lax.axis_index("gy")
    top = None
    for s in range(SUB):
        wave = top_speed([patch_ref[0, 0, f, :, s * LANE : (s + 1) * LANE] for f in range(FIELDS)])
        top = wave if top is None else jnp.maximum(top, wave)
    pieces = [box_ref[pl.ds(f * BOX_ROWS + me * tiles, tiles), :] for f in range(FIELDS)]
    for k in range(parts):
        for f in range(FIELDS):
            at = k * rows + f * tiles
            pay_ref[at : at + tiles, :] = pieces[f]
        pay_ref[(k + 1) * rows - SUB : (k + 1) * rows, :] = top

    start = start_ref[0, 0]
    row = lax.shift_right_logical(start * 2675, 17)
    offset = BOX * (row & 1) + start - row * STRIDE
    near = lax.shift_right_logical(row, 1) - me * tiles
    mine = (near >= 0) & (near < tiles)
    patch = lax.broadcasted_iota(jnp.int32, start.shape, 1)
    meta_ref[0:4, 0:patches] = which_ref[0, 0] * rows + jnp.where(mine, near, 0)
    meta_ref[4:8, 0:patches] = (HALF * (patch & (SUB - 1)) - offset) & (LANE - 1)
    meta_ref[8:12, 0:patches] = jnp.where(mine, patch & (SUB - 1), -1)


def strip_kernel(parts, rows, tiles, patches, meta_ref, pay_ref, out_ref):
    top = pay_ref[rows - SUB : rows, :]
    for k in range(1, parts):
        top = jnp.maximum(top, pay_ref[(k + 1) * rows - SUB : (k + 1) * rows, :])
    block = lane_of() // HALF
    lines = 4 * patches // SUB
    out_ref[FIELDS * lines :, :] = top

    def line(v, carry):
        side, first = v // (patches // SUB), v % (patches // SUB) * SUB
        acc = jnp.zeros((SUB, LANE), jnp.float32)
        for m in range(SUB):
            p = first + m
            at, shift, fills = meta_ref[side, p], meta_ref[4 + side, p], meta_ref[8 + side, p]
            strip = pay_ref[pl.ds(at, FIELDS, stride=tiles), :]
            strip = jnp.concatenate([strip, jnp.zeros((SUB - FIELDS, LANE), jnp.float32)], axis=0)
            acc = jnp.where(block == fills, pltpu.roll(strip, shift, 1), acc)
        out_ref[pl.ds(v, FIELDS, stride=lines), :] = acc[:FIELDS, :]
        return carry

    lax.fori_loop(0, lines, line, 0)


def step_kernel(sources, count, patches, slots, around_ref, owner_ref, *refs):
    group = len(sources)
    raw_refs, strip_refs, out_ref = refs[:group], refs[group : 2 * group], refs[2 * group]
    cells, states, strips, placed, items = refs[2 * group + 1 :]
    me = lax.axis_index("gy")
    lines = 4 * patches // SUB
    capacity = slots // group
    side_base = patches * FULL
    row_base = side_base + 2 * patches * SIDE

    for i in range(slots):
        items[patches + i] = -1

    def rank_source(source, carry):
        rank = jnp.int32(0)
        for i in range(count):
            p = source * count + i
            items[p] = p
            hit = owner_ref[0, 0, 0, p] == me
            items[patches + jnp.where(hit, source * capacity + rank, slots)] = p
            rank = rank + jnp.where(hit, 1, 0)
        return carry

    lax.fori_loop(0, group, rank_source, 0)

    def take_field(f, carry):
        for k in range(group):
            base = sources[k](me) * (count * ROWS) + f * SUB
            for s in range(SUB):
                states[pl.ds(base + s, count, stride=ROWS), :] = raw_refs[k][0, 0, f, :, s * LANE : (s + 1) * LANE]
        return carry

    lax.fori_loop(0, FIELDS, take_field, 0)

    def joined(at, join):
        return functools.reduce(join, [ref[at : at + SUB, :] for ref in strip_refs])

    for h in range(lines // SUB):
        u = [joined(f * lines + h * SUB, jnp.add) for f in range(FIELDS)]
        for q, plane in enumerate(with_primitives(u)):
            strips[q * lines + h * SUB : q * lines + (h + 1) * SUB, :] = plane
    time_step = courant / jnp.max(joined(FIELDS * lines, jnp.maximum))
    lane, sub = lane_of(), sub_of()
    down = 2 * sub + lane // (2 * PX)
    along = HALF * sub + (lane & (PX - 1)) // 2

    def wide(q, v, pick):
        return take_lanes(jnp.broadcast_to(strips[pl.ds(q * lines + v, 1), :], (SUB, LANE)), pick)

    def coarse_sides(r, carry):
        v = r // 2
        for m in range(SUB // 2):
            turn = r % 2 * (SUB // 2) + m
            first = pl.multiple_of(side_base + (v * SUB + turn) * SIDE, SUB)
            for q in range(X_PLANES):
                cells[pl.ds(first + q * SUB, SUB), :] = wide(q, v, HALF * turn + down)
        return carry

    lax.fori_loop(0, lines, coarse_sides, 0)

    def coarse_rows(v, carry):
        first = pl.multiple_of(row_base + v * FULL, SUB)
        for q in range(PLANES):
            cells[pl.ds(first + q * SUB, SUB), :] = wide(q, lines // 2 + v, along)
        return carry

    lax.fori_loop(0, lines // 2, coarse_rows, 0)

    def change_of(p):
        near = [around_ref[0, 0, side, p] for side in range(4)]
        first = pl.multiple_of(p * FULL, SUB)

        def beside(side):
            base = jnp.where(near[side] >= 0, near[side] * FULL, side_base + (side * patches + p) * SIDE)
            base = pl.multiple_of(base, SUB)
            return [cells[pl.ds(base + q * SUB, SUB), :] for q in range(X_PLANES)]

        def facing(side, row):
            line = (side - SOUTH) * patches + p
            at_coarse = row_base + line // SUB * FULL + line % SUB
            return jnp.where(near[side] >= 0, near[side] * FULL + row, at_coarse)

        def rows_at(at):
            return [cells[pl.ds(at, SUB, stride=SUB), :]] + [
                jnp.broadcast_to(cells[pl.ds(at + q * SUB, 1), :], (SUB, LANE)) for q in (VY, PRESSURE, WAVE_Y)
            ]

        own = [cells[pl.ds(first + q * SUB, SUB), :] for q in range(PLANES)]
        across = x_part(own, beside(WEST), beside(EAST))
        border = [rows_at(at) for at in (first, first + SUB - 1, facing(SOUTH, SUB - 1), facing(NORTH, 0))]
        along = y_part(own, y_border(*border))
        return own, [a + b for a, b in zip(across, along)]

    def section(stage, carry):
        start = stage * (patches * ROWS)

        def prepare(i, carry):
            for b in range(SUB):
                p = i * SUB + b
                first = pl.multiple_of(start + p * ROWS, SUB)
                u = [states[pl.ds(first + f * SUB, SUB), :] for f in range(FIELDS)]
                first = pl.multiple_of(p * FULL, SUB)
                for q, plane in enumerate(with_primitives(u)):
                    cells[pl.ds(first + q * SUB, SUB), :] = plane
            return carry

        lax.fori_loop(0, patches // SUB, prepare, 0)

        def advance(i, carry):
            made = []
            for b in range(BATCH):
                p = jnp.maximum(items[stage * patches + i * BATCH + b], 0)
                own, change = change_of(p)
                made.append([own[f] + time_step * change[f] for f in range(FIELDS)])
            for b in range(BATCH):
                first = pl.multiple_of(start + (patches + i * BATCH + b) * ROWS, SUB)
                for f in range(FIELDS):
                    states[pl.ds(first + f * SUB, SUB), :] = made[b][f]
            return carry

        lax.fori_loop(0, jnp.where(stage == 0, patches, slots) // BATCH, advance, 0)
        return carry

    lax.fori_loop(0, 2, section, 0)

    def finish(j, carry):
        p = items[patches + j]
        old = pl.multiple_of(jnp.maximum(p, 0) * ROWS, SUB)
        new = pl.multiple_of((2 * patches + j) * ROWS, SUB)
        for f in range(FIELDS):
            end = 0.5 * states[pl.ds(old + f * SUB, SUB), :] + 0.5 * states[pl.ds(new + f * SUB, SUB), :]
            at = (f * (slots // SUB) + j // SUB) * (SUB * SUB) + j % SUB
            placed[pl.ds(at, SUB, stride=SUB), :] = jnp.where(p >= 0, end, 0.0)
        return carry

    lax.fori_loop(0, slots, finish, 0)

    def write(f, carry):
        for t in range(slots // SUB):
            for s in range(SUB):
                at = pl.multiple_of(((f * (slots // SUB) + t) * SUB + s) * SUB, SUB)
                out_ref[0, 0, f, t * SUB : (t + 1) * SUB, s * LANE : (s + 1) * LANE] = placed[pl.ds(at, SUB), :]
        return carry

    lax.fori_loop(0, FIELDS, write, 0)


def limit(*row_counts):
    return pltpu.CompilerParams(vmem_limit_bytes=(sum(row_counts) * LANE * 4 * 5 // 4) + (1 << 20))


def per_device(patch_state, coarse_boxes, new_owner, neighbors, coarse_box, coarse_start):
    count = patch_state.shape[2]
    n_gx, n_gz, group = lax.axis_size("gx"), lax.axis_size("gz"), lax.axis_size("gy")
    parts = n_gx * n_gz
    patches = count * group
    lines = 4 * patches // SUB
    slots = group * max(2, 2 * count // group)
    tiles = BOX_ROWS // group
    rows = -(-tiles * FIELDS // SUB) * SUB + SUB
    strip_rows = FIELDS * lines + SUB
    vmem = pl.BlockSpec(memory_space=pltpu.VMEM)
    smem = pl.BlockSpec(memory_space=pltpu.SMEM)
    f32 = jnp.float32

    def sides_first(x):
        return jnp.swapaxes(x, 2, 3)

    def to_group(x):
        blocks = [x]
        for mask in masks_of(group):
            blocks = blocks + [lax.ppermute(b, "gy", [(i, i ^ mask) for i in range(group)]) for b in blocks]
        return blocks

    sources = [lambda me: me]
    for mask in masks_of(group):
        sources = sources + [lambda me, f=f, mask=mask: f(me) ^ mask for f in sources]

    raw = sides_first(patch_state)
    raws = to_group(raw)

    payload, meta = pl.pallas_call(
        functools.partial(pack_kernel, parts, tiles, rows, patches),
        out_shape=(
            jax.ShapeDtypeStruct((parts * rows, LANE), f32),
            jax.ShapeDtypeStruct((16, max(LANE, patches)), jnp.int32),
        ),
        in_specs=[vmem] * 4,
        out_specs=(vmem,) * 2,
        compiler_params=limit(parts * rows, count * ROWS, FIELDS * BOX_ROWS),
        name="pack",
    )(raw, coarse_boxes.reshape(FIELDS * BOX_ROWS, LANE), sides_first(coarse_box), sides_first(coarse_start))

    payload = lax.all_to_all(payload, ("gx", "gz"), split_axis=0, concat_axis=0, tiled=True)

    strip = pl.pallas_call(
        functools.partial(strip_kernel, parts, rows, tiles, patches),
        out_shape=jax.ShapeDtypeStruct((strip_rows, LANE), f32),
        in_specs=[smem, vmem],
        out_specs=vmem,
        compiler_params=limit(parts * rows, strip_rows),
        name="strips",
    )(meta, payload)
    strips = to_group(strip)

    scratch_rows = [
        patches * FULL + 2 * patches * SIDE + lines // 2 * FULL,
        (2 * patches + slots) * ROWS,
        PLANES * lines,
        FIELDS * slots * SUB,
    ]
    out = pl.pallas_call(
        functools.partial(step_kernel, sources, count, patches, slots),
        out_shape=jax.ShapeDtypeStruct((1, 1, FIELDS, slots, SUB * LANE), f32),
        in_specs=[smem, smem] + [vmem] * (2 * group),
        out_specs=vmem,
        scratch_shapes=[pltpu.VMEM((n, LANE), f32) for n in scratch_rows]
        + [pltpu.SMEM((patches + slots + 1,), jnp.int32)],
        compiler_params=limit(*scratch_rows, patches * ROWS, group * strip_rows, FIELDS * slots * SUB),
        name="step",
    )(sides_first(neighbors), sides_first(new_owner), *raws, *strips)
    return sides_first(out)


def solution(mesh):
    in_specs = (
        P("gx", "gz", "gy", None, None),
        P(("gx", "gz"), None, None),
        P("gx", "gz", None, None),
        P("gx", "gz", None, None),
        P("gx", "gz", None, None),
        P("gx", "gz", None, None),
    )
    out_specs = P("gx", "gz", "gy", None, None)
    return jax.shard_map(
        per_device, mesh=mesh, in_specs=in_specs, out_specs=out_specs, check_vma=False
    )
```

time: 52.3 us -> 40.8 us (0.78)
  the two profiles are of different devices: /device:TPU:4 before, /device:TPU:0 now
where the time goes in v1:
time: 40.8 us; the launch traced here: 40.5 us
  Pallas kernels  16.6 us (41%)
  starting transfers between devices  10.6 us (26%)
  waiting for transfers between devices  10.1 us (25%)
  local copies, waits for them, and re-layouts  3.16 us (8%)
    pallas_call x1, Pallas kernels, per_device(): pl.pallas_call(functools.partial(step_kernel, sources, count, patches, sl...  13.7 us
    ppermute x6, waiting for transfers between devices, to_group(): lax.ppermute(b, 'gy', [(i, i ^ mask) for i in range(group)])  7.87 us
    all_to_all x1, starting transfers between devices, per_device(): lax.all_to_all(payload, ('gx', 'gz'), split_axis=0, concat_axis=0, tiled=...  7.38 us
    ppermute x6, starting transfers between devices, to_group(): lax.ppermute(b, 'gy', [(i, i ^ mask) for i in range(group)])  3.18 us
    unnamed x14, local copies, waits for them, and re-layouts  3.16 us
    all_to_all x1, waiting for transfers between devices, per_device(): lax.all_to_all(payload, ('gx', 'gz'), split_axis=0, concat_axis=0, tiled=...  2.22 us
    pallas_call x1, Pallas kernels, per_device(): pl.pallas_call(functools.partial(strip_kernel, parts, rows, tiles, patche...  2.19 us
  transfers between devices with their start and end apart: 7, of which 4 were waited for; matrix products, arithmetic and copies ran while one was open for 0% of the time, Pallas kernels for 5%

profile of v1, /device:TPU:0, one launch (start us, length us, event | category | flops | bytes accessed | tf_op | source)
XLA Modules:
  0.0 40.5 jit_solution(16886515017121698927)
XLA Ops:
  0.0 0.0 copy-start.4
  0.0 0.0 copy-start.3
  0.0 0.7 %copy-done.4 = s32[1,1,32,4]{2,3,1,0:T(4,128)S(1)} copy-done((s32[1,1,32,4]{2,3,1,0:T(4,128)S(1)}, s32[1,1,32,4]{2,3,1,0:T(4,128)}, u32[]{:S(2)}) %copy-start.4) | copy-done | bytes 536
  0.7 0.0 copy-done.3
  0.7 0.0 copy-start
  0.7 0.9 %copy-done = f32[1,1,8,5,1024]{4,2,3,1,0:T(8,128)S(1)} copy-done((f32[1,1,8,5,1024]{4,2,3,1,0:T(8,128)S(1)}, f32[1,1,8,5,1024]{4,2,3,1,0:T(8,128)}, u32[]{:S(2)}) %copy-start) | copy-done | bytes 163864
  1.6 0.0 copy-start.2
  1.6 0.9 %copy-done.2 = f32[1,5,4096]{2,0,1:T(1,128)S(1)} copy-done((f32[1,5,4096]{2,0,1:T(1,128)S(1)}, f32[1,5,4096]{2,0,1:T(1,128)}, u32[]{:S(2)}) %copy-start.2) | copy-done | bytes 81944
  2.5 0.7 %pack.1 = (f32[384,128]{1,0:T(8,128)}, s32[16,128]{1,0:T(8,128)S(1)}) custom-call(f32[1,1,5,8,1024]{4,3,2,1,0:T(8,128)S(1)} %bitcast.10, f32[160,128]{1,0:T(8,128)S(1)} %bitcast.14, s32[1,1,4,32]{3,2,1,0:T(4,128)S(1)} %bitcast.15, s32[1,1,4,32]{3,2,1,0:T(4,128)S(1)} %bitcast.16), custom_call_target="tpu_custom_call" | custom-call | tf_op jit(solution)/shard_map/pack/pallas_call | solution.py:364
  3.2 0.0 copy-start.1
  3.2 7.4 %all-to-all-start = ((f32[8,48,128]{2,1,0:T(8,128)}), f32[8,48,128]{2,1,0:T(8,128)S(1)}, u32[]{:S(2)}, u32[]{:S(2)}) async-start(f32[8,48,128]{2,1,0:T(8,128)} %bitcast.6), calls=%async_computation | async-start | bytes 393216 | tf_op jit(solution)/shard_map/all_to_all | solution.py:376
  10.6 0.0 copy-done.1
  10.6 1.6 %collective-permute-start = (f32[1,1,5,8,1024]{4,3,2,1,0:T(8,128)S(1)}, f32[1,1,5,8,1024]{4,3,2,1,0:T(8,128)S(1)}, u32[]{:S(2)}, u32[]{:S(2)}) collective-permute-start(f32[1,1,5,8,1024]{4,3,2,1,0:T(8,128)S(1)} %bitcast.11), channel_id=1, source_target_pairs={{0,4},{2,6},{4,0},{6,2},{1,5},{3,7},{5,1},{7,3},{8,12},{10,14},{12... | collective-permute-start | bytes 491528 | tf_op jit(solution)/shard_map/ppermute | solution.py:354
  12.2 0.0 collective-permute-start.1
  12.2 4.1 %collective-permute-done.refs_1_ = f32[1,1,5,8,1024]{4,3,2,1,0:T(8,128)S(1)} collective-permute-done((f32[1,1,5,8,1024]{4,3,2,1,0:T(8,128)S(1)}, f32[1,1,5,8,1024]{4,3,2,1,0:T(8,128)S(1)}, u32[]{:S(2)}, u32[]{:S(2)}) %collective-permute-start) | collective-permute-done | bytes 163872 | tf_op jit(solution)/shard_map/ppermute | solution.py:354
  16.3 0.0 collective-permute-start.2
  16.3 2.2 %all-to-all-done = f32[8,48,128]{2,1,0:T(8,128)S(1)} async-done(((f32[8,48,128]{2,1,0:T(8,128)}), f32[8,48,128]{2,1,0:T(8,128)S(1)}, u32[]{:S(2)}, u32[]{:S(2)}) %all-to-all-start) | async-done | bytes 196640 | tf_op jit(solution)/shard_map/all_to_all | solution.py:376
  18.6 2.2 %strips.1.refs_4_ = f32[88,128]{1,0:T(8,128)S(1)} custom-call(s32[16,128]{1,0:T(8,128)S(1)} %get-tuple-element.7.meta_ref, f32[384,128]{1,0:T(8,128)S(1)} %bitcast.9), custom_call_target="tpu_custom_call" | custom-call | tf_op jit(solution)/shard_map/strips/pallas_call | solution.py:378
  20.8 0.0 copy-start.5
  20.8 1.6 %collective-permute-start.3 = (f32[88,128]{1,0:T(8,128)S(1)}, f32[88,128]{1,0:T(8,128)S(1)}, u32[]{:S(2)}, u32[]{:S(2)}) collective-permute-start(f32[88,128]{1,0:T(8,128)S(1)} %strips.1.refs_4_), channel_id=1, source_target_pairs={{0,4},{2,6},{4,0},{6,2},{1,5},{3,7},{5,1},{7,3},{8,12},{10,14},{12... | collective-permute-start | bytes 135176 | tf_op jit(solution)/shard_map/ppermute | solution.py:354
  22.3 0.0 collective-permute-start.4
  22.3 2.5 %collective-permute-done.3.refs_5_ = f32[88,128]{1,0:T(8,128)S(1)} collective-permute-done((f32[88,128]{1,0:T(8,128)S(1)}, f32[88,128]{1,0:T(8,128)S(1)}, u32[]{:S(2)}, u32[]{:S(2)}) %collective-permute-start.3) | collective-permute-done | bytes 45088 | tf_op jit(solution)/shard_map/ppermute | solution.py:354
  24.9 0.0 collective-permute-start.5
  24.9 0.0 collective-permute-done.1.refs_2_
  24.9 0.0 collective-permute-done.2.refs_3_
  24.9 0.0 collective-permute-done.4.refs_6_
  24.9 1.2 %collective-permute-done.5.refs_7_ = f32[88,128]{1,0:T(8,128)S(1)} collective-permute-done((f32[88,128]{1,0:T(8,128)S(1)}, f32[88,128]{1,0:T(8,128)S(1)}, u32[]{:S(2)}, u32[]{:S(2)}) %collective-permute-start.5) | collective-permute-done | bytes 45088 | tf_op jit(solution)/shard_map/ppermute | solution.py:354
  26.1 0.0 copy-start.6
  26.1 0.0 copy-done.5
  26.1 0.7 %copy-done.6 = s32[1,1,32,1]{2,3,1,0:T(1,128)S(1)} copy-done((s32[1,1,32,1]{2,3,1,0:T(1,128)S(1)}, s32[1,1,32,1]{2,3,1,0:T(1,128)}, u32[]{:S(2)}) %copy-start.6) | copy-done | bytes 152
  26.8 13.7 %step.1 = f32[1,1,5,16,1024]{4,3,2,1,0:T(8,128)} custom-call(s32[1,1,4,32]{3,2,1,0:T(4,128)S(1)} %bitcast.17, s32[1,1,1,32]{3,2,1,0:T(1,128)S(1)} %bitcast.18, f32[1,1,5,8,1024]{4,3,2,1,0:T(8,128)S(1)} %bitcast.13, f32[1,1,5,8,1024]{4,3,2,1,0:T(8,128)S(1)} %collective-permute-done.refs_1_, f32[1,1,5,8,1024]{4,3,2,1,0:T(8,128)S(1)} %collective-permute-done.1.refs_2_, ...), custom_call_target="tpu_custom_call" | custom-call | tf_op jit(solution)/shard_map/step/pallas_call | solution.py:394
Async XLA Ops:
  0.0 0.7 %copy-start.4 = (s32[1,1,32,4]{2,3,1,0:T(4,128)S(1)}, s32[1,1,32,4]{2,3,1,0:T(4,128)}, u32[]{:S(2)}) copy-start(s32[1,1,32,4]{2,3,1,0:T(4,128)} %param.11) | copy-start | bytes 1540
  0.0 0.7 %copy-start.3 = (s32[1,1,32,4]{2,3,1,0:T(4,128)S(1)}, s32[1,1,32,4]{2,3,1,0:T(4,128)}, u32[]{:S(2)}) copy-start(s32[1,1,32,4]{2,3,1,0:T(4,128)} %param.10) | copy-start | bytes 1540
  0.7 0.9 %copy-start = (f32[1,1,8,5,1024]{4,2,3,1,0:T(8,128)S(1)}, f32[1,1,8,5,1024]{4,2,3,1,0:T(8,128)}, u32[]{:S(2)}) copy-start(f32[1,1,8,5,1024]{4,2,3,1,0:T(8,128)} %param.6) | copy-start | bytes 491524
  1.6 0.9 %copy-start.2 = (f32[1,5,4096]{2,0,1:T(1,128)S(1)}, f32[1,5,4096]{2,0,1:T(1,128)}, u32[]{:S(2)}) copy-start(f32[1,5,4096]{2,0,1:T(1,128)} %param.7) | copy-start | bytes 245764
  3.2 7.4 %copy-start.1 = (f32[1,1,8,5,1024]{4,2,3,1,0:T(8,128)S(1)}, f32[1,1,8,5,1024]{4,2,3,1,0:T(8,128)}, u32[]{:S(2)}) copy-start(f32[1,1,8,5,1024]{4,2,3,1,0:T(8,128)} %param.6) | copy-start | bytes 491524
  3.2 15.3 %all-to-all-start = ((f32[8,48,128]{2,1,0:T(8,128)}), f32[8,48,128]{2,1,0:T(8,128)S(1)}, u32[]{:S(2)}, u32[]{:S(2)}) async-start(f32[8,48,128]{2,1,0:T(8,128)} %bitcast.6), calls=%async_computation | async-start | bytes 393216 | tf_op jit(solution)/shard_map/all_to_all | solution.py:376
  10.6 5.7 %collective-permute-start = (f32[1,1,5,8,1024]{4,3,2,1,0:T(8,128)S(1)}, f32[1,1,5,8,1024]{4,3,2,1,0:T(8,128)S(1)}, u32[]{:S(2)}, u32[]{:S(2)}) collective-permute-start(f32[1,1,5,8,1024]{4,3,2,1,0:T(8,128)S(1)} %bitcast.11), channel_id=1, source_target_pairs={{0,4},{2,6},{4,0},{6,2},{1,5},{3,7},{5,1},{7,3},{8,12},{10,14},{12... | collective-permute-start | bytes 491528 | tf_op jit(solution)/shard_map/ppermute | solution.py:354
  12.2 12.7 %collective-permute-start.1 = (f32[1,1,5,8,1024]{4,3,2,1,0:T(8,128)S(1)}, f32[1,1,5,8,1024]{4,3,2,1,0:T(8,128)S(1)}, u32[]{:S(2)}, u32[]{:S(2)}) collective-permute-start(f32[1,1,5,8,1024]{4,3,2,1,0:T(8,128)S(1)} %bitcast.12), channel_id=1, source_target_pairs={{0,2},{2,0},{4,6},{6,4},{1,3},{3,1},{5,7},{7,5},{8,10},{10,8},{12,... | collective-permute-start | bytes 491528 | tf_op jit(solution)/shard_map/ppermute | solution.py:354
  16.3 8.5 %collective-permute-start.2 = (f32[1,1,5,8,1024]{4,3,2,1,0:T(8,128)S(1)}, f32[1,1,5,8,1024]{4,3,2,1,0:T(8,128)S(1)}, u32[]{:S(2)}, u32[]{:S(2)}) collective-permute-start(f32[1,1,5,8,1024]{4,3,2,1,0:T(8,128)S(1)} %collective-permute-done.refs_1_), channel_id=1, source_target_pairs={{0,2},{2,0},{4,6},{6,4},{1,3},{3,1},{5,7},{7,5},{8,10},{10,8},{12,... | collective-permute-start | bytes 491528 | tf_op jit(solution)/shard_map/ppermute | solution.py:354
  20.8 5.3 %copy-start.5 = (s32[1,1,32,4]{2,3,1,0:T(4,128)S(1)}, s32[1,1,32,4]{2,3,1,0:T(4,128)}, u32[]{:S(2)}) copy-start(s32[1,1,32,4]{2,3,1,0:T(4,128)} %param.9) | copy-start | bytes 1540
  20.8 4.1 %collective-permute-start.3 = (f32[88,128]{1,0:T(8,128)S(1)}, f32[88,128]{1,0:T(8,128)S(1)}, u32[]{:S(2)}, u32[]{:S(2)}) collective-permute-start(f32[88,128]{1,0:T(8,128)S(1)} %strips.1.refs_4_), channel_id=1, source_target_pairs={{0,4},{2,6},{4,0},{6,2},{1,5},{3,7},{5,1},{7,3},{8,12},{10,14},{12... | collective-permute-start | bytes 135176 | tf_op jit(solution)/shard_map/ppermute | solution.py:354
  22.3 2.5 %collective-permute-start.4 = (f32[88,128]{1,0:T(8,128)S(1)}, f32[88,128]{1,0:T(8,128)S(1)}, u32[]{:S(2)}, u32[]{:S(2)}) collective-permute-start(f32[88,128]{1,0:T(8,128)S(1)} %strips.1.refs_4_), channel_id=1, source_target_pairs={{0,2},{2,0},{4,6},{6,4},{1,3},{3,1},{5,7},{7,5},{8,10},{10,8},{12,... | collective-permute-start | bytes 135176 | tf_op jit(solution)/shard_map/ppermute | solution.py:354
  24.9 1.2 %collective-permute-start.5 = (f32[88,128]{1,0:T(8,128)S(1)}, f32[88,128]{1,0:T(8,128)S(1)}, u32[]{:S(2)}, u32[]{:S(2)}) collective-permute-start(f32[88,128]{1,0:T(8,128)S(1)} %collective-permute-done.3.refs_5_), channel_id=1, source_target_pairs={{0,2},{2,0},{4,6},{6,4},{1,3},{3,1},{5,7},{7,5},{8,10},{10,8},{12,... | collective-permute-start | bytes 135176 | tf_op jit(solution)/shard_map/ppermute | solution.py:354
  26.1 0.7 %copy-start.6 = (s32[1,1,32,1]{2,3,1,0:T(1,128)S(1)}, s32[1,1,32,1]{2,3,1,0:T(1,128)}, u32[]{:S(2)}) copy-start(s32[1,1,32,1]{2,3,1,0:T(1,128)} %param.8) | copy-start | bytes 388

commit v2 on v1

v2 whole, which is shorter than its diff:
```python
import functools

import jax
import jax.numpy as jnp
from jax import lax
from jax.experimental import pallas as pl
from jax.experimental.pallas import tpu as pltpu
from jax.sharding import PartitionSpec as P

FIELDS = 5
PX = 32
BOX = 64
SUB = 8
LANE = 128
HALF = PX // 2
STRIDE = BOX - HALF + 1
BOX_ROWS = BOX * BOX // LANE
heat_ratio = 1.4
courant = 0.3
WEST, EAST, SOUTH, NORTH = range(4)
BLOCKS = LANE // PX
DEEP = PX // BLOCKS
SPAN = PX + 2 * SUB
PLANE = (DEEP + 2) * SPAN
FACES = PX + SUB
AUX = 2 * (FIELDS + 1)


def spot(row, column):
    return (row + 1) * SPAN + SUB + column


def masks_of(n):
    return [n >> (i + 1) for i in range(n.bit_length() - 1)]


def primitive(u):
    inverse = 1.0 / u[0]
    vx, vy, vz = u[1] * inverse, u[2] * inverse, u[3] * inverse
    kinetic = u[1] * (0.5 * vx) + u[2] * (0.5 * vy) + u[3] * (0.5 * vz)
    pressure = (heat_ratio - 1.0) * (u[4] - kinetic)
    sound = jnp.sqrt(heat_ratio * pressure * inverse)
    return vx, vy, pressure, sound


def half_flux(u, moving, pressure, sound, normal):
    half = 0.5 * moving
    flux = [u[f] * half for f in range(FIELDS)]
    flux[normal] = flux[normal] + 0.5 * pressure
    flux[4] = flux[4] + pressure * half
    return flux + [0.5 * (jnp.abs(moving) + sound)]


def face_flux(low_u, low_aux, u, aux):
    wave = jnp.maximum(low_aux[FIELDS], aux[FIELDS])
    return [low_aux[f] + aux[f] - wave * (u[f] - low_u[f]) for f in range(FIELDS)]


def lane_of():
    return lax.broadcasted_iota(jnp.int32, (SUB, LANE), 1)


def sub_of():
    return lax.broadcasted_iota(jnp.int32, (SUB, LANE), 0)


def take_lanes(x, lanes):
    return jnp.take_along_axis(x, lanes, axis=1, mode="promise_in_bounds")


def top_speed(u):
    vx, vy, _, sound = primitive(u)
    return jnp.maximum(jnp.abs(vx), jnp.abs(vy)) + sound


def pack_kernel(parts, tiles, rows, patches, patch_ref, box_ref, which_ref, start_ref, pay_ref, meta_ref):
    me = lax.axis_index("gy")
    top = None
    for s in range(SUB):
        wave = top_speed([patch_ref[0, 0, f, :, s * LANE : (s + 1) * LANE] for f in range(FIELDS)])
        top = wave if top is None else jnp.maximum(top, wave)
    pieces = [box_ref[pl.ds(f * BOX_ROWS + me * tiles, tiles), :] for f in range(FIELDS)]
    for k in range(parts):
        for f in range(FIELDS):
            at = k * rows + f * tiles
            pay_ref[at : at + tiles, :] = pieces[f]
        pay_ref[(k + 1) * rows - SUB : (k + 1) * rows, :] = top

    start = start_ref[0, 0]
    row = lax.shift_right_logical(start * 2675, 17)
    offset = BOX * (row & 1) + start - row * STRIDE
    near = lax.shift_right_logical(row, 1) - me * tiles
    mine = (near >= 0) & (near < tiles)
    patch = lax.broadcasted_iota(jnp.int32, start.shape, 1)
    meta_ref[0:4, 0:patches] = which_ref[0, 0] * rows + jnp.where(mine, near, 0)
    meta_ref[4:8, 0:patches] = (HALF * (patch & (SUB - 1)) - offset) & (LANE - 1)
    meta_ref[8:12, 0:patches] = jnp.where(mine, patch & (SUB - 1), -1)


def strip_kernel(parts, rows, tiles, patches, meta_ref, pay_ref, out_ref):
    top = pay_ref[rows - SUB : rows, :]
    for k in range(1, parts):
        top = jnp.maximum(top, pay_ref[(k + 1) * rows - SUB : (k + 1) * rows, :])
    block = lane_of() // HALF
    lines = 4 * patches // SUB
    out_ref[FIELDS * lines :, :] = top

    for v in range(lines):
        side, first = v // (patches // SUB), v % (patches // SUB) * SUB
        acc = jnp.zeros((SUB, LANE), jnp.float32)
        for m in range(SUB):
            p = first + m
            at, shift, fills = meta_ref[side, p], meta_ref[4 + side, p], meta_ref[8 + side, p]
            strip = pay_ref[pl.ds(at, FIELDS, stride=tiles), :]
            strip = jnp.concatenate([strip, jnp.zeros((SUB - FIELDS, LANE), jnp.float32)], axis=0)
            acc = jnp.where(block == fills, pltpu.roll(strip, shift, 1), acc)
        out_ref[pl.ds(v, FIELDS, stride=lines), :] = acc[:FIELDS, :]


def step_kernel(group, count, patches, slots, around_ref, owner_ref, *refs):
    raw_refs, strip_refs, out_ref = refs[:group], refs[group : 2 * group], refs[2 * group]
    first_u, second_u, aux_ref, dx_ref, strips, doubled, coarse_ref, table, slot_ref = refs[2 * group + 1 :]
    me = lax.axis_index("gy")
    lines = 4 * patches // SUB
    capacity = slots // group
    sets = patches // PX
    lane, sub = lane_of(), sub_of()
    block, in_block = lane // PX, lane & (PX - 1)
    turn = me * count

    for i in range(slots):
        slot_ref[i] = -1

    def rank_source(source, carry):
        rank = jnp.int32(0)
        for i in range(count):
            p = source * count + i
            hit = owner_ref[0, 0, 0, p] == me
            slot_ref[jnp.where(hit, source * capacity + rank, slots)] = p
            rank = rank + jnp.where(hit, 1, 0)
        return carry

    lax.fori_loop(0, group, rank_source, 0)

    def take_field(f, carry):
        for g in range(sets):
            base = (g * FIELDS + f) * PLANE
            for h in range(2):
                tiles = []
                for q in range(BLOCKS):
                    at = (q * 2 + h) * LANE
                    for k in range(PX // count):
                        tiles.append(raw_refs[g * (PX // count) + k][0, 0, f, :, at : at + LANE])
                cells = jnp.concatenate(tiles, axis=0).T
                for i in range(BLOCKS):
                    to = pl.multiple_of(base + spot(h * BLOCKS + i, 0), SUB)
                    first_u[pl.ds(to, PX), :] = cells[i * PX : (i + 1) * PX, :]
        return carry

    lax.fori_loop(0, FIELDS, take_field, 0)

    def joined(at, join):
        return functools.reduce(join, [ref[at : at + SUB, :] for ref in strip_refs])

    for at in range(0, FIELDS * lines, SUB):
        strips[at : at + SUB, :] = joined(at, jnp.add)
    time_step = courant / jnp.max(joined(FIELDS * lines, jnp.maximum))
    part = HALF * sub + (lane & (HALF - 1))
    for t in range(4 * patches // LANE):
        tiles = []
        for v in range(t * HALF, (t + 1) * HALF):
            tile = None
            for f in range(FIELDS):
                row = jnp.broadcast_to(strips[f * lines + v : f * lines + v + 1, :], (SUB, LANE))
                wide = take_lanes(row, part)
                tile = wide if tile is None else jnp.where(lane // HALF == f, wide, tile)
            tiles.append(tile)
        cells = jnp.concatenate(tiles, axis=0).T
        for n in range(FIELDS * 2):
            for twice in range(2):
                at = t * FIELDS * PX + n * HALF + twice
                doubled[pl.ds(at, SUB, stride=2), :] = cells[n * SUB : (n + 1) * SUB, :]

    table[0:4, 0:patches] = around_ref[0, 0]
    picks, origins, coarses = [], [], []
    for g in range(sets):
        patch = (g * PX + in_block) ^ turn
        for side in range(4):
            near = take_lanes(jnp.broadcast_to(table[side : side + 1, :], (SUB, LANE)), patch)
            place = jnp.maximum(near, 0) ^ turn
            pick, origin = place & (PX - 1), lax.shift_right_logical(place, 5)
            lacking = jnp.where(near < 0, 1, 0)
            if side in (WEST, EAST):
                pick = pick + PX * block
            else:
                edge, step = (0, -PX) if side == SOUTH else (BLOCKS - 1, PX)
                across = pick + (LANE - PX if side == SOUTH else 0)
                pick = jnp.where(block == edge, across, lane + step)
                origin = jnp.where(block == edge, origin, g)
                lacking = jnp.where(block == edge, lacking, 0)
            picks.append(pick)
            origins.append(origin)
            coarses.append(lacking)

    def coarse_field(f, carry):
        for g in range(sets):
            patch = (g * PX + in_block) ^ turn
            base = (g * FIELDS + f) * (10 * SUB)
            for side in range(4):
                t, shift = side * patches // LANE, side * patches % LANE
                pieces = [
                    take_lanes(
                        doubled[pl.ds(pl.multiple_of(t * FIELDS * PX + f * PX + SUB * i, SUB), SUB), :], patch + shift
                    )
                    for i in range(BLOCKS)
                ]
                if side in (WEST, EAST):
                    x = pieces[0]
                    for q in range(1, BLOCKS):
                        x = jnp.where(block == q, pieces[q], x)
                    coarse_ref[pl.ds(pl.multiple_of(base + side * SUB, SUB), SUB), :] = x
                else:
                    for i in range(BLOCKS):
                        to = base + (2 + (side - SOUTH) * BLOCKS + i) * SUB
                        coarse_ref[pl.ds(pl.multiple_of(to, SUB), SUB), :] = pieces[i]
        return carry

    lax.fori_loop(0, FIELDS, coarse_field, 0)

    def fill_ghosts(u_ref):
        def field(f, carry):
            bases = [pl.multiple_of((g * FIELDS + f) * PLANE, SUB) for g in range(sets)]

            def ghost(g, side, load, kept):
                x = None
                for o in range(sets):
                    moved = take_lanes(load(bases[o]), picks[4 * g + side])
                    x = moved if x is None else jnp.where(origins[4 * g + side] == o, moved, x)
                at = pl.multiple_of(((g * FIELDS + f) * 10 + kept) * SUB, SUB)
                return jnp.where(coarses[4 * g + side] != 0, coarse_ref[pl.ds(at, SUB), :], x)

            made = []
            for g in range(sets):
                for side, column, to in ((WEST, PX - 1, -1), (EAST, 0, PX)):
                    x = ghost(g, side, lambda b, c=column: u_ref[pl.ds(b + spot(0, c), DEEP, stride=SPAN), :], side)
                    made.append((pl.ds(bases[g] + spot(0, to), DEEP, stride=SPAN), x))
                for side, row, to in ((SOUTH, DEEP - 1, -1), (NORTH, 0, DEEP)):
                    for i in range(BLOCKS):
                        x = ghost(
                            g,
                            side,
                            lambda b, r=row, i=i: u_ref[pl.ds(b + spot(r, SUB * i), SUB), :],
                            2 + (side - SOUTH) * BLOCKS + i,
                        )
                        made.append((pl.ds(bases[g] + spot(to, SUB * i), SUB), x))
            for at, x in made:
                u_ref[at, :] = x
            return carry

        lax.fori_loop(0, FIELDS, field, 0)

    def halves(u_ref, g, rows, axes):
        u = [u_ref[rows((g * FIELDS + f) * PLANE), :] for f in range(FIELDS)]
        vx, vy, pressure, sound = primitive(u)
        for axis in axes:
            made = half_flux(u, (vx, vy)[axis], pressure, sound, axis + 1)
            for n, x in enumerate(made):
                aux_ref[rows((g * AUX + axis * (FIELDS + 1) + n) * PLANE), :] = x

    def section(u_ref, to_ref, last):
        fill_ghosts(u_ref)
        for g in range(sets):

            def cells(r, carry):
                for i in range(BLOCKS):
                    halves(u_ref, g, lambda b, i=i: pl.ds(pl.multiple_of(b + spot(r, SUB * i), SUB), SUB), (0, 1))
                return carry

            lax.fori_loop(0, DEEP, cells, 0)
            for r in (-1, DEEP):
                for i in range(BLOCKS):
                    halves(u_ref, g, lambda b, r=r, i=i: pl.ds(b + spot(r, SUB * i), SUB), (1,))
            for c in (-1, PX):
                halves(u_ref, g, lambda b, c=c: pl.ds(b + spot(0, c), DEEP, stride=SPAN), (0,))

        for g in range(sets):

            def load(at, axis):
                u = [u_ref[pl.ds((g * FIELDS + f) * PLANE + at, SUB), :] for f in range(FIELDS)]
                start = g * AUX + axis * (FIELDS + 1)
                return u, [aux_ref[pl.ds((start + n) * PLANE + at, SUB), :] for n in range(FIELDS + 1)]

            def across(r, carry):
                for i in range(BLOCKS + 1):
                    at = pl.multiple_of(spot(r, SUB * i), SUB)
                    faces = face_flux(*load(at - 1, 0), *load(at, 0))
                    for f in range(FIELDS):
                        to = pl.multiple_of((f * DEEP + r) * FACES + SUB * i, SUB)
                        dx_ref[pl.ds(to, SUB), :] = faces[f]
                return carry

            lax.fori_loop(0, DEEP, across, 0)

            def along(i, carry):
                low_u, low_aux = load(pl.multiple_of(spot(-1, SUB * i), SUB), 1)
                low_faces = None
                for r in range(DEEP + 1):
                    u, aux = load(pl.multiple_of(spot(r, SUB * i), SUB), 1)
                    faces = face_flux(low_u, low_aux, u, aux)
                    for f in range(FIELDS):
                        if r == 0:
                            continue
                        west = pl.multiple_of((f * DEEP + r - 1) * FACES + SUB * i, SUB)
                        change = dx_ref[pl.ds(west, SUB), :] - dx_ref[pl.ds(west + 1, SUB), :]
                        change = change + (low_faces[f] - faces[f])
                        new = low_u[f] + time_step * change
                        to = pl.ds(pl.multiple_of((g * FIELDS + f) * PLANE + spot(r - 1, SUB * i), SUB), SUB)
                        to_ref[to, :] = 0.5 * to_ref[to, :] + 0.5 * new if last else new
                    low_u, low_aux, low_faces = u, aux, faces
                return carry

            lax.fori_loop(0, BLOCKS, along, 0)

    section(first_u, second_u, False)
    section(second_u, first_u, True)

    held = jnp.full((SUB, LANE), -1, jnp.int32)
    for j in range(slots):
        held = jnp.where(in_block == j, slot_ref[j], held)
    place = jnp.maximum(held, 0) ^ turn
    pick, origin = PX * block + (place & (PX - 1)), lax.shift_right_logical(place, 5)

    def give_field(f, carry):
        for h in range(2):
            tiles = []
            for i in range(LANE // SUB):
                at = spot(h * BLOCKS + i // BLOCKS, SUB * (i % BLOCKS))
                x = None
                for g in range(sets):
                    from_set = pl.ds(pl.multiple_of((g * FIELDS + f) * PLANE + at, SUB), SUB)
                    moved = take_lanes(first_u[from_set, :], pick)
                    x = moved if x is None else jnp.where(origin == g, moved, x)
                tiles.append(jnp.where(held >= 0, x, 0.0))
            cells = jnp.concatenate(tiles, axis=0).T
            for q in range(BLOCKS):
                at = (q * 2 + h) * LANE
                out_ref[0, 0, f, :, at : at + LANE] = cells[q * PX : q * PX + slots, :]
        return carry

    lax.fori_loop(0, FIELDS, give_field, 0)


def limit(*row_counts):
    return pltpu.CompilerParams(vmem_limit_bytes=(sum(row_counts) * LANE * 4 * 5 // 4) + (1 << 20))


def per_device(patch_state, coarse_boxes, new_owner, neighbors, coarse_box, coarse_start):
    count = patch_state.shape[2]
    n_gx, n_gz, group = lax.axis_size("gx"), lax.axis_size("gz"), lax.axis_size("gy")
    parts = n_gx * n_gz
    patches = count * group
    lines = 4 * patches // SUB
    slots = group * max(2, 2 * count // group)
    tiles = BOX_ROWS // group
    rows = -(-tiles * FIELDS // SUB) * SUB + SUB
    strip_rows = FIELDS * lines + SUB
    vmem = pl.BlockSpec(memory_space=pltpu.VMEM)
    smem = pl.BlockSpec(memory_space=pltpu.SMEM)
    f32 = jnp.float32

    def sides_first(x):
        return jnp.swapaxes(x, 2, 3)

    def to_group(x):
        blocks = [x] + [None] * (group - 1)
        have = [0]
        for mask in masks_of(group):
            for k in have:
                blocks[k ^ mask] = lax.ppermute(blocks[k], "gy", [(i, i ^ mask) for i in range(group)])
            have = have + [k ^ mask for k in have]
        return blocks

    raw = sides_first(patch_state)
    raws = [raw] + [lax.ppermute(raw, "gy", [(i, i ^ k) for i in range(group)]) for k in range(1, group)]

    payload, meta = pl.pallas_call(
        functools.partial(pack_kernel, parts, tiles, rows, patches),
        out_shape=(
            jax.ShapeDtypeStruct((parts * rows, LANE), f32),
            jax.ShapeDtypeStruct((16, max(LANE, patches)), jnp.int32),
        ),
        in_specs=[vmem] * 4,
        out_specs=(vmem,) * 2,
        name="pack",
    )(raw, coarse_boxes.reshape(FIELDS * BOX_ROWS, LANE), sides_first(coarse_box), sides_first(coarse_start))

    payload = lax.all_to_all(payload, ("gx", "gz"), split_axis=0, concat_axis=0, tiled=True)

    strip = pl.pallas_call(
        functools.partial(strip_kernel, parts, rows, tiles, patches),
        out_shape=jax.ShapeDtypeStruct((strip_rows, LANE), f32),
        in_specs=[smem, vmem],
        out_specs=vmem,
        compiler_params=limit(parts * rows, strip_rows),
        name="strips",
    )(meta, payload)
    strips = to_group(strip)

    sets = patches // PX
    scratch_rows = [
        sets * FIELDS * PLANE,
        sets * FIELDS * PLANE,
        sets * AUX * PLANE,
        FIELDS * DEEP * FACES,
        FIELDS * lines,
        4 * patches // LANE * FIELDS * PX,
        sets * FIELDS * 10 * SUB,
    ]
    out = pl.pallas_call(
        functools.partial(step_kernel, group, count, patches, slots),
        out_shape=jax.ShapeDtypeStruct((1, 1, FIELDS, slots, SUB * LANE), f32),
        in_specs=[vmem, smem] + [vmem] * (2 * group),
        out_specs=vmem,
        scratch_shapes=[pltpu.VMEM((n, LANE), f32) for n in scratch_rows]
        + [pltpu.VMEM((SUB, LANE), jnp.int32), pltpu.SMEM((slots + 1,), jnp.int32)],
        compiler_params=limit(*scratch_rows, 2 * patches * FIELDS * SUB, group * strip_rows, FIELDS * slots * SUB),
        name="step",
    )(sides_first(neighbors), sides_first(new_owner), *raws, *strips)
    return sides_first(out)


def solution(mesh):
    in_specs = (
        P("gx", "gz", "gy", None, None),
        P(("gx", "gz"), None, None),
        P("gx", "gz", None, None),
        P("gx", "gz", None, None),
        P("gx", "gz", None, None),
        P("gx", "gz", None, None),
    )
    out_specs = P("gx", "gz", "gy", None, None)
    return jax.shard_map(
        per_device, mesh=mesh, in_specs=in_specs, out_specs=out_specs, check_vma=False
    )
```

time: 40.8 us -> 30.4 us (0.75)
  Pallas kernels: 16.6 us -> 8.78 us
  local copies, waits for them, and re-layouts: 3.16 us -> 0.67 us
    pallas_call x1, Pallas kernels: 13.7 us -> 6.21 us  [per_device(): pl.pallas_call(functools.partial(step_kernel, group, count, patches, slot...]
    ppermute x6, waiting for transfers between devices: 7.87 us -> 3.73 us  [the longest x3 3.72 us: to_group(): lax.ppermute(blocks[k], 'gy', [(i, i ^ mask) for i in range(group)])]
    all_to_all x1, waiting for transfers between devices: 2.22 us -> 6.02 us  [per_device(): lax.all_to_all(payload, ('gx', 'gz'), split_axis=0, concat_axis=0, tiled=...]
    unnamed x14 -> x8, local copies, waits for them, and re-layouts: 3.16 us -> 0.67 us
    pallas_call x1, Pallas kernels: 2.19 us -> 0.89 us  [per_device(): pl.pallas_call(functools.partial(strip_kernel, parts, rows, tiles, patche...]
    pallas_call x1, Pallas kernels: 0.72 us -> 1.68 us  [per_device(): pl.pallas_call(functools.partial(pack_kernel, parts, tiles, rows, patches...]
  transfers between devices with their start and end apart: 7 -> 7, of which waited for: 4 -> 3; matrix products, arithmetic and copies ran while one was open for 0% -> 0% of each run, Pallas kernels for 5% -> 3%
where the time goes in v2:
time: 30.4 us; the launch traced here: 30.1 us
  starting transfers between devices  10.9 us (36%)
  waiting for transfers between devices  9.75 us (32%)
  Pallas kernels  8.78 us (29%)
  local copies, waits for them, and re-layouts  0.67 us (2%)
    all_to_all x1, starting transfers between devices, per_device(): lax.all_to_all(payload, ('gx', 'gz'), split_axis=0, concat_axis=0, tiled=...  7.38 us
    pallas_call x1, Pallas kernels, per_device(): pl.pallas_call(functools.partial(step_kernel, group, count, patches, slot...  6.21 us
    all_to_all x1, waiting for transfers between devices, per_device(): lax.all_to_all(payload, ('gx', 'gz'), split_axis=0, concat_axis=0, tiled=...  6.02 us
    ppermute x3, waiting for transfers between devices, to_group(): lax.ppermute(blocks[k], 'gy', [(i, i ^ mask) for i in range(group)])  3.72 us
    ppermute x3, starting transfers between devices, per_device(): lax.ppermute(raw, 'gy', [(i, i ^ k) for i in range(group)])  1.93 us
    pallas_call x1, Pallas kernels, per_device(): pl.pallas_call(functools.partial(pack_kernel, parts, tiles, rows, patches...  1.68 us
    ppermute x3, starting transfers between devices, to_group(): lax.ppermute(blocks[k], 'gy', [(i, i ^ mask) for i in range(group)])  1.59 us
    pallas_call x1, Pallas kernels, per_device(): pl.pallas_call(functools.partial(strip_kernel, parts, rows, tiles, patche...  0.89 us
  transfers between devices with their start and end apart: 7, of which 3 were waited for; matrix products, arithmetic and copies ran while one was open for 0% of the time, Pallas kernels for 3%

profile of v2, /device:TPU:0, one launch (start us, length us, event | category | flops | bytes accessed | tf_op | source)
XLA Modules:
  0.0 30.1 jit_solution(2332914396069872795)
XLA Ops:
  0.0 1.7 %pack.1 = (f32[384,128]{1,0:T(8,128)}, s32[16,128]{1,0:T(8,128)}) custom-call(f32[1,1,5,8,1024]{4,3,2,1,0:T(8,128)} %bitcast.10, f32[160,128]{1,0:T(8,128)} %bitcast.18, s32[1,1,4,32]{3,2,1,0:T(4,128)} %bitcast.19, s32[1,1,4,32]{3,2,1,0:T(4,128)} %bitcast.20), custom_call_target="tpu_custom_call" | custom-call | tf_op jit(solution)/shard_map/pack/pallas_call | solution.py:386
  1.7 0.0 copy-start
  1.7 0.0 copy-start.1
  1.7 7.4 %all-to-all-start = ((f32[8,48,128]{2,1,0:T(8,128)}), f32[8,48,128]{2,1,0:T(8,128)S(1)}, u32[]{:S(2)}, u32[]{:S(2)}) async-start(f32[8,48,128]{2,1,0:T(8,128)} %bitcast.17), calls=%async_computation | async-start | bytes 393216 | tf_op jit(solution)/shard_map/all_to_all | solution.py:397
  9.1 0.0 copy-done
  9.1 0.7 %collective-permute-start.2 = (f32[1,1,5,8,1024]{4,3,2,1,0:T(8,128)S(1)}, f32[1,1,5,8,1024]{4,3,2,1,0:T(8,128)S(1)}, u32[]{:S(2)}, u32[]{:S(2)}) collective-permute-start(f32[1,1,5,8,1024]{4,3,2,1,0:T(8,128)S(1)} %bitcast.11), channel_id=1, source_target_pairs={{0,6},{2,4},{4,2},{6,0},{1,7},{3,5},{5,3},{7,1},{8,14},{10,12},{12... | collective-permute-start | bytes 491528 | tf_op jit(solution)/shard_map/ppermute | solution.py:384
  9.8 0.9 %collective-permute-start.1 = (f32[1,1,5,8,1024]{4,3,2,1,0:T(8,128)S(1)}, f32[1,1,5,8,1024]{4,3,2,1,0:T(8,128)S(1)}, u32[]{:S(2)}, u32[]{:S(2)}) collective-permute-start(f32[1,1,5,8,1024]{4,3,2,1,0:T(8,128)S(1)} %bitcast.12), channel_id=1, source_target_pairs={{0,4},{2,6},{4,0},{6,2},{1,5},{3,7},{5,1},{7,3},{8,12},{10,14},{12... | collective-permute-start | bytes 491528 | tf_op jit(solution)/shard_map/ppermute | solution.py:384
  10.7 0.3 collective-permute-start
  11.0 6.0 %all-to-all-done = f32[8,48,128]{2,1,0:T(8,128)S(1)} async-done(((f32[8,48,128]{2,1,0:T(8,128)}), f32[8,48,128]{2,1,0:T(8,128)S(1)}, u32[]{:S(2)}, u32[]{:S(2)}) %all-to-all-start) | async-done | bytes 196640 | tf_op jit(solution)/shard_map/all_to_all | solution.py:397
  17.0 0.0 copy-done.1
  17.0 0.9 %strips.1.refs_4_ = f32[88,128]{1,0:T(8,128)S(1)} custom-call(s32[16,128]{1,0:T(8,128)S(1)} %copy-done.1, f32[384,128]{1,0:T(8,128)S(1)} %bitcast.9), custom_call_target="tpu_custom_call" | custom-call | tf_op jit(solution)/shard_map/strips/pallas_call | solution.py:399
  17.9 0.0 copy-start.2
  17.9 1.6 %collective-permute-start.4 = (f32[88,128]{1,0:T(8,128)S(1)}, f32[88,128]{1,0:T(8,128)S(1)}, u32[]{:S(2)}, u32[]{:S(2)}) collective-permute-start(f32[88,128]{1,0:T(8,128)S(1)} %strips.1.refs_4_), channel_id=1, source_target_pairs={{0,4},{2,6},{4,0},{6,2},{1,5},{3,7},{5,1},{7,3},{8,12},{10,14},{12... | collective-permute-start | bytes 135176 | tf_op jit(solution)/shard_map/ppermute | solution.py:379
  19.5 0.0 collective-permute-start.3
  19.5 2.5 %collective-permute-done.4.refs_6_ = f32[88,128]{1,0:T(8,128)S(1)} collective-permute-done((f32[88,128]{1,0:T(8,128)S(1)}, f32[88,128]{1,0:T(8,128)S(1)}, u32[]{:S(2)}, u32[]{:S(2)}) %collective-permute-start.4) | collective-permute-done | bytes 45088 | tf_op jit(solution)/shard_map/ppermute | solution.py:379
  22.1 0.0 collective-permute-start.5
  22.1 0.0 collective-permute-done.2.refs_3_
  22.1 0.0 collective-permute-done.1.refs_2_
  22.1 0.0 collective-permute-done.refs_1_
  22.1 0.0 collective-permute-done.3.refs_5_
  22.1 1.2 %collective-permute-done.5.refs_7_ = f32[88,128]{1,0:T(8,128)S(1)} collective-permute-done((f32[88,128]{1,0:T(8,128)S(1)}, f32[88,128]{1,0:T(8,128)S(1)}, u32[]{:S(2)}, u32[]{:S(2)}) %collective-permute-start.5) | collective-permute-done | bytes 45088 | tf_op jit(solution)/shard_map/ppermute | solution.py:379
  23.3 0.0 copy-start.3
  23.3 0.0 copy-done.2
  23.3 0.7 %copy-done.3 = s32[1,1,32,1]{2,3,1,0:T(1,128)S(1)} copy-done((s32[1,1,32,1]{2,3,1,0:T(1,128)S(1)}, s32[1,1,32,1]{2,3,1,0:T(1,128)}, u32[]{:S(2)}) %copy-start.3) | copy-done | bytes 152
  23.9 6.2 %step.1 = f32[1,1,5,16,1024]{4,3,2,1,0:T(8,128)} custom-call(s32[1,1,4,32]{3,2,1,0:T(4,128)S(1)} %bitcast.15, s32[1,1,1,32]{3,2,1,0:T(1,128)S(1)} %bitcast.16, f32[1,1,5,8,1024]{4,3,2,1,0:T(8,128)S(1)} %bitcast.14, f32[1,1,5,8,1024]{4,3,2,1,0:T(8,128)S(1)} %collective-permute-done.refs_1_, f32[1,1,5,8,1024]{4,3,2,1,0:T(8,128)S(1)} %collective-permute-done.1.refs_2_, ...), custom_call_target="tpu_custom_call" | custom-call | tf_op jit(solution)/shard_map/step/pallas_call | solution.py:419
Async XLA Ops:
  1.7 7.4 %copy-start = (f32[1,1,8,5,1024]{4,2,3,1,0:T(8,128)S(1)}, f32[1,1,8,5,1024]{4,2,3,1,0:T(8,128)}, u32[]{:S(2)}) copy-start(f32[1,1,8,5,1024]{4,2,3,1,0:T(8,128)} %param.6) | copy-start | bytes 491524
  1.7 15.3 %copy-start.1 = (s32[16,128]{1,0:T(8,128)S(1)}, s32[16,128]{1,0:T(8,128)}, u32[]{:S(2)}) copy-start(s32[16,128]{1,0:T(8,128)} %get-tuple-element.7.meta_ref) | copy-start | bytes 24580
  1.7 15.3 %all-to-all-start = ((f32[8,48,128]{2,1,0:T(8,128)}), f32[8,48,128]{2,1,0:T(8,128)S(1)}, u32[]{:S(2)}, u32[]{:S(2)}) async-start(f32[8,48,128]{2,1,0:T(8,128)} %bitcast.17), calls=%async_computation | async-start | bytes 393216 | tf_op jit(solution)/shard_map/all_to_all | solution.py:397
  9.1 13.0 %collective-permute-start.2 = (f32[1,1,5,8,1024]{4,3,2,1,0:T(8,128)S(1)}, f32[1,1,5,8,1024]{4,3,2,1,0:T(8,128)S(1)}, u32[]{:S(2)}, u32[]{:S(2)}) collective-permute-start(f32[1,1,5,8,1024]{4,3,2,1,0:T(8,128)S(1)} %bitcast.11), channel_id=1, source_target_pairs={{0,6},{2,4},{4,2},{6,0},{1,7},{3,5},{5,3},{7,1},{8,14},{10,12},{12... | collective-permute-start | bytes 491528 | tf_op jit(solution)/shard_map/ppermute | solution.py:384
  9.8 12.2 %collective-permute-start.1 = (f32[1,1,5,8,1024]{4,3,2,1,0:T(8,128)S(1)}, f32[1,1,5,8,1024]{4,3,2,1,0:T(8,128)S(1)}, u32[]{:S(2)}, u32[]{:S(2)}) collective-permute-start(f32[1,1,5,8,1024]{4,3,2,1,0:T(8,128)S(1)} %bitcast.12), channel_id=1, source_target_pairs={{0,4},{2,6},{4,0},{6,2},{1,5},{3,7},{5,1},{7,3},{8,12},{10,14},{12... | collective-permute-start | bytes 491528 | tf_op jit(solution)/shard_map/ppermute | solution.py:384
  10.7 11.3 %collective-permute-start = (f32[1,1,5,8,1024]{4,3,2,1,0:T(8,128)S(1)}, f32[1,1,5,8,1024]{4,3,2,1,0:T(8,128)S(1)}, u32[]{:S(2)}, u32[]{:S(2)}) collective-permute-start(f32[1,1,5,8,1024]{4,3,2,1,0:T(8,128)S(1)} %bitcast.13), channel_id=1, source_target_pairs={{0,2},{2,0},{4,6},{6,4},{1,3},{3,1},{5,7},{7,5},{8,10},{10,8},{12,... | collective-permute-start | bytes 491528 | tf_op jit(solution)/shard_map/ppermute | solution.py:384
  17.9 5.4 %copy-start.2 = (s32[1,1,32,4]{2,3,1,0:T(4,128)S(1)}, s32[1,1,32,4]{2,3,1,0:T(4,128)}, u32[]{:S(2)}) copy-start(s32[1,1,32,4]{2,3,1,0:T(4,128)} %param.9) | copy-start | bytes 1540
  17.9 4.1 %collective-permute-start.4 = (f32[88,128]{1,0:T(8,128)S(1)}, f32[88,128]{1,0:T(8,128)S(1)}, u32[]{:S(2)}, u32[]{:S(2)}) collective-permute-start(f32[88,128]{1,0:T(8,128)S(1)} %strips.1.refs_4_), channel_id=1, source_target_pairs={{0,4},{2,6},{4,0},{6,2},{1,5},{3,7},{5,1},{7,3},{8,12},{10,14},{12... | collective-permute-start | bytes 135176 | tf_op jit(solution)/shard_map/ppermute | solution.py:379
  19.5 2.6 %collective-permute-start.3 = (f32[88,128]{1,0:T(8,128)S(1)}, f32[88,128]{1,0:T(8,128)S(1)}, u32[]{:S(2)}, u32[]{:S(2)}) collective-permute-start(f32[88,128]{1,0:T(8,128)S(1)} %strips.1.refs_4_), channel_id=1, source_target_pairs={{0,2},{2,0},{4,6},{6,4},{1,3},{3,1},{5,7},{7,5},{8,10},{10,8},{12,... | collective-permute-start | bytes 135176 | tf_op jit(solution)/shard_map/ppermute | solution.py:379
  22.1 1.2 %collective-permute-start.5 = (f32[88,128]{1,0:T(8,128)S(1)}, f32[88,128]{1,0:T(8,128)S(1)}, u32[]{:S(2)}, u32[]{:S(2)}) collective-permute-start(f32[88,128]{1,0:T(8,128)S(1)} %collective-permute-done.4.refs_6_), channel_id=1, source_target_pairs={{0,2},{2,0},{4,6},{6,4},{1,3},{3,1},{5,7},{7,5},{8,10},{10,8},{12,... | collective-permute-start | bytes 135176 | tf_op jit(solution)/shard_map/ppermute | solution.py:379
  23.3 0.7 %copy-start.3 = (s32[1,1,32,1]{2,3,1,0:T(1,128)S(1)}, s32[1,1,32,1]{2,3,1,0:T(1,128)}, u32[]{:S(2)}) copy-start(s32[1,1,32,1]{2,3,1,0:T(1,128)} %param.8) | copy-start | bytes 388

commit v3 on v2

--- a/solution.py
+++ b/solution.py
@@ -30,6 +30,10 @@
     return (row + 1) * SPAN + SUB + column
 
 
+def power_of_two(n):
+    return n & (n - 1) == 0
+
+
 def masks_of(n):
     return [n >> (i + 1) for i in range(n.bit_length() - 1)]
 
@@ -73,18 +77,23 @@
     return jnp.maximum(jnp.abs(vx), jnp.abs(vy)) + sound
 
 
-def pack_kernel(parts, tiles, rows, patches, patch_ref, box_ref, which_ref, start_ref, pay_ref, meta_ref):
+def place_of(me, other, n):
+    if power_of_two(n):
+        return me ^ other
+    behind = me - other
+    return jnp.where(behind < 0, behind + n, behind)
+
+
+def pack_kernel(tiles, rows, patches, mesh_sizes, patch_ref, box_ref, which_ref, start_ref, pay_ref, meta_ref):
+    n_gx, n_gz = mesh_sizes
     me = lax.axis_index("gy")
     top = None
     for s in range(SUB):
         wave = top_speed([patch_ref[0, 0, f, :, s * LANE : (s + 1) * LANE] for f in range(FIELDS)])
         top = wave if top is None else jnp.maximum(top, wave)
-    pieces = [box_ref[pl.ds(f * BOX_ROWS + me * tiles, tiles), :] for f in range(FIELDS)]
-    for k in range(parts):
-        for f in range(FIELDS):
-            at = k * rows + f * tiles
-            pay_ref[at : at + tiles, :] = pieces[f]
-        pay_ref[(k + 1) * rows - SUB : (k + 1) * rows, :] = top
+    for f in range(FIELDS):
+        pay_ref[f * tiles : (f + 1) * tiles, :] = box_ref[pl.ds(f * BOX_ROWS + me * tiles, tiles), :]
+    pay_ref[rows - SUB : rows, :] = top
 
     start = start_ref[0, 0]
     row = lax.shift_right_logical(start * 2675, 17)
@@ -92,7 +101,12 @@
     near = lax.shift_right_logical(row, 1) - me * tiles
     mine = (near >= 0) & (near < tiles)
     patch = lax.broadcasted_iota(jnp.int32, start.shape, 1)
-    meta_ref[0:4, 0:patches] = which_ref[0, 0] * rows + jnp.where(mine, near, 0)
+    which = which_ref[0, 0]
+    gz_bits = n_gz.bit_length() - 1
+    place = place_of(lax.axis_index("gx"), lax.shift_right_logical(which, gz_bits), n_gx) + n_gx * place_of(
+        lax.axis_index("gz"), which & (n_gz - 1), n_gz
+    )
+    meta_ref[0:4, 0:patches] = place * rows + jnp.where(mine, near, 0)
     meta_ref[4:8, 0:patches] = (HALF * (patch & (SUB - 1)) - offset) & (LANE - 1)
     meta_ref[8:12, 0:patches] = jnp.where(mine, patch & (SUB - 1), -1)
 
@@ -371,39 +385,47 @@
     def sides_first(x):
         return jnp.swapaxes(x, 2, 3)
 
-    def to_group(x):
-        blocks = [x] + [None] * (group - 1)
-        have = [0]
-        for mask in masks_of(group):
-            for k in have:
-                blocks[k ^ mask] = lax.ppermute(blocks[k], "gy", [(i, i ^ mask) for i in range(group)])
-            have = have + [k ^ mask for k in have]
-        return blocks
-
     raw = sides_first(patch_state)
-    raws = [raw] + [lax.ppermute(raw, "gy", [(i, i ^ k) for i in range(group)]) for k in range(1, group)]
-
     payload, meta = pl.pallas_call(
-        functools.partial(pack_kernel, parts, tiles, rows, patches),
-        out_shape=(
-            jax.ShapeDtypeStruct((parts * rows, LANE), f32),
-            jax.ShapeDtypeStruct((16, max(LANE, patches)), jnp.int32),
-        ),
+        functools.partial(pack_kernel, tiles, rows, patches, (n_gx, n_gz)),
+        out_shape=(pltpu.VMEM((rows, LANE), f32), jax.ShapeDtypeStruct((16, max(LANE, patches)), jnp.int32)),
         in_specs=[vmem] * 4,
         out_specs=(vmem,) * 2,
         name="pack",
     )(raw, coarse_boxes.reshape(FIELDS * BOX_ROWS, LANE), sides_first(coarse_box), sides_first(coarse_start))
 
-    payload = lax.all_to_all(payload, ("gx", "gz"), split_axis=0, concat_axis=0, tiled=True)
+    def gathered(x, axis, n):
+        if power_of_two(n):
+            perms = [[(i, i ^ k) for i in range(n)] for k in range(1, n)]
+        else:
+            perms = [[(i, (i + k) % n) for i in range(n)] for k in range(1, n)]
+        return jnp.concatenate([x] + [lax.ppermute(x, axis, perm) for perm in perms], axis=0)
+
+    payload = gathered(gathered(payload, "gx", n_gx), "gz", n_gz)
 
     strip = pl.pallas_call(
         functools.partial(strip_kernel, parts, rows, tiles, patches),
-        out_shape=jax.ShapeDtypeStruct((strip_rows, LANE), f32),
+        out_shape=pltpu.VMEM((strip_rows, LANE), f32),
         in_specs=[smem, vmem],
         out_specs=vmem,
         compiler_params=limit(parts * rows, strip_rows),
         name="strips",
     )(meta, payload)
+
+    def to_group(x, after=None):
+        blocks, have = [x] + [None] * (group - 1), [0]
+        masks = masks_of(group)
+        for mask in masks:
+            perm = [(i, i ^ mask) for i in range(group)]
+            for k in have:
+                block = blocks[k]
+                if after is not None and mask == masks[-1] and k:
+                    block, _ = lax.optimization_barrier((block, after))
+                blocks[k ^ mask] = lax.ppermute(block, "gy", perm)
+            have = have + [k ^ mask for k in have]
+        return blocks
+
+    raws = to_group(raw, strip)
     strips = to_group(strip)
 
     sets = patches // PX

time: 30.4 us -> 29.5 us (0.970)
  waiting for transfers between devices: 9.75 us -> 9.09 us
    all_to_all x1 -> x0, starting transfers between devices: 7.38 us -> none  [per_device(): lax.all_to_all(payload, ('gx', 'gz'), split_axis=0, concat_axis=0, tiled=...]
    ppermute x6 -> x10, starting transfers between devices: 3.51 us -> 10.7 us  [the longest x4 7.17 us: gathered(): lax.ppermute(x, axis, perm)]
    all_to_all x1 -> x0, waiting for transfers between devices: 6.02 us -> none  [per_device(): lax.all_to_all(payload, ('gx', 'gz'), split_axis=0, concat_axis=0, tiled=...]
    ppermute x6 -> x10, waiting for transfers between devices: 3.73 us -> 9.09 us  [the longest x4 5.51 us: gathered(): lax.ppermute(x, axis, perm)]
    unnamed x8 -> x12, local copies, waits for them, and re-layouts: 0.67 us -> 0.68 us
  transfers between devices with their start and end apart: 7 -> 10, of which waited for: 3 -> 4; matrix products, arithmetic and copies ran while one was open for 0% -> 0% of each run, Pallas kernels for 3% -> 3%
where the time goes in v3:
time: 29.5 us; the launch traced here: 29.3 us
  starting transfers between devices  10.7 us (36%)
  waiting for transfers between devices  9.09 us (31%)
  Pallas kernels  8.74 us (30%)
  local copies, waits for them, and re-layouts  0.69 us (2%)
    ppermute x4, starting transfers between devices, gathered(): lax.ppermute(x, axis, perm)  7.17 us
    pallas_call x1, Pallas kernels, per_device(): pl.pallas_call(functools.partial(step_kernel, group, count, patches, slot...  6.22 us
    ppermute x4, waiting for transfers between devices, gathered(): lax.ppermute(x, axis, perm)  5.51 us
    ppermute x6, waiting for transfers between devices, to_group(): blocks[k ^ mask] = lax.ppermute(block, 'gy', perm)  3.58 us
    ppermute x6, starting transfers between devices, to_group(): blocks[k ^ mask] = lax.ppermute(block, 'gy', perm)  3.57 us
    pallas_call x1, Pallas kernels, per_device(): pl.pallas_call(functools.partial(pack_kernel, tiles, rows, patches, (n_gx...  1.63 us
    pallas_call x1, Pallas kernels, per_device(): pl.pallas_call(functools.partial(strip_kernel, parts, rows, tiles, patche...  0.89 us
    unnamed x12, local copies, waits for them, and re-layouts  0.68 us
  transfers between devices with their start and end apart: 10, of which 4 were waited for; matrix products, arithmetic and copies ran while one was open for 0% of the time, Pallas kernels for 3%

profile of v3, /device:TPU:0, one launch (start us, length us, event | category | flops | bytes accessed | tf_op | source)
XLA Modules:
  0.0 29.3 jit_solution(11543614845586729213)
XLA Ops:
  0.0 0.0 copy-start
  0.0 1.6 %pack.1 = (f32[48,128]{1,0:T(8,128)S(1)}, s32[16,128]{1,0:T(8,128)}) custom-call(f32[1,1,5,8,1024]{4,3,2,1,0:T(8,128)} %bitcast.7, f32[160,128]{1,0:T(8,128)} %bitcast.13, s32[1,1,4,32]{3,2,1,0:T(4,128)} %bitcast.14, s32[1,1,4,32]{3,2,1,0:T(4,128)} %bitcast.15), custom_call_target="tpu_custom_call" | custom-call | tf_op jit(solution)/shard_map/pack/pallas_call | solution.py:389
  1.6 5.0 %collective-permute-start.4 = (f32[48,128]{1,0:T(8,128)S(1)}, f32[48,128]{1,0:T(8,128)S(1)}, u32[]{:S(2)}, u32[]{:S(2)}) collective-permute-start(f32[48,128]{1,0:T(8,128)S(1)} %get-tuple-element.9), channel_id=1, source_target_pairs={{0,24},{8,16},{16,8},{24,0},{1,25},{9,17},{17,9},{25,1},{2,26},{10... | collective-permute-start | bytes 73736 | tf_op jit(solution)/shard_map/ppermute | solution.py:402
  6.7 0.0 collective-permute-start.3
  6.7 0.6 %collective-permute-start.2 = (f32[48,128]{1,0:T(8,128)S(1)}, f32[48,128]{1,0:T(8,128)S(1)}, u32[]{:S(2)}, u32[]{:S(2)}) collective-permute-start(f32[48,128]{1,0:T(8,128)S(1)} %get-tuple-element.9), channel_id=1, source_target_pairs={{0,8},{8,0},{16,24},{24,16},{1,9},{9,1},{17,25},{25,17},{2,10},{10... | collective-permute-start | bytes 73736 | tf_op jit(solution)/shard_map/ppermute | solution.py:402
  7.3 0.0 copy-done
  7.3 1.7 %collective-permute-start.1 = (f32[1,1,5,8,1024]{4,3,2,1,0:T(8,128)S(1)}, f32[1,1,5,8,1024]{4,3,2,1,0:T(8,128)S(1)}, u32[]{:S(2)}, u32[]{:S(2)}) collective-permute-start(f32[1,1,5,8,1024]{4,3,2,1,0:T(8,128)S(1)} %bitcast.8), channel_id=1, source_target_pairs={{0,4},{2,6},{4,0},{6,2},{1,5},{3,7},{5,1},{7,3},{8,12},{10,14},{12... | collective-permute-start | bytes 491528 | tf_op jit(solution)/shard_map/ppermute | solution.py:424
  9.0 0.0 collective-permute-start
  9.0 0.0 collective-permute-done.4
  9.0 2.4 %collective-permute-done.3 = f32[48,128]{1,0:T(8,128)S(1)} collective-permute-done((f32[48,128]{1,0:T(8,128)S(1)}, f32[48,128]{1,0:T(8,128)S(1)}, u32[]{:S(2)}, u32[]{:S(2)}) %collective-permute-start.3) | collective-permute-done | bytes 24608 | tf_op jit(solution)/shard_map/ppermute | solution.py:402
  11.4 0.0 collective-permute-done.2
  11.4 1.6 %collective-permute-start.5 = (f32[192,128]{1,0:T(8,128)S(1)}, f32[192,128]{1,0:T(8,128)S(1)}, u32[]{:S(2)}, u32[]{:S(2)}) collective-permute-start(f32[192,128]{1,0:T(8,128)S(1)} %pad_maximum_fusion), channel_id=1, source_target_pairs={{0,1},{1,0},{2,3},{3,2},{4,5},{5,4},{6,7},{7,6},{8,9},{9,8},{10,11... | collective-permute-start | bytes 294920 | tf_op jit(solution)/shard_map/ppermute | solution.py:402
  13.0 0.0 copy-start.1
  13.0 3.1 %collective-permute-done.5 = f32[192,128]{1,0:T(8,128)S(1)} collective-permute-done((f32[192,128]{1,0:T(8,128)S(1)}, f32[192,128]{1,0:T(8,128)S(1)}, u32[]{:S(2)}, u32[]{:S(2)}) %collective-permute-start.5) | collective-permute-done | bytes 98336 | tf_op jit(solution)/shard_map/ppermute | solution.py:402
  16.1 0.0 copy-done.1
  16.1 0.9 %strips.1.refs_4_ = f32[88,128]{1,0:T(8,128)S(1)} custom-call(s32[16,128]{1,0:T(8,128)S(1)} %copy-done.1, f32[384,128]{1,0:T(8,128)S(1)} %constant_dynamic-update-slice_fusion.pay_ref), custom_call_target="tpu_custom_call" | custom-call | tf_op jit(solution)/shard_map/strips/pallas_call | solution.py:406
  17.0 0.0 copy-start.2
  17.0 0.0 collective-permute-done.1.refs_2_
  17.1 0.1 collective-permute-start.6
  17.1 1.6 %collective-permute-start.8 = (f32[88,128]{1,0:T(8,128)S(1)}, f32[88,128]{1,0:T(8,128)S(1)}, u32[]{:S(2)}, u32[]{:S(2)}) collective-permute-start(f32[88,128]{1,0:T(8,128)S(1)} %strips.1.refs_4_), channel_id=1, source_target_pairs={{0,4},{2,6},{4,0},{6,2},{1,5},{3,7},{5,1},{7,3},{8,12},{10,14},{12... | collective-permute-start | bytes 135176 | tf_op jit(solution)/shard_map/ppermute | solution.py:424
  18.7 0.2 collective-permute-start.7
  18.9 2.4 %collective-permute-done.8.refs_6_ = f32[88,128]{1,0:T(8,128)S(1)} collective-permute-done((f32[88,128]{1,0:T(8,128)S(1)}, f32[88,128]{1,0:T(8,128)S(1)}, u32[]{:S(2)}, u32[]{:S(2)}) %collective-permute-start.8) | collective-permute-done | bytes 45088 | tf_op jit(solution)/shard_map/ppermute | solution.py:424
  21.2 0.0 collective-permute-start.9
  21.2 0.0 collective-permute-done.refs_1_
  21.2 0.0 collective-permute-done.7.refs_5_
  21.3 1.2 %collective-permute-done.9.refs_7_ = f32[88,128]{1,0:T(8,128)S(1)} collective-permute-done((f32[88,128]{1,0:T(8,128)S(1)}, f32[88,128]{1,0:T(8,128)S(1)}, u32[]{:S(2)}, u32[]{:S(2)}) %collective-permute-start.9) | collective-permute-done | bytes 45088 | tf_op jit(solution)/shard_map/ppermute | solution.py:424
  22.5 0.0 collective-permute-done.6.refs_3_
  22.5 0.0 copy-start.3
  22.5 0.0 copy-done.2
  22.5 0.6 %copy-done.3 = s32[1,1,32,1]{2,3,1,0:T(1,128)S(1)} copy-done((s32[1,1,32,1]{2,3,1,0:T(1,128)S(1)}, s32[1,1,32,1]{2,3,1,0:T(1,128)}, u32[]{:S(2)}) %copy-start.3) | copy-done | bytes 152
  23.1 6.2 %step.1 = f32[1,1,5,16,1024]{4,3,2,1,0:T(8,128)} custom-call(s32[1,1,4,32]{3,2,1,0:T(4,128)S(1)} %bitcast.11, s32[1,1,1,32]{3,2,1,0:T(1,128)S(1)} %bitcast.12, f32[1,1,5,8,1024]{4,3,2,1,0:T(8,128)S(1)} %bitcast.10, f32[1,1,5,8,1024]{4,3,2,1,0:T(8,128)S(1)} %collective-permute-done.refs_1_, f32[1,1,5,8,1024]{4,3,2,1,0:T(8,128)S(1)} %collective-permute-done.1.refs_2_, ...), custom_call_target="tpu_custom_call" | custom-call | tf_op jit(solution)/shard_map/step/pallas_call | solution.py:441
  (6 shorter events, 0.0 us)
Async XLA Ops:
  0.0 7.3 %copy-start = (f32[1,1,8,5,1024]{4,2,3,1,0:T(8,128)S(1)}, f32[1,1,8,5,1024]{4,2,3,1,0:T(8,128)}, u32[]{:S(2)}) copy-start(f32[1,1,8,5,1024]{4,2,3,1,0:T(8,128)} %param.6) | copy-start | bytes 491524
  1.6 7.4 %collective-permute-start.4 = (f32[48,128]{1,0:T(8,128)S(1)}, f32[48,128]{1,0:T(8,128)S(1)}, u32[]{:S(2)}, u32[]{:S(2)}) collective-permute-start(f32[48,128]{1,0:T(8,128)S(1)} %get-tuple-element.9), channel_id=1, source_target_pairs={{0,24},{8,16},{16,8},{24,0},{1,25},{9,17},{17,9},{25,1},{2,26},{10... | collective-permute-start | bytes 73736 | tf_op jit(solution)/shard_map/ppermute | solution.py:402
  6.7 4.7 %collective-permute-start.3 = (f32[48,128]{1,0:T(8,128)S(1)}, f32[48,128]{1,0:T(8,128)S(1)}, u32[]{:S(2)}, u32[]{:S(2)}) collective-permute-start(f32[48,128]{1,0:T(8,128)S(1)} %get-tuple-element.9), channel_id=1, source_target_pairs={{0,16},{8,24},{16,0},{24,8},{1,17},{9,25},{17,1},{25,9},{2,18},{10... | collective-permute-start | bytes 73736 | tf_op jit(solution)/shard_map/ppermute | solution.py:402
  6.7 4.7 %collective-permute-start.2 = (f32[48,128]{1,0:T(8,128)S(1)}, f32[48,128]{1,0:T(8,128)S(1)}, u32[]{:S(2)}, u32[]{:S(2)}) collective-permute-start(f32[48,128]{1,0:T(8,128)S(1)} %get-tuple-element.9), channel_id=1, source_target_pairs={{0,8},{8,0},{16,24},{24,16},{1,9},{9,1},{17,25},{25,17},{2,10},{10... | collective-permute-start | bytes 73736 | tf_op jit(solution)/shard_map/ppermute | solution.py:402
  7.3 9.8 %collective-permute-start.1 = (f32[1,1,5,8,1024]{4,3,2,1,0:T(8,128)S(1)}, f32[1,1,5,8,1024]{4,3,2,1,0:T(8,128)S(1)}, u32[]{:S(2)}, u32[]{:S(2)}) collective-permute-start(f32[1,1,5,8,1024]{4,3,2,1,0:T(8,128)S(1)} %bitcast.8), channel_id=1, source_target_pairs={{0,4},{2,6},{4,0},{6,2},{1,5},{3,7},{5,1},{7,3},{8,12},{10,14},{12... | collective-permute-start | bytes 491528 | tf_op jit(solution)/shard_map/ppermute | solution.py:424
  9.0 12.3 %collective-permute-start = (f32[1,1,5,8,1024]{4,3,2,1,0:T(8,128)S(1)}, f32[1,1,5,8,1024]{4,3,2,1,0:T(8,128)S(1)}, u32[]{:S(2)}, u32[]{:S(2)}) collective-permute-start(f32[1,1,5,8,1024]{4,3,2,1,0:T(8,128)S(1)} %bitcast.9), channel_id=1, source_target_pairs={{0,2},{2,0},{4,6},{6,4},{1,3},{3,1},{5,7},{7,5},{8,10},{10,8},{12,... | collective-permute-start | bytes 491528 | tf_op jit(solution)/shard_map/ppermute | solution.py:424
  11.4 4.7 %collective-permute-start.5 = (f32[192,128]{1,0:T(8,128)S(1)}, f32[192,128]{1,0:T(8,128)S(1)}, u32[]{:S(2)}, u32[]{:S(2)}) collective-permute-start(f32[192,128]{1,0:T(8,128)S(1)} %pad_maximum_fusion), channel_id=1, source_target_pairs={{0,1},{1,0},{2,3},{3,2},{4,5},{5,4},{6,7},{7,6},{8,9},{9,8},{10,11... | collective-permute-start | bytes 294920 | tf_op jit(solution)/shard_map/ppermute | solution.py:402
  13.0 3.1 %copy-start.1 = (s32[16,128]{1,0:T(8,128)S(1)}, s32[16,128]{1,0:T(8,128)}, u32[]{:S(2)}) copy-start(s32[16,128]{1,0:T(8,128)} %get-tuple-element.8.meta_ref) | copy-start | bytes 24580
  17.0 5.4 %copy-start.2 = (s32[1,1,32,4]{2,3,1,0:T(4,128)S(1)}, s32[1,1,32,4]{2,3,1,0:T(4,128)}, u32[]{:S(2)}) copy-start(s32[1,1,32,4]{2,3,1,0:T(4,128)} %param.9) | copy-start | bytes 1540
  17.1 5.4 %collective-permute-start.6 = (f32[1,1,5,8,1024]{4,3,2,1,0:T(8,128)S(1)}, f32[1,1,5,8,1024]{4,3,2,1,0:T(8,128)S(1)}, u32[]{:S(2)}, u32[]{:S(2)}) collective-permute-start(f32[1,1,5,8,1024]{4,3,2,1,0:T(8,128)S(1)} %collective-permute-done.1.refs_2_), channel_id=1, source_target_pairs={{0,2},{2,0},{4,6},{6,4},{1,3},{3,1},{5,7},{7,5},{8,10},{10,8},{12,... | collective-permute-start | bytes 491528 | tf_op jit(solution)/shard_map/ppermute | solution.py:424
  17.1 4.1 %collective-permute-start.8 = (f32[88,128]{1,0:T(8,128)S(1)}, f32[88,128]{1,0:T(8,128)S(1)}, u32[]{:S(2)}, u32[]{:S(2)}) collective-permute-start(f32[88,128]{1,0:T(8,128)S(1)} %strips.1.refs_4_), channel_id=1, source_target_pairs={{0,4},{2,6},{4,0},{6,2},{1,5},{3,7},{5,1},{7,3},{8,12},{10,14},{12... | collective-permute-start | bytes 135176 | tf_op jit(solution)/shard_map/ppermute | solution.py:424
  18.7 2.5 %collective-permute-start.7 = (f32[88,128]{1,0:T(8,128)S(1)}, f32[88,128]{1,0:T(8,128)S(1)}, u32[]{:S(2)}, u32[]{:S(2)}) collective-permute-start(f32[88,128]{1,0:T(8,128)S(1)} %strips.1.refs_4_), channel_id=1, source_target_pairs={{0,2},{2,0},{4,6},{6,4},{1,3},{3,1},{5,7},{7,5},{8,10},{10,8},{12,... | collective-permute-start | bytes 135176 | tf_op jit(solution)/shard_map/ppermute | solution.py:424
  21.2 1.2 %collective-permute-start.9 = (f32[88,128]{1,0:T(8,128)S(1)}, f32[88,128]{1,0:T(8,128)S(1)}, u32[]{:S(2)}, u32[]{:S(2)}) collective-permute-start(f32[88,128]{1,0:T(8,128)S(1)} %collective-permute-done.8.refs_6_), channel_id=1, source_target_pairs={{0,2},{2,0},{4,6},{6,4},{1,3},{3,1},{5,7},{7,5},{8,10},{10,8},{12,... | collective-permute-start | bytes 135176 | tf_op jit(solution)/shard_map/ppermute | solution.py:424
  22.5 0.7 %copy-start.3 = (s32[1,1,32,1]{2,3,1,0:T(1,128)S(1)}, s32[1,1,32,1]{2,3,1,0:T(1,128)}, u32[]{:S(2)}) copy-start(s32[1,1,32,1]{2,3,1,0:T(1,128)} %param.8) | copy-start | bytes 388

commit v4 on v3

v4 whole, which is shorter than its diff:
```python
import functools

import jax
import jax.numpy as jnp
from jax import lax
from jax.experimental import pallas as pl
from jax.experimental.pallas import tpu as pltpu
from jax.sharding import PartitionSpec as P

FIELDS = 5
PX = 32
BOX = 64
SUB = 8
LANE = 128
HALF = PX // 2
STRIDE = BOX - HALF + 1
BOX_ROWS = BOX * BOX // LANE
heat_ratio = 1.4
courant = 0.3
WEST, EAST, SOUTH, NORTH = range(4)
BLOCKS = LANE // PX
DEEP = PX // BLOCKS
SPAN = PX + 2 * SUB
PLANE = (DEEP + 2) * SPAN
FACES = PX + SUB
AUX = 2 * (FIELDS + 1)


def spot(row, column):
    return (row + 1) * SPAN + SUB + column


def power_of_two(n):
    return n & (n - 1) == 0


def masks_of(n):
    return [n >> (i + 1) for i in range(n.bit_length() - 1)]


def primitive(u):
    inverse = 1.0 / u[0]
    vx, vy, vz = u[1] * inverse, u[2] * inverse, u[3] * inverse
    kinetic = u[1] * (0.5 * vx) + u[2] * (0.5 * vy) + u[3] * (0.5 * vz)
    pressure = (heat_ratio - 1.0) * (u[4] - kinetic)
    sound = jnp.sqrt(heat_ratio * pressure * inverse)
    return vx, vy, pressure, sound


def half_flux(u, moving, pressure, sound, normal):
    half = 0.5 * moving
    flux = [u[f] * half for f in range(FIELDS)]
    flux[normal] = flux[normal] + 0.5 * pressure
    flux[4] = flux[4] + pressure * half
    return flux + [0.5 * (jnp.abs(moving) + sound)]


def face_flux(low_u, low_aux, u, aux):
    wave = jnp.maximum(low_aux[FIELDS], aux[FIELDS])
    return [low_aux[f] + aux[f] - wave * (u[f] - low_u[f]) for f in range(FIELDS)]


def lane_of():
    return lax.broadcasted_iota(jnp.int32, (SUB, LANE), 1)


def sub_of():
    return lax.broadcasted_iota(jnp.int32, (SUB, LANE), 0)


def take_lanes(x, lanes):
    return jnp.take_along_axis(x, lanes, axis=1, mode="promise_in_bounds")


def top_speed(u):
    vx, vy, _, sound = primitive(u)
    return jnp.maximum(jnp.abs(vx), jnp.abs(vy)) + sound


def place_of(me, other, n):
    if power_of_two(n):
        return me ^ other
    behind = me - other
    return jnp.where(behind < 0, behind + n, behind)


def pack_kernel(tiles, rows, patches, mesh_sizes, patch_ref, box_ref, which_ref, start_ref, pay_ref, meta_ref):
    n_gx, n_gz = mesh_sizes
    me = lax.axis_index("gy")
    top = None
    for s in range(SUB):
        wave = top_speed([patch_ref[0, 0, f, :, s * LANE : (s + 1) * LANE] for f in range(FIELDS)])
        top = wave if top is None else jnp.maximum(top, wave)
    for f in range(FIELDS):
        pay_ref[f * tiles : (f + 1) * tiles, :] = box_ref[pl.ds(f * BOX_ROWS + me * tiles, tiles), :]
    pay_ref[rows - SUB : rows, :] = top

    start = start_ref[0, 0]
    row = lax.shift_right_logical(start * 2675, 17)
    offset = BOX * (row & 1) + start - row * STRIDE
    near = lax.shift_right_logical(row, 1) - me * tiles
    mine = (near >= 0) & (near < tiles)
    patch = lax.broadcasted_iota(jnp.int32, start.shape, 1)
    which = which_ref[0, 0]
    gz_bits = n_gz.bit_length() - 1
    place = place_of(lax.axis_index("gx"), lax.shift_right_logical(which, gz_bits), n_gx) + n_gx * place_of(
        lax.axis_index("gz"), which & (n_gz - 1), n_gz
    )
    meta_ref[0:4, 0:patches] = place * rows + jnp.where(mine, near, 0)
    meta_ref[4:8, 0:patches] = (HALF * (patch & (SUB - 1)) - offset) & (LANE - 1)
    meta_ref[8:12, 0:patches] = jnp.where(mine, patch & (SUB - 1), -1)


def strip_kernel(parts, rows, tiles, patches, meta_ref, pay_ref, out_ref):
    top = pay_ref[rows - SUB : rows, :]
    for k in range(1, parts):
        top = jnp.maximum(top, pay_ref[(k + 1) * rows - SUB : (k + 1) * rows, :])
    block = lane_of() // HALF
    lines = 4 * patches // SUB
    out_ref[FIELDS * lines :, :] = top

    for v in range(lines):
        side, first = v // (patches // SUB), v % (patches // SUB) * SUB
        acc = jnp.zeros((SUB, LANE), jnp.float32)
        for m in range(SUB):
            p = first + m
            at, shift, fills = meta_ref[side, p], meta_ref[4 + side, p], meta_ref[8 + side, p]
            strip = pay_ref[pl.ds(at, FIELDS, stride=tiles), :]
            strip = jnp.concatenate([strip, jnp.zeros((SUB - FIELDS, LANE), jnp.float32)], axis=0)
            acc = jnp.where(block == fills, pltpu.roll(strip, shift, 1), acc)
        out_ref[pl.ds(v, FIELDS, stride=lines), :] = acc[:FIELDS, :]


def lanes_at(lanes_ref, g, side, kind):
    at = ((g * 4 + side) * 3 + kind) * SUB
    return lanes_ref[at : at + SUB, :]


def held_at(lanes_ref, sets):
    return lanes_ref[sets * 4 * 3 * SUB : (sets * 4 * 3 + 1) * SUB, :]


def fill_ghosts(u_ref, lanes_ref, coarse_ref, sets):
    for f in range(FIELDS):
        for g in range(sets):

            def ghost(side, at, kept):
                x = None
                for o in range(sets):
                    start = (o * FIELDS + f) * PLANE + at
                    edge = pl.ds(start, DEEP, stride=SPAN) if side in (WEST, EAST) else pl.ds(start, SUB)
                    moved = take_lanes(u_ref[edge, :], lanes_at(lanes_ref, g, side, 0))
                    x = moved if x is None else jnp.where(lanes_at(lanes_ref, g, side, 1) == o, moved, x)
                if coarse_ref is None:
                    return x
                start = ((g * FIELDS + f) * 10 + kept) * SUB
                return jnp.where(lanes_at(lanes_ref, g, side, 2) != 0, coarse_ref[start : start + SUB, :], x)

            base = (g * FIELDS + f) * PLANE
            for side, column, to in ((WEST, PX - 1, -1), (EAST, 0, PX)):
                u_ref[pl.ds(base + spot(0, to), DEEP, stride=SPAN), :] = ghost(side, spot(0, column), side)
            for side, row, to in ((SOUTH, DEEP - 1, -1), (NORTH, 0, DEEP)):
                for i in range(BLOCKS):
                    kept = 2 + (side - SOUTH) * BLOCKS + i
                    u_ref[pl.ds(base + spot(to, SUB * i), SUB), :] = ghost(side, spot(row, SUB * i), kept)


def halves_of(u, axis):
    vx, vy, pressure, sound = primitive(u)
    return half_flux(u, (vx, vy)[axis], pressure, sound, axis + 1)


def fill_halves(u_ref, aux_ref, sets):
    def fill(g, rows, axes):
        u = [u_ref[rows((g * FIELDS + f) * PLANE), :] for f in range(FIELDS)]
        vx, vy, pressure, sound = primitive(u)
        for axis in axes:
            for n, x in enumerate(half_flux(u, (vx, vy)[axis], pressure, sound, axis + 1)):
                aux_ref[rows((g * AUX + axis * (FIELDS + 1) + n) * PLANE), :] = x

    for g in range(sets):

        def cells(r, carry):
            for half in range(2):
                for i in range(BLOCKS):
                    at = spot(2 * r + half, SUB * i)
                    fill(g, lambda b, at=at: pl.ds(pl.multiple_of(b + at, SUB), SUB), (0, 1))
            return carry

        lax.fori_loop(0, DEEP // 2, cells, 0)
        for r in (-1, DEEP):
            for i in range(BLOCKS):
                fill(g, lambda b, at=spot(r, SUB * i): pl.ds(b + at, SUB), (1,))
        for c in (-1, PX):
            fill(g, lambda b, at=spot(0, c): pl.ds(b + at, DEEP, stride=SPAN), (0,))


def load_cells(u_ref, aux_ref, g, axis, rows):
    u = [u_ref[rows((g * FIELDS + f) * PLANE), :] for f in range(FIELDS)]
    start = g * AUX + axis * (FIELDS + 1)
    return u, [aux_ref[rows((start + n) * PLANE), :] for n in range(FIELDS + 1)]


def at_row(at):
    return lambda b: pl.ds(b + at, SUB)


def fill_x_faces(u_ref, aux_ref, dx_ref, g, base):
    def across(r, carry):
        for half in range(2):
            row = 2 * r + half
            for i in range(BLOCKS + 1):
                at = pl.multiple_of(spot(row, SUB * i), SUB)
                low = load_cells(u_ref, aux_ref, g, 0, at_row(at - 1))
                faces = face_flux(*low, *load_cells(u_ref, aux_ref, g, 0, at_row(at)))
                for f in range(FIELDS):
                    to = pl.multiple_of(base + (f * DEEP + row) * FACES + SUB * i, SUB)
                    dx_ref[pl.ds(to, SUB), :] = faces[f]
        return carry

    lax.fori_loop(0, DEEP // 2, across, 0)


def x_change(dx_ref, base, f, row, i):
    west = pl.multiple_of(base + (f * DEEP + row) * FACES + SUB * i, SUB)
    return dx_ref[pl.ds(west, SUB), :] - dx_ref[pl.ds(west + 1, SUB), :]


def prepare_kernel(group, count, patches, slots, around_ref, owner_ref, *refs):
    raw_refs = refs[:group]
    u_ref, edge_ref, dx_ref, dy_ref, lanes_ref, aux_ref, table, slot_ref = refs[group:]
    me = lax.axis_index("gy")
    capacity = slots // group
    sets = patches // PX
    lane = lane_of()
    block, in_block = lane // PX, lane & (PX - 1)
    turn = me * count

    for f in range(FIELDS):
        for g in range(sets):
            for h in range(2):
                tiles = []
                for q in range(BLOCKS):
                    at = (q * 2 + h) * LANE
                    for k in range(PX // count):
                        tiles.append(raw_refs[g * (PX // count) + k][0, 0, f, :, at : at + LANE])
                cells = jnp.concatenate(tiles, axis=0).T
                for i in range(BLOCKS):
                    to = (g * FIELDS + f) * PLANE + spot(h * BLOCKS + i, 0)
                    u_ref[to : to + PX, :] = cells[i * PX : (i + 1) * PX, :]

    for i in range(slots):
        slot_ref[i] = -1

    def rank_source(source, carry):
        rank = jnp.int32(0)
        for i in range(count):
            p = source * count + i
            hit = owner_ref[0, 0, 0, p] == me
            slot_ref[jnp.where(hit, source * capacity + rank, slots)] = p
            rank = rank + jnp.where(hit, 1, 0)
        return carry

    lax.fori_loop(0, group, rank_source, 0)
    held = jnp.full((SUB, LANE), -1, jnp.int32)
    for j in range(slots):
        held = jnp.where(in_block == j, slot_ref[j], held)
    lanes_ref[sets * 4 * 3 * SUB :, :] = held

    table[0:4, 0:patches] = around_ref[0, 0]
    for g in range(sets):
        patch = (g * PX + in_block) ^ turn
        for side in range(4):
            near = take_lanes(jnp.broadcast_to(table[side : side + 1, :], (SUB, LANE)), patch)
            place = jnp.maximum(near, 0) ^ turn
            pick, origin = place & (PX - 1), lax.shift_right_logical(place, 5)
            lacking = jnp.where(near < 0, 1, 0)
            if side in (WEST, EAST):
                pick = pick + PX * block
            else:
                edge, step = (0, -PX) if side == SOUTH else (BLOCKS - 1, PX)
                across = pick + (LANE - PX if side == SOUTH else 0)
                pick = jnp.where(block == edge, across, lane + step)
                origin = jnp.where(block == edge, origin, g)
                lacking = jnp.where(block == edge, lacking, 0)
            for kind, x in enumerate((pick, origin, lacking)):
                at = ((g * 4 + side) * 3 + kind) * SUB
                lanes_ref[at : at + SUB, :] = x

    fill_ghosts(u_ref, lanes_ref, None, sets)
    fill_halves(u_ref, aux_ref, sets)
    for g in range(sets):
        fill_x_faces(u_ref, aux_ref, dx_ref, g, g * FIELDS * DEEP * FACES)

        def along(i, carry):
            low = load_cells(u_ref, aux_ref, g, 1, at_row(pl.multiple_of(spot(-1, SUB * i), SUB)))
            for r in range(DEEP + 1):
                cell = load_cells(u_ref, aux_ref, g, 1, at_row(pl.multiple_of(spot(r, SUB * i), SUB)))
                for f, face in enumerate(face_flux(*low, *cell)):
                    to = pl.multiple_of(((g * FIELDS + f) * (DEEP + 1) + r) * PX + SUB * i, SUB)
                    dy_ref[pl.ds(to, SUB), :] = face
                low = cell
            return carry

        lax.fori_loop(0, BLOCKS, along, 0)
        for side in range(4):
            for i, rows in enumerate(edge_rows(side)):
                for n in range(FIELDS + 1):
                    start = g * AUX + (0 if side in (WEST, EAST) else FIELDS + 1) + n
                    to = edge_place(g, side, i, n)
                    edge_ref[to : to + SUB, :] = aux_ref[rows(start * PLANE), :]


def edge_rows(side):
    if side in (WEST, EAST):
        at = spot(0, 0 if side == WEST else PX - 1)
        return [lambda b: pl.ds(b + at, DEEP, stride=SPAN)]
    return [at_row(spot(0 if side == SOUTH else DEEP - 1, SUB * i)) for i in range(BLOCKS)]


def edge_place(g, side, i, n):
    kept = side if side in (WEST, EAST) else 2 + (side - SOUTH) * BLOCKS + i
    return ((g * 10 + kept) * (FIELDS + 1) + n) * SUB


def step_kernel(group, count, patches, slots, *refs):
    u_ref, edge_ref, dx_ref, dy_ref, lanes_ref = refs[:5]
    strip_refs, out_ref = refs[5 : 5 + group], refs[5 + group]
    next_u, next_aux, next_dx, strips, doubled, coarse_ref, border_ref = refs[6 + group :]
    lines = 4 * patches // SUB
    sets = patches // PX
    lane, sub = lane_of(), sub_of()
    block, in_block = lane // PX, lane & (PX - 1)
    turn = lax.axis_index("gy") * count

    def joined(at, join):
        return functools.reduce(join, [ref[at : at + SUB, :] for ref in strip_refs])

    for at in range(0, FIELDS * lines, SUB):
        strips[at : at + SUB, :] = joined(at, jnp.add)
    time_step = courant / jnp.max(joined(FIELDS * lines, jnp.maximum))
    part = HALF * sub + (lane & (HALF - 1))
    for t in range(4 * patches // LANE):
        tiles = []
        for v in range(t * HALF, (t + 1) * HALF):
            tile = None
            for f in range(FIELDS):
                row = jnp.broadcast_to(strips[f * lines + v : f * lines + v + 1, :], (SUB, LANE))
                wide = take_lanes(row, part)
                tile = wide if tile is None else jnp.where(lane // HALF == f, wide, tile)
            tiles.append(tile)
        cells = jnp.concatenate(tiles, axis=0).T
        for n in range(FIELDS * 2):
            for twice in range(2):
                at = t * FIELDS * PX + n * HALF + twice
                doubled[pl.ds(at, SUB, stride=2), :] = cells[n * SUB : (n + 1) * SUB, :]

    for g in range(sets):
        patch = (g * PX + in_block) ^ turn
        for side in range(4):
            t, shift = side * patches // LANE, side * patches % LANE
            for f in range(FIELDS):
                pieces = []
                for i in range(BLOCKS):
                    at = t * FIELDS * PX + f * PX + SUB * i
                    pieces.append(take_lanes(doubled[at : at + SUB, :], patch + shift))
                base = (g * FIELDS + f) * 10
                if side in (WEST, EAST):
                    x = pieces[0]
                    for q in range(1, BLOCKS):
                        x = jnp.where(block == q, pieces[q], x)
                    coarse_ref[(base + side) * SUB : (base + side + 1) * SUB, :] = x
                else:
                    for i in range(BLOCKS):
                        at = (base + 2 + (side - SOUTH) * BLOCKS + i) * SUB
                        coarse_ref[at : at + SUB, :] = pieces[i]

    size = FIELDS * DEEP * FACES
    for g in range(sets):
        for at in range(0, size, SUB):
            next_dx[g * size + at : g * size + at + SUB, :] = dx_ref[g * size + at : g * size + at + SUB, :]

        def coarse_cells(kept, axis):
            at = [((g * FIELDS + f) * 10 + kept) * SUB for f in range(FIELDS)]
            u = [coarse_ref[a : a + SUB, :] for a in at]
            return u, halves_of(u, axis)

        def own_cells(side, i):
            rows = edge_rows(side)[i]
            places = [edge_place(g, side, i, n) for n in range(FIELDS + 1)]
            u = [u_ref[rows((g * FIELDS + f) * PLANE), :] for f in range(FIELDS)]
            return u, [edge_ref[at : at + SUB, :] for at in places]

        for side, face in ((WEST, 0), (EAST, PX)):
            beyond, own = coarse_cells(side, 0), own_cells(side, 0)
            faces = face_flux(*beyond, *own) if side == WEST else face_flux(*own, *beyond)
            lacking = lanes_at(lanes_ref, g, side, 2) != 0
            for f in range(FIELDS):
                rows = pl.ds(g * size + f * DEEP * FACES + face, DEEP, stride=FACES)
                next_dx[rows, :] = jnp.where(lacking, faces[f], dx_ref[rows, :])
        for side, face in ((SOUTH, 0), (NORTH, DEEP)):
            lacking = lanes_at(lanes_ref, g, side, 2) != 0
            for i in range(BLOCKS):
                kept = (side - SOUTH) * BLOCKS + i
                beyond, own = coarse_cells(2 + kept, 1), own_cells(side, i)
                faces = face_flux(*beyond, *own) if side == SOUTH else face_flux(*own, *beyond)
                for f in range(FIELDS):
                    fine = ((g * FIELDS + f) * (DEEP + 1) + face) * PX + SUB * i
                    to = ((g * FIELDS + f) * 8 + kept) * SUB
                    border_ref[to : to + SUB, :] = jnp.where(lacking, faces[f], dy_ref[fine : fine + SUB, :])

        def update(f, carry):
            for i in range(BLOCKS):
                for r in range(DEEP):
                    faces = []
                    for n in (r, r + 1):
                        if n in (0, DEEP):
                            at = ((g * FIELDS + f) * 8 + (BLOCKS if n else 0) + i) * SUB
                            faces.append(border_ref[pl.ds(pl.multiple_of(at, SUB), SUB), :])
                        else:
                            at = ((g * FIELDS + f) * (DEEP + 1) + n) * PX + SUB * i
                            faces.append(dy_ref[pl.ds(pl.multiple_of(at, SUB), SUB), :])
                    change = x_change(next_dx, g * size, f, r, i) + (faces[0] - faces[1])
                    at = pl.ds(pl.multiple_of((g * FIELDS + f) * PLANE + spot(r, SUB * i), SUB), SUB)
                    next_u[at, :] = u_ref[at, :] + time_step * change
            return carry

        lax.fori_loop(0, FIELDS, update, 0)

    fill_ghosts(next_u, lanes_ref, coarse_ref, sets)
    fill_halves(next_u, next_aux, sets)
    for g in range(sets):
        fill_x_faces(next_u, next_aux, next_dx, g, g * size)

        def along(half, carry):
            for i in (2 * half, 2 * half + 1):
                low = load_cells(next_u, next_aux, g, 1, at_row(pl.multiple_of(spot(-1, SUB * i), SUB)))
                low_faces = None
                for r in range(DEEP + 1):
                    cell = load_cells(next_u, next_aux, g, 1, at_row(pl.multiple_of(spot(r, SUB * i), SUB)))
                    faces = face_flux(*low, *cell)
                    for f in range(FIELDS):
                        if r == 0:
                            continue
                        change = x_change(next_dx, g * size, f, r - 1, i) + (low_faces[f] - faces[f])
                        new = low[0][f] + time_step * change
                        at = pl.ds(pl.multiple_of((g * FIELDS + f) * PLANE + spot(r - 1, SUB * i), SUB), SUB)
                        next_u[at, :] = 0.5 * u_ref[at, :] + 0.5 * new
                    low, low_faces = cell, faces
            return carry

        lax.fori_loop(0, BLOCKS // 2, along, 0)

    held = held_at(lanes_ref, sets)
    place = jnp.maximum(held, 0) ^ turn
    pick, origin = PX * block + (place & (PX - 1)), lax.shift_right_logical(place, 5)
    for f in range(FIELDS):
        for h in range(2):
            tiles = []
            for i in range(LANE // SUB):
                at = spot(h * BLOCKS + i // BLOCKS, SUB * (i % BLOCKS))
                x = None
                for g in range(sets):
                    start = (g * FIELDS + f) * PLANE + at
                    moved = take_lanes(next_u[start : start + SUB, :], pick)
                    x = moved if x is None else jnp.where(origin == g, moved, x)
                tiles.append(jnp.where(held >= 0, x, 0.0))
            cells = jnp.concatenate(tiles, axis=0).T
            for q in range(BLOCKS):
                at = (q * 2 + h) * LANE
                out_ref[0, 0, f, :, at : at + LANE] = cells[q * PX : q * PX + slots, :]


def limit(*row_counts):
    return pltpu.CompilerParams(vmem_limit_bytes=(sum(row_counts) * LANE * 4 * 5 // 4) + (1 << 20))


def per_device(patch_state, coarse_boxes, new_owner, neighbors, coarse_box, coarse_start):
    count = patch_state.shape[2]
    n_gx, n_gz, group = lax.axis_size("gx"), lax.axis_size("gz"), lax.axis_size("gy")
    parts = n_gx * n_gz
    patches = count * group
    lines = 4 * patches // SUB
    slots = group * max(2, 2 * count // group)
    tiles = BOX_ROWS // group
    rows = -(-tiles * FIELDS // SUB) * SUB + SUB
    strip_rows = FIELDS * lines + SUB
    vmem = pl.BlockSpec(memory_space=pltpu.VMEM)
    smem = pl.BlockSpec(memory_space=pltpu.SMEM)
    f32 = jnp.float32

    def sides_first(x):
        return jnp.swapaxes(x, 2, 3)

    raw = sides_first(patch_state)
    payload, meta = pl.pallas_call(
        functools.partial(pack_kernel, tiles, rows, patches, (n_gx, n_gz)),
        out_shape=(pltpu.VMEM((rows, LANE), f32), jax.ShapeDtypeStruct((16, max(LANE, patches)), jnp.int32)),
        in_specs=[vmem] * 4,
        out_specs=(vmem,) * 2,
        name="pack",
    )(raw, coarse_boxes.reshape(FIELDS * BOX_ROWS, LANE), sides_first(coarse_box), sides_first(coarse_start))

    def gathered(x, axis, n):
        if power_of_two(n):
            perms = [[(i, i ^ k) for i in range(n)] for k in range(1, n)]
        else:
            perms = [[(i, (i + k) % n) for i in range(n)] for k in range(1, n)]
        return jnp.concatenate([x] + [lax.ppermute(x, axis, perm) for perm in perms], axis=0)

    payload = gathered(gathered(payload, "gx", n_gx), "gz", n_gz)

    strip = pl.pallas_call(
        functools.partial(strip_kernel, parts, rows, tiles, patches),
        out_shape=pltpu.VMEM((strip_rows, LANE), f32),
        in_specs=[smem, vmem],
        out_specs=vmem,
        compiler_params=limit(parts * rows, strip_rows),
        name="strips",
    )(meta, payload)

    def to_group(x, after=None):
        blocks, have = [x] + [None] * (group - 1), [0]
        masks = masks_of(group)
        for mask in masks:
            perm = [(i, i ^ mask) for i in range(group)]
            for k in have:
                block = blocks[k]
                if after is not None and mask == masks[-1] and k:
                    block, _ = lax.optimization_barrier((block, after))
                blocks[k ^ mask] = lax.ppermute(block, "gy", perm)
            have = have + [k ^ mask for k in have]
        return blocks

    raws = to_group(raw, strip)

    sets = patches // PX
    made_rows = [
        sets * FIELDS * PLANE,
        sets * 10 * (FIELDS + 1) * SUB,
        sets * FIELDS * DEEP * FACES,
        sets * FIELDS * (DEEP + 1) * PX,
    ]
    lane_rows = (sets * 4 * 3 + 1) * SUB
    made = pl.pallas_call(
        functools.partial(prepare_kernel, group, count, patches, slots),
        out_shape=[pltpu.VMEM((n, LANE), f32) for n in made_rows] + [pltpu.VMEM((lane_rows, LANE), jnp.int32)],
        in_specs=[vmem, smem] + [vmem] * group,
        out_specs=[vmem] * 5,
        scratch_shapes=[
            pltpu.VMEM((sets * AUX * PLANE, LANE), f32),
            pltpu.VMEM((SUB, LANE), jnp.int32),
            pltpu.SMEM((slots + 1,), jnp.int32),
        ],
        compiler_params=limit(*made_rows, sets * AUX * PLANE, lane_rows, patches * FIELDS * SUB),
        cost_estimate=pl.CostEstimate(flops=patches * 1024 * 300, bytes_accessed=patches * 40000, transcendentals=0),
        name="prepare",
    )(sides_first(neighbors), sides_first(new_owner), *raws)

    strips = to_group(strip, made[4])
    scratch_rows = [sets * FIELDS * PLANE, sets * AUX * PLANE, sets * FIELDS * DEEP * FACES] + [
        FIELDS * lines,
        4 * patches // LANE * FIELDS * PX,
        sets * FIELDS * 10 * SUB,
        sets * FIELDS * 8 * SUB,
    ]
    out = pl.pallas_call(
        functools.partial(step_kernel, group, count, patches, slots),
        out_shape=jax.ShapeDtypeStruct((1, 1, FIELDS, slots, SUB * LANE), f32),
        in_specs=[vmem] * (5 + group),
        out_specs=vmem,
        scratch_shapes=[pltpu.VMEM((n, LANE), f32) for n in scratch_rows],
        compiler_params=limit(*scratch_rows, *made_rows, lane_rows, group * strip_rows, FIELDS * slots * SUB),
        name="step",
    )(*made, *strips)
    return sides_first(out)


def solution(mesh):
    in_specs = (
        P("gx", "gz", "gy", None, None),
        P(("gx", "gz"), None, None),
        P("gx", "gz", None, None),
        P("gx", "gz", None, None),
        P("gx", "gz", None, None),
        P("gx", "gz", None, None),
    )
    out_specs = P("gx", "gz", "gy", None, None)
    return jax.shard_map(
        per_device, mesh=mesh, in_specs=in_specs, out_specs=out_specs, check_vma=False
    )
```

time: 29.5 us -> 29.7 us (level)
  local copies, waits for them, and re-layouts: 0.69 us -> 2.96 us
  Pallas kernels: 8.74 us -> 7.38 us
  waiting for transfers between devices: 9.09 us -> 7.87 us
  starting transfers between devices: 10.7 us -> 11.1 us
    pallas_call x1, Pallas kernels: 6.22 us -> 3 us  [per_device(): pl.pallas_call(functools.partial(step_kernel, group, count, patches, slot...]
    ppermute x6, waiting for transfers between devices: 3.58 us -> 0.89 us  [to_group(): blocks[k ^ mask] = lax.ppermute(block, 'gy', perm)]
    unnamed x12, local copies, waits for them, and re-layouts: 0.68 us -> 2.95 us
    pallas_call x0 -> x1, Pallas kernels: none -> 1.9 us  [per_device(): pl.pallas_call(functools.partial(prepare_kernel, group, count, patches, s...]
    ppermute x4, waiting for transfers between devices: 5.51 us -> 6.98 us  [gathered(): lax.ppermute(x, axis, perm)]
    ppermute x6, starting transfers between devices: 3.57 us -> 3.97 us  [to_group(): blocks[k ^ mask] = lax.ppermute(block, 'gy', perm)]
  transfers between devices with their start and end apart: 10 -> 10, of which waited for: 4 -> 4; matrix products, arithmetic and copies ran while one was open for 0% -> 0% of each run, Pallas kernels for 3% -> 9%
where the time goes in v4:
time: 29.7 us; the launch traced here: 29.4 us
  starting transfers between devices  11.1 us (37%)
  waiting for transfers between devices  7.87 us (26%)
  Pallas kernels  7.38 us (25%)
  local copies, waits for them, and re-layouts  2.96 us (10%)
    ppermute x4, starting transfers between devices, gathered(): lax.ppermute(x, axis, perm)  7.17 us
    ppermute x4, waiting for transfers between devices, gathered(): lax.ppermute(x, axis, perm)  6.98 us
    ppermute x6, starting transfers between devices, to_group(): blocks[k ^ mask] = lax.ppermute(block, 'gy', perm)  3.97 us
    pallas_call x1, Pallas kernels, per_device(): pl.pallas_call(functools.partial(step_kernel, group, count, patches, slot...  3 us
    unnamed x12, local copies, waits for them, and re-layouts  2.95 us
    pallas_call x1, Pallas kernels, per_device(): pl.pallas_call(functools.partial(prepare_kernel, group, count, patches, s...  1.9 us
    pallas_call x1, Pallas kernels, per_device(): pl.pallas_call(functools.partial(pack_kernel, tiles, rows, patches, (n_gx...  1.59 us
    pallas_call x1, Pallas kernels, per_device(): pl.pallas_call(functools.partial(strip_kernel, parts, rows, tiles, patche...  0.89 us
  transfers between devices with their start and end apart: 10, of which 4 were waited for; matrix products, arithmetic and copies ran while one was open for 0% of the time, Pallas kernels for 9%

profile of v4, /device:TPU:0, one launch (start us, length us, event | category | flops | bytes accessed | tf_op | source)
XLA Modules:
  0.0 29.4 jit_solution(2761065949256411034)
XLA Ops:
  0.0 1.6 %pack.1 = (f32[48,128]{1,0:T(8,128)S(1)}, s32[16,128]{1,0:T(8,128)}) custom-call(f32[1,1,5,8,1024]{4,3,2,1,0:T(8,128)} %bitcast.7, f32[160,128]{1,0:T(8,128)} %bitcast.13, s32[1,1,4,32]{3,2,1,0:T(4,128)} %bitcast.14, s32[1,1,4,32]{3,2,1,0:T(4,128)} %bitcast.15), custom_call_target="tpu_custom_call" | custom-call | tf_op jit(solution)/shard_map/pack/pallas_call | solution.py:496
  1.6 3.0 %collective-permute-start.2 = (f32[48,128]{1,0:T(8,128)S(1)}, f32[48,128]{1,0:T(8,128)S(1)}, u32[]{:S(2)}, u32[]{:S(2)}) collective-permute-start(f32[48,128]{1,0:T(8,128)S(1)} %get-tuple-element.15), channel_id=1, source_target_pairs={{0,8},{8,0},{16,24},{24,16},{1,9},{9,1},{17,25},{25,17},{2,10},{10... | collective-permute-start | bytes 73736 | tf_op jit(solution)/shard_map/ppermute | solution.py:509
  4.6 2.6 %collective-permute-start.3 = (f32[48,128]{1,0:T(8,128)S(1)}, f32[48,128]{1,0:T(8,128)S(1)}, u32[]{:S(2)}, u32[]{:S(2)}) collective-permute-start(f32[48,128]{1,0:T(8,128)S(1)} %get-tuple-element.15), channel_id=1, source_target_pairs={{0,16},{8,24},{16,0},{24,8},{1,17},{9,25},{17,1},{25,9},{2,18},{10... | collective-permute-start | bytes 73736 | tf_op jit(solution)/shard_map/ppermute | solution.py:509
  7.2 0.0 collective-permute-start.4
  7.2 1.7 %collective-permute-start.1 = (f32[1,1,5,8,1024]{4,3,2,1,0:T(8,128)}, f32[1,1,5,8,1024]{4,3,2,1,0:T(8,128)S(1)}, u32[]{:S(2)}, u32[]{:S(2)}) collective-permute-start(f32[1,1,5,8,1024]{4,3,2,1,0:T(8,128)} %bitcast.8), channel_id=1, source_target_pairs={{0,4},{2,6},{4,0},{6,2},{1,5},{3,7},{5,1},{7,3},{8,12},{10,14},{12... | collective-permute-start | bytes 491528 | tf_op jit(solution)/shard_map/ppermute | solution.py:531
  9.0 0.0 collective-permute-start
  9.0 0.0 collective-permute-done.2
  9.0 0.7 %collective-permute-done.3 = f32[48,128]{1,0:T(8,128)S(1)} collective-permute-done((f32[48,128]{1,0:T(8,128)S(1)}, f32[48,128]{1,0:T(8,128)S(1)}, u32[]{:S(2)}, u32[]{:S(2)}) %collective-permute-start.3) | collective-permute-done | bytes 24608 | tf_op jit(solution)/shard_map/ppermute | solution.py:509
  9.7 3.1 %collective-permute-done.4 = f32[48,128]{1,0:T(8,128)S(1)} collective-permute-done((f32[48,128]{1,0:T(8,128)S(1)}, f32[48,128]{1,0:T(8,128)S(1)}, u32[]{:S(2)}, u32[]{:S(2)}) %collective-permute-start.4) | collective-permute-done | bytes 24608 | tf_op jit(solution)/shard_map/ppermute | solution.py:509
  12.8 1.6 %collective-permute-start.5 = (f32[192,128]{1,0:T(8,128)S(1)}, f32[192,128]{1,0:T(8,128)S(1)}, u32[]{:S(2)}, u32[]{:S(2)}) collective-permute-start(f32[192,128]{1,0:T(8,128)S(1)} %pad_maximum_fusion), channel_id=1, source_target_pairs={{0,1},{1,0},{2,3},{3,2},{4,5},{5,4},{6,7},{7,6},{8,9},{9,8},{10,11... | collective-permute-start | bytes 294920 | tf_op jit(solution)/shard_map/ppermute | solution.py:509
  14.4 3.1 %collective-permute-done.5 = f32[192,128]{1,0:T(8,128)S(1)} collective-permute-done((f32[192,128]{1,0:T(8,128)S(1)}, f32[192,128]{1,0:T(8,128)S(1)}, u32[]{:S(2)}, u32[]{:S(2)}) %collective-permute-start.5) | collective-permute-done | bytes 98336 | tf_op jit(solution)/shard_map/ppermute | solution.py:509
  17.5 0.0 copy-start.1
  17.6 0.7 %copy-done.1 = s32[16,128]{1,0:T(8,128)S(1)} copy-done((s32[16,128]{1,0:T(8,128)S(1)}, s32[16,128]{1,0:T(8,128)}, u32[]{:S(2)}) %copy-start.1) | copy-done | bytes 8216
  18.2 0.9 %strips.1.refs_5_ = f32[88,128]{1,0:T(8,128)S(1)} custom-call(s32[16,128]{1,0:T(8,128)S(1)} %copy-done.1, f32[384,128]{1,0:T(8,128)S(1)} %constant_dynamic-update-slice_fusion.pay_ref), custom_call_target="tpu_custom_call" | custom-call | tf_op jit(solution)/shard_map/strips/pallas_call | solution.py:513
  19.1 0.0 collective-permute-done.1.refs_2_
  19.1 0.1 collective-permute-start.6
  19.2 1.6 %collective-permute-start.8 = (f32[88,128]{1,0:T(8,128)S(1)}, f32[88,128]{1,0:T(8,128)S(1)}, u32[]{:S(2)}, u32[]{:S(2)}) collective-permute-start(f32[88,128]{1,0:T(8,128)S(1)} %strips.1.refs_5_), channel_id=1, source_target_pairs={{0,4},{2,6},{4,0},{6,2},{1,5},{3,7},{5,1},{7,3},{8,12},{10,14},{12... | collective-permute-start | bytes 135176 | tf_op jit(solution)/shard_map/ppermute | solution.py:531
  20.8 0.2 collective-permute-start.7
  21.0 0.0 collective-permute-done.refs_1_
  21.0 0.0 collective-permute-done.6.refs_3_
  21.0 0.0 copy-start
  21.0 0.9 %copy-done = f32[1,1,8,5,1024]{4,2,3,1,0:T(8,128)S(1)} copy-done((f32[1,1,8,5,1024]{4,2,3,1,0:T(8,128)S(1)}, f32[1,1,8,5,1024]{4,2,3,1,0:T(8,128)}, u32[]{:S(2)}) %copy-start) | copy-done | bytes 163864
  21.9 0.0 copy-start.2
  21.9 0.7 %copy-done.2 = s32[1,1,32,4]{2,3,1,0:T(4,128)S(1)} copy-done((s32[1,1,32,4]{2,3,1,0:T(4,128)S(1)}, s32[1,1,32,4]{2,3,1,0:T(4,128)}, u32[]{:S(2)}) %copy-start.2) | copy-done | bytes 536
  22.6 0.0 copy-start.3
  22.6 0.7 %copy-done.3 = s32[1,1,32,1]{2,3,1,0:T(1,128)S(1)} copy-done((s32[1,1,32,1]{2,3,1,0:T(1,128)S(1)}, s32[1,1,32,1]{2,3,1,0:T(1,128)}, u32[]{:S(2)}) %copy-start.3) | copy-done | bytes 152
  23.2 1.9 %prepare.1 = (f32[2400,128]{1,0:T(8,128)S(1)}, f32[480,128]{1,0:T(8,128)S(1)}, f32[1600,128]{1,0:T(8,128)S(1)}, f32[1440,128]{1,0:T(8,128)S(1)}, s32[104,128]{1,0:T(8,128)S(1)}) custom-call(s32[1,1,4,32]{3,2,1,0:T(4,128)S(1)} %bitcast.11, s32[1,1,1,32]{3,2,1,0:T(1,128)S(1)} %bitcast.12, f32[1,1,5,8,1024]{4,3,2,1,0:T(8,128)S(1)} %bitcast.10, ...), custom_call_target="tpu_custom_call" | custom-call | flops 9830400 | bytes 1280000 | tf_op jit(solution)/shard_map/prepare/pallas_call | solution.py:545
  25.1 0.0 collective-permute-done.8.refs_7_
  25.2 0.4 %collective-permute-start.9 = (f32[88,128]{1,0:T(8,128)S(1)}, f32[88,128]{1,0:T(8,128)S(1)}, u32[]{:S(2)}, u32[]{:S(2)}) collective-permute-start(f32[88,128]{1,0:T(8,128)S(1)} %collective-permute-done.8.refs_7_), channel_id=1, source_target_pairs={{0,2},{2,0},{4,6},{6,4},{1,3},{3,1},{5,7},{7,5},{8,10},{10,8},{12,... | collective-permute-start | bytes 135176 | tf_op jit(solution)/shard_map/ppermute | solution.py:531
  25.6 0.0 collective-permute-done.7.refs_6_
  25.6 0.9 %collective-permute-done.9.refs_8_ = f32[88,128]{1,0:T(8,128)S(1)} collective-permute-done((f32[88,128]{1,0:T(8,128)S(1)}, f32[88,128]{1,0:T(8,128)S(1)}, u32[]{:S(2)}, u32[]{:S(2)}) %collective-permute-start.9) | collective-permute-done | bytes 45088 | tf_op jit(solution)/shard_map/ppermute | solution.py:531
  26.5 3.0 %step.1 = f32[1,1,5,16,1024]{4,3,2,1,0:T(8,128)} custom-call(f32[2400,128]{1,0:T(8,128)S(1)} %get-tuple-element.17.refs_0_, f32[480,128]{1,0:T(8,128)S(1)} %get-tuple-element.18.refs_1_, f32[1600,128]{1,0:T(8,128)S(1)} %get-tuple-element.19.refs_2_, f32[1440,128]{1,0:T(8,128)S(1)} %get-tuple-element.20.refs_3_, s32[104,128]{1,0:T(8,128)S(1)} %get-tuple-element.21.refs_4_, ...), custom_call_target="tpu_custom_call" | custom-call | tf_op jit(solution)/shard_map/step/pallas_call | solution.py:567
  (6 shorter events, 0.0 us)
Async XLA Ops:
  1.6 7.4 %collective-permute-start.2 = (f32[48,128]{1,0:T(8,128)S(1)}, f32[48,128]{1,0:T(8,128)S(1)}, u32[]{:S(2)}, u32[]{:S(2)}) collective-permute-start(f32[48,128]{1,0:T(8,128)S(1)} %get-tuple-element.15), channel_id=1, source_target_pairs={{0,8},{8,0},{16,24},{24,16},{1,9},{9,1},{17,25},{25,17},{2,10},{10... | collective-permute-start | bytes 73736 | tf_op jit(solution)/shard_map/ppermute | solution.py:509
  4.6 5.1 %collective-permute-start.3 = (f32[48,128]{1,0:T(8,128)S(1)}, f32[48,128]{1,0:T(8,128)S(1)}, u32[]{:S(2)}, u32[]{:S(2)}) collective-permute-start(f32[48,128]{1,0:T(8,128)S(1)} %get-tuple-element.15), channel_id=1, source_target_pairs={{0,16},{8,24},{16,0},{24,8},{1,17},{9,25},{17,1},{25,9},{2,18},{10... | collective-permute-start | bytes 73736 | tf_op jit(solution)/shard_map/ppermute | solution.py:509
  7.2 5.6 %collective-permute-start.4 = (f32[48,128]{1,0:T(8,128)S(1)}, f32[48,128]{1,0:T(8,128)S(1)}, u32[]{:S(2)}, u32[]{:S(2)}) collective-permute-start(f32[48,128]{1,0:T(8,128)S(1)} %get-tuple-element.15), channel_id=1, source_target_pairs={{0,24},{8,16},{16,8},{24,0},{1,25},{9,17},{17,9},{25,1},{2,26},{10... | collective-permute-start | bytes 73736 | tf_op jit(solution)/shard_map/ppermute | solution.py:509
  7.2 11.9 %collective-permute-start.1 = (f32[1,1,5,8,1024]{4,3,2,1,0:T(8,128)}, f32[1,1,5,8,1024]{4,3,2,1,0:T(8,128)S(1)}, u32[]{:S(2)}, u32[]{:S(2)}) collective-permute-start(f32[1,1,5,8,1024]{4,3,2,1,0:T(8,128)} %bitcast.8), channel_id=1, source_target_pairs={{0,4},{2,6},{4,0},{6,2},{1,5},{3,7},{5,1},{7,3},{8,12},{10,14},{12... | collective-permute-start | bytes 491528 | tf_op jit(solution)/shard_map/ppermute | solution.py:531
  9.0 12.0 %collective-permute-start = (f32[1,1,5,8,1024]{4,3,2,1,0:T(8,128)}, f32[1,1,5,8,1024]{4,3,2,1,0:T(8,128)S(1)}, u32[]{:S(2)}, u32[]{:S(2)}) collective-permute-start(f32[1,1,5,8,1024]{4,3,2,1,0:T(8,128)} %bitcast.9), channel_id=1, source_target_pairs={{0,2},{2,0},{4,6},{6,4},{1,3},{3,1},{5,7},{7,5},{8,10},{10,8},{12,... | collective-permute-start | bytes 491528 | tf_op jit(solution)/shard_map/ppermute | solution.py:531
  12.8 4.7 %collective-permute-start.5 = (f32[192,128]{1,0:T(8,128)S(1)}, f32[192,128]{1,0:T(8,128)S(1)}, u32[]{:S(2)}, u32[]{:S(2)}) collective-permute-start(f32[192,128]{1,0:T(8,128)S(1)} %pad_maximum_fusion), channel_id=1, source_target_pairs={{0,1},{1,0},{2,3},{3,2},{4,5},{5,4},{6,7},{7,6},{8,9},{9,8},{10,11... | collective-permute-start | bytes 294920 | tf_op jit(solution)/shard_map/ppermute | solution.py:509
  17.5 0.7 %copy-start.1 = (s32[16,128]{1,0:T(8,128)S(1)}, s32[16,128]{1,0:T(8,128)}, u32[]{:S(2)}) copy-start(s32[16,128]{1,0:T(8,128)} %get-tuple-element.14.meta_ref) | copy-start | bytes 24580
  19.1 1.8 %collective-permute-start.6 = (f32[1,1,5,8,1024]{4,3,2,1,0:T(8,128)S(1)}, f32[1,1,5,8,1024]{4,3,2,1,0:T(8,128)S(1)}, u32[]{:S(2)}, u32[]{:S(2)}) collective-permute-start(f32[1,1,5,8,1024]{4,3,2,1,0:T(8,128)S(1)} %collective-permute-done.1.refs_2_), channel_id=1, source_target_pairs={{0,2},{2,0},{4,6},{6,4},{1,3},{3,1},{5,7},{7,5},{8,10},{10,8},{12,... | collective-permute-start | bytes 491528 | tf_op jit(solution)/shard_map/ppermute | solution.py:531
  19.2 5.9 %collective-permute-start.8 = (f32[88,128]{1,0:T(8,128)S(1)}, f32[88,128]{1,0:T(8,128)S(1)}, u32[]{:S(2)}, u32[]{:S(2)}) collective-permute-start(f32[88,128]{1,0:T(8,128)S(1)} %strips.1.refs_5_), channel_id=1, source_target_pairs={{0,4},{2,6},{4,0},{6,2},{1,5},{3,7},{5,1},{7,3},{8,12},{10,14},{12... | collective-permute-start | bytes 135176 | tf_op jit(solution)/shard_map/ppermute | solution.py:531
  20.8 4.8 %collective-permute-start.7 = (f32[88,128]{1,0:T(8,128)S(1)}, f32[88,128]{1,0:T(8,128)S(1)}, u32[]{:S(2)}, u32[]{:S(2)}) collective-permute-start(f32[88,128]{1,0:T(8,128)S(1)} %strips.1.refs_5_), channel_id=1, source_target_pairs={{0,2},{2,0},{4,6},{6,4},{1,3},{3,1},{5,7},{7,5},{8,10},{10,8},{12,... | collective-permute-start | bytes 135176 | tf_op jit(solution)/shard_map/ppermute | solution.py:531
  21.0 0.9 %copy-start = (f32[1,1,8,5,1024]{4,2,3,1,0:T(8,128)S(1)}, f32[1,1,8,5,1024]{4,2,3,1,0:T(8,128)}, u32[]{:S(2)}) copy-start(f32[1,1,8,5,1024]{4,2,3,1,0:T(8,128)} %param.6) | copy-start | bytes 491524
  21.9 0.7 %copy-start.2 = (s32[1,1,32,4]{2,3,1,0:T(4,128)S(1)}, s32[1,1,32,4]{2,3,1,0:T(4,128)}, u32[]{:S(2)}) copy-start(s32[1,1,32,4]{2,3,1,0:T(4,128)} %param.9) | copy-start | bytes 1540
  22.6 0.7 %copy-start.3 = (s32[1,1,32,1]{2,3,1,0:T(1,128)S(1)}, s32[1,1,32,1]{2,3,1,0:T(1,128)}, u32[]{:S(2)}) copy-start(s32[1,1,32,1]{2,3,1,0:T(1,128)} %param.8) | copy-start | bytes 388
  25.2 1.3 %collective-permute-start.9 = (f32[88,128]{1,0:T(8,128)S(1)}, f32[88,128]{1,0:T(8,128)S(1)}, u32[]{:S(2)}, u32[]{:S(2)}) collective-permute-start(f32[88,128]{1,0:T(8,128)S(1)} %collective-permute-done.8.refs_7_), channel_id=1, source_target_pairs={{0,2},{2,0},{4,6},{6,4},{1,3},{3,1},{5,7},{7,5},{8,10},{10,8},{12,... | collective-permute-start | bytes 135176 | tf_op jit(solution)/shard_map/ppermute | solution.py:531

commit v5 on v4

--- a/solution.py
+++ b/solution.py
@@ -77,177 +77,13 @@
     return jnp.maximum(jnp.abs(vx), jnp.abs(vy)) + sound
 
 
-def place_of(me, other, n):
-    if power_of_two(n):
-        return me ^ other
-    behind = me - other
-    return jnp.where(behind < 0, behind + n, behind)
-
-
-def pack_kernel(tiles, rows, patches, mesh_sizes, patch_ref, box_ref, which_ref, start_ref, pay_ref, meta_ref):
-    n_gx, n_gz = mesh_sizes
-    me = lax.axis_index("gy")
-    top = None
-    for s in range(SUB):
-        wave = top_speed([patch_ref[0, 0, f, :, s * LANE : (s + 1) * LANE] for f in range(FIELDS)])
-        top = wave if top is None else jnp.maximum(top, wave)
-    for f in range(FIELDS):
-        pay_ref[f * tiles : (f + 1) * tiles, :] = box_ref[pl.ds(f * BOX_ROWS + me * tiles, tiles), :]
-    pay_ref[rows - SUB : rows, :] = top
-
-    start = start_ref[0, 0]
-    row = lax.shift_right_logical(start * 2675, 17)
-    offset = BOX * (row & 1) + start - row * STRIDE
-    near = lax.shift_right_logical(row, 1) - me * tiles
-    mine = (near >= 0) & (near < tiles)
-    patch = lax.broadcasted_iota(jnp.int32, start.shape, 1)
-    which = which_ref[0, 0]
-    gz_bits = n_gz.bit_length() - 1
-    place = place_of(lax.axis_index("gx"), lax.shift_right_logical(which, gz_bits), n_gx) + n_gx * place_of(
-        lax.axis_index("gz"), which & (n_gz - 1), n_gz
-    )
-    meta_ref[0:4, 0:patches] = place * rows + jnp.where(mine, near, 0)
-    meta_ref[4:8, 0:patches] = (HALF * (patch & (SUB - 1)) - offset) & (LANE - 1)
-    meta_ref[8:12, 0:patches] = jnp.where(mine, patch & (SUB - 1), -1)
-
-
-def strip_kernel(parts, rows, tiles, patches, meta_ref, pay_ref, out_ref):
-    top = pay_ref[rows - SUB : rows, :]
-    for k in range(1, parts):
-        top = jnp.maximum(top, pay_ref[(k + 1) * rows - SUB : (k + 1) * rows, :])
-    block = lane_of() // HALF
-    lines = 4 * patches // SUB
-    out_ref[FIELDS * lines :, :] = top
-
-    for v in range(lines):
-        side, first = v // (patches // SUB), v % (patches // SUB) * SUB
-        acc = jnp.zeros((SUB, LANE), jnp.float32)
-        for m in range(SUB):
-            p = first + m
-            at, shift, fills = meta_ref[side, p], meta_ref[4 + side, p], meta_ref[8 + side, p]
-            strip = pay_ref[pl.ds(at, FIELDS, stride=tiles), :]
-            strip = jnp.concatenate([strip, jnp.zeros((SUB - FIELDS, LANE), jnp.float32)], axis=0)
-            acc = jnp.where(block == fills, pltpu.roll(strip, shift, 1), acc)
-        out_ref[pl.ds(v, FIELDS, stride=lines), :] = acc[:FIELDS, :]
-
-
-def lanes_at(lanes_ref, g, side, kind):
-    at = ((g * 4 + side) * 3 + kind) * SUB
-    return lanes_ref[at : at + SUB, :]
-
-
-def held_at(lanes_ref, sets):
-    return lanes_ref[sets * 4 * 3 * SUB : (sets * 4 * 3 + 1) * SUB, :]
-
-
-def fill_ghosts(u_ref, lanes_ref, coarse_ref, sets):
-    for f in range(FIELDS):
-        for g in range(sets):
-
-            def ghost(side, at, kept):
-                x = None
-                for o in range(sets):
-                    start = (o * FIELDS + f) * PLANE + at
-                    edge = pl.ds(start, DEEP, stride=SPAN) if side in (WEST, EAST) else pl.ds(start, SUB)
-                    moved = take_lanes(u_ref[edge, :], lanes_at(lanes_ref, g, side, 0))
-                    x = moved if x is None else jnp.where(lanes_at(lanes_ref, g, side, 1) == o, moved, x)
-                if coarse_ref is None:
-                    return x
-                start = ((g * FIELDS + f) * 10 + kept) * SUB
-                return jnp.where(lanes_at(lanes_ref, g, side, 2) != 0, coarse_ref[start : start + SUB, :], x)
-
-            base = (g * FIELDS + f) * PLANE
-            for side, column, to in ((WEST, PX - 1, -1), (EAST, 0, PX)):
-                u_ref[pl.ds(base + spot(0, to), DEEP, stride=SPAN), :] = ghost(side, spot(0, column), side)
-            for side, row, to in ((SOUTH, DEEP - 1, -1), (NORTH, 0, DEEP)):
-                for i in range(BLOCKS):
-                    kept = 2 + (side - SOUTH) * BLOCKS + i
-                    u_ref[pl.ds(base + spot(to, SUB * i), SUB), :] = ghost(side, spot(row, SUB * i), kept)
-
-
-def halves_of(u, axis):
-    vx, vy, pressure, sound = primitive(u)
-    return half_flux(u, (vx, vy)[axis], pressure, sound, axis + 1)
-
-
-def fill_halves(u_ref, aux_ref, sets):
-    def fill(g, rows, axes):
-        u = [u_ref[rows((g * FIELDS + f) * PLANE), :] for f in range(FIELDS)]
-        vx, vy, pressure, sound = primitive(u)
-        for axis in axes:
-            for n, x in enumerate(half_flux(u, (vx, vy)[axis], pressure, sound, axis + 1)):
-                aux_ref[rows((g * AUX + axis * (FIELDS + 1) + n) * PLANE), :] = x
-
-    for g in range(sets):
-
-        def cells(r, carry):
-            for half in range(2):
-                for i in range(BLOCKS):
-                    at = spot(2 * r + half, SUB * i)
-                    fill(g, lambda b, at=at: pl.ds(pl.multiple_of(b + at, SUB), SUB), (0, 1))
-            return carry
-
-        lax.fori_loop(0, DEEP // 2, cells, 0)
-        for r in (-1, DEEP):
-            for i in range(BLOCKS):
-                fill(g, lambda b, at=spot(r, SUB * i): pl.ds(b + at, SUB), (1,))
-        for c in (-1, PX):
-            fill(g, lambda b, at=spot(0, c): pl.ds(b + at, DEEP, stride=SPAN), (0,))
-
-
-def load_cells(u_ref, aux_ref, g, axis, rows):
-    u = [u_ref[rows((g * FIELDS + f) * PLANE), :] for f in range(FIELDS)]
-    start = g * AUX + axis * (FIELDS + 1)
-    return u, [aux_ref[rows((start + n) * PLANE), :] for n in range(FIELDS + 1)]
-
-
-def at_row(at):
-    return lambda b: pl.ds(b + at, SUB)
-
-
-def fill_x_faces(u_ref, aux_ref, dx_ref, g, base):
-    def across(r, carry):
-        for half in range(2):
-            row = 2 * r + half
-            for i in range(BLOCKS + 1):
-                at = pl.multiple_of(spot(row, SUB * i), SUB)
-                low = load_cells(u_ref, aux_ref, g, 0, at_row(at - 1))
-                faces = face_flux(*low, *load_cells(u_ref, aux_ref, g, 0, at_row(at)))
-                for f in range(FIELDS):
-                    to = pl.multiple_of(base + (f * DEEP + row) * FACES + SUB * i, SUB)
-                    dx_ref[pl.ds(to, SUB), :] = faces[f]
-        return carry
-
-    lax.fori_loop(0, DEEP // 2, across, 0)
-
-
-def x_change(dx_ref, base, f, row, i):
-    west = pl.multiple_of(base + (f * DEEP + row) * FACES + SUB * i, SUB)
-    return dx_ref[pl.ds(west, SUB), :] - dx_ref[pl.ds(west + 1, SUB), :]
-
-
-def prepare_kernel(group, count, patches, slots, around_ref, owner_ref, *refs):
-    raw_refs = refs[:group]
-    u_ref, edge_ref, dx_ref, dy_ref, lanes_ref, aux_ref, table, slot_ref = refs[group:]
+def make_lanes(group, count, patches, slots, around_ref, owner_ref, lanes_ref, table, slot_ref):
     me = lax.axis_index("gy")
     capacity = slots // group
     sets = patches // PX
     lane = lane_of()
     block, in_block = lane // PX, lane & (PX - 1)
     turn = me * count
-
-    for f in range(FIELDS):
-        for g in range(sets):
-            for h in range(2):
-                tiles = []
-                for q in range(BLOCKS):
-                    at = (q * 2 + h) * LANE
-                    for k in range(PX // count):
-                        tiles.append(raw_refs[g * (PX // count) + k][0, 0, f, :, at : at + LANE])
-                cells = jnp.concatenate(tiles, axis=0).T
-                for i in range(BLOCKS):
-                    to = (g * FIELDS + f) * PLANE + spot(h * BLOCKS + i, 0)
-                    u_ref[to : to + PX, :] = cells[i * PX : (i + 1) * PX, :]
 
     for i in range(slots):
         slot_ref[i] = -1
@@ -287,6 +123,178 @@
                 at = ((g * 4 + side) * 3 + kind) * SUB
                 lanes_ref[at : at + SUB, :] = x
 
+
+def place_of(me, other, n):
+    if power_of_two(n):
+        return me ^ other
+    behind = me - other
+    return jnp.where(behind < 0, behind + n, behind)
+
+
+def pack_kernel(tiles, rows, group, count, patches, slots, mesh_sizes, *refs):
+    owner_ref, around_ref, which_ref, start_ref, patch_ref, box_ref = refs[:6]
+    pay_ref, raw_ref, meta_ref, lanes_ref, table, slot_ref = refs[6:]
+    n_gx, n_gz = mesh_sizes
+    raw_ref[...] = patch_ref[...]
+    me = lax.axis_index("gy")
+    top = None
+    for s in range(SUB):
+        wave = top_speed([patch_ref[0, 0, f, :, s * LANE : (s + 1) * LANE] for f in range(FIELDS)])
+        top = wave if top is None else jnp.maximum(top, wave)
+    for f in range(FIELDS):
+        pay_ref[f * tiles : (f + 1) * tiles, :] = box_ref[pl.ds(f * BOX_ROWS + me * tiles, tiles), :]
+    pay_ref[rows - SUB : rows, :] = top
+
+    start = start_ref[0, 0]
+    row = lax.shift_right_logical(start * 2675, 17)
+    offset = BOX * (row & 1) + start - row * STRIDE
+    near = lax.shift_right_logical(row, 1) - me * tiles
+    mine = (near >= 0) & (near < tiles)
+    patch = lax.broadcasted_iota(jnp.int32, start.shape, 1)
+    which = which_ref[0, 0]
+    gz_bits = n_gz.bit_length() - 1
+    place = place_of(lax.axis_index("gx"), lax.shift_right_logical(which, gz_bits), n_gx) + n_gx * place_of(
+        lax.axis_index("gz"), which & (n_gz - 1), n_gz
+    )
+    meta_ref[0:4, 0:patches] = place * rows + jnp.where(mine, near, 0)
+    meta_ref[4:8, 0:patches] = (HALF * (patch & (SUB - 1)) - offset) & (LANE - 1)
+    meta_ref[8:12, 0:patches] = jnp.where(mine, patch & (SUB - 1), -1)
+    make_lanes(group, count, patches, slots, around_ref, owner_ref, lanes_ref, table, slot_ref)
+
+
+def strip_kernel(parts, rows, tiles, patches, meta_ref, pay_ref, out_ref):
+    top = pay_ref[rows - SUB : rows, :]
+    for k in range(1, parts):
+        top = jnp.maximum(top, pay_ref[(k + 1) * rows - SUB : (k + 1) * rows, :])
+    block = lane_of() // HALF
+    lines = 4 * patches // SUB
+    out_ref[FIELDS * lines :, :] = top
+
+    for v in range(lines):
+        side, first = v // (patches // SUB), v % (patches // SUB) * SUB
+        acc = jnp.zeros((SUB, LANE), jnp.float32)
+        for m in range(SUB):
+            p = first + m
+            at, shift, fills = meta_ref[side, p], meta_ref[4 + side, p], meta_ref[8 + side, p]
+            strip = pay_ref[pl.ds(at, FIELDS, stride=tiles), :]
+            strip = jnp.concatenate([strip, jnp.zeros((SUB - FIELDS, LANE), jnp.float32)], axis=0)
+            acc = jnp.where(block == fills, pltpu.roll(strip, shift, 1), acc)
+        out_ref[pl.ds(v, FIELDS, stride=lines), :] = acc[:FIELDS, :]
+
+
+def lanes_at(lanes_ref, g, side, kind):
+    at = ((g * 4 + side) * 3 + kind) * SUB
+    return lanes_ref[at : at + SUB, :]
+
+
+def held_at(lanes_ref, sets):
+    return lanes_ref[sets * 4 * 3 * SUB : (sets * 4 * 3 + 1) * SUB, :]
+
+
+def fill_ghosts(u_ref, lanes_ref, coarse_ref, sets):
+    for f in range(FIELDS):
+        for g in range(sets):
+
+            def ghost(side, at, kept):
+                x = None
+                for o in range(sets):
+                    start = (o * FIELDS + f) * PLANE + at
+                    edge = pl.ds(start, DEEP, stride=SPAN) if side in (WEST, EAST) else pl.ds(start, SUB)
+                    moved = take_lanes(u_ref[edge, :], lanes_at(lanes_ref, g, side, 0))
+                    x = moved if x is None else jnp.where(lanes_at(lanes_ref, g, side, 1) == o, moved, x)
+                if coarse_ref is None:
+                    return x
+                start = ((g * FIELDS + f) * 10 + kept) * SUB
+                return jnp.where(lanes_at(lanes_ref, g, side, 2) != 0, coarse_ref[start : start + SUB, :], x)
+
+            base = (g * FIELDS + f) * PLANE
+            for side, column, to in ((WEST, PX - 1, -1), (EAST, 0, PX)):
+                u_ref[pl.ds(base + spot(0, to), DEEP, stride=SPAN), :] = ghost(side, spot(0, column), side)
+            for side, row, to in ((SOUTH, DEEP - 1, -1), (NORTH, 0, DEEP)):
+                for i in range(BLOCKS):
+                    kept = 2 + (side - SOUTH) * BLOCKS + i
+                    u_ref[pl.ds(base + spot(to, SUB * i), SUB), :] = ghost(side, spot(row, SUB * i), kept)
+
+
+def halves_of(u, axis):
+    vx, vy, pressure, sound = primitive(u)
+    return half_flux(u, (vx, vy)[axis], pressure, sound, axis + 1)
+
+
+def fill_halves(u_ref, aux_ref, sets):
+    def fill(g, rows, axes):
+        u = [u_ref[rows((g * FIELDS + f) * PLANE), :] for f in range(FIELDS)]
+        vx, vy, pressure, sound = primitive(u)
+        for axis in axes:
+            for n, x in enumerate(half_flux(u, (vx, vy)[axis], pressure, sound, axis + 1)):
+                aux_ref[rows((g * AUX + axis * (FIELDS + 1) + n) * PLANE), :] = x
+
+    for g in range(sets):
+
+        def cells(r, carry):
+            for half in range(2):
+                for i in range(BLOCKS):
+                    at = spot(2 * r + half, SUB * i)
+                    fill(g, lambda b, at=at: pl.ds(pl.multiple_of(b + at, SUB), SUB), (0, 1))
+            return carry
+
+        lax.fori_loop(0, DEEP // 2, cells, 0)
+        for r in (-1, DEEP):
+            for i in range(BLOCKS):
+                fill(g, lambda b, at=spot(r, SUB * i): pl.ds(b + at, SUB), (1,))
+        for c in (-1, PX):
+            fill(g, lambda b, at=spot(0, c): pl.ds(b + at, DEEP, stride=SPAN), (0,))
+
+
+def load_cells(u_ref, aux_ref, g, axis, rows):
+    u = [u_ref[rows((g * FIELDS + f) * PLANE), :] for f in range(FIELDS)]
+    start = g * AUX + axis * (FIELDS + 1)
+    return u, [aux_ref[rows((start + n) * PLANE), :] for n in range(FIELDS + 1)]
+
+
+def at_row(at):
+    return lambda b: pl.ds(b + at, SUB)
+
+
+def fill_x_faces(u_ref, aux_ref, dx_ref, g, base):
+    def across(r, carry):
+        for half in range(2):
+            row = 2 * r + half
+            for i in range(BLOCKS + 1):
+                at = pl.multiple_of(spot(row, SUB * i), SUB)
+                low = load_cells(u_ref, aux_ref, g, 0, at_row(at - 1))
+                faces = face_flux(*low, *load_cells(u_ref, aux_ref, g, 0, at_row(at)))
+                for f in range(FIELDS):
+                    to = pl.multiple_of(base + (f * DEEP + row) * FACES + SUB * i, SUB)
+                    dx_ref[pl.ds(to, SUB), :] = faces[f]
+        return carry
+
+    lax.fori_loop(0, DEEP // 2, across, 0)
+
+
+def x_change(dx_ref, base, f, row, i):
+    west = pl.multiple_of(base + (f * DEEP + row) * FACES + SUB * i, SUB)
+    return dx_ref[pl.ds(west, SUB), :] - dx_ref[pl.ds(west + 1, SUB), :]
+
+
+def prepare_kernel(group, count, patches, lanes_ref, *refs):
+    raw_refs = refs[:group]
+    u_ref, edge_ref, dx_ref, dy_ref, aux_ref = refs[group:]
+    sets = patches // PX
+
+    for f in range(FIELDS):
+        for g in range(sets):
+            for h in range(2):
+                tiles = []
+                for q in range(BLOCKS):
+                    at = (q * 2 + h) * LANE
+                    for k in range(PX // count):
+                        tiles.append(raw_refs[g * (PX // count) + k][0, 0, f, :, at : at + LANE])
+                cells = jnp.concatenate(tiles, axis=0).T
+                for i in range(BLOCKS):
+                    to = (g * FIELDS + f) * PLANE + spot(h * BLOCKS + i, 0)
+                    u_ref[to : to + PX, :] = cells[i * PX : (i + 1) * PX, :]
+
     fill_ghosts(u_ref, lanes_ref, None, sets)
     fill_halves(u_ref, aux_ref, sets)
     for g in range(sets):
@@ -492,14 +500,27 @@
     def sides_first(x):
         return jnp.swapaxes(x, 2, 3)
 
-    raw = sides_first(patch_state)
-    payload, meta = pl.pallas_call(
-        functools.partial(pack_kernel, tiles, rows, patches, (n_gx, n_gz)),
-        out_shape=(pltpu.VMEM((rows, LANE), f32), jax.ShapeDtypeStruct((16, max(LANE, patches)), jnp.int32)),
-        in_specs=[vmem] * 4,
-        out_specs=(vmem,) * 2,
+    sets = patches // PX
+    payload, raw, meta, lanes = pl.pallas_call(
+        functools.partial(pack_kernel, tiles, rows, group, count, patches, slots, (n_gx, n_gz)),
+        out_shape=(
+            pltpu.VMEM((rows, LANE), f32),
+            pltpu.VMEM((1, 1, FIELDS, count, SUB * LANE), f32),
+            pltpu.VMEM((16, max(LANE, patches)), jnp.int32),
+            pltpu.VMEM(((sets * 4 * 3 + 1) * SUB, LANE), jnp.int32),
+        ),
+        in_specs=[smem] + [vmem] * 5,
+        out_specs=(vmem,) * 4,
+        scratch_shapes=[pltpu.VMEM((SUB, LANE), jnp.int32), pltpu.SMEM((slots + 1,), jnp.int32)],
         name="pack",
-    )(raw, coarse_boxes.reshape(FIELDS * BOX_ROWS, LANE), sides_first(coarse_box), sides_first(coarse_start))
+    )(
+        sides_first(new_owner),
+        sides_first(neighbors),
+        sides_first(coarse_box),
+        sides_first(coarse_start),
+        sides_first(patch_state),
+        coarse_boxes.reshape(FIELDS * BOX_ROWS, LANE),
+    )
 
     def gathered(x, axis, n):
         if power_of_two(n):
@@ -534,30 +555,24 @@
 
     raws = to_group(raw, strip)
 
-    sets = patches // PX
     made_rows = [
         sets * FIELDS * PLANE,
         sets * 10 * (FIELDS + 1) * SUB,
         sets * FIELDS * DEEP * FACES,
         sets * FIELDS * (DEEP + 1) * PX,
     ]
-    lane_rows = (sets * 4 * 3 + 1) * SUB
     made = pl.pallas_call(
-        functools.partial(prepare_kernel, group, count, patches, slots),
-        out_shape=[pltpu.VMEM((n, LANE), f32) for n in made_rows] + [pltpu.VMEM((lane_rows, LANE), jnp.int32)],
-        in_specs=[vmem, smem] + [vmem] * group,
-        out_specs=[vmem] * 5,
-        scratch_shapes=[
-            pltpu.VMEM((sets * AUX * PLANE, LANE), f32),
-            pltpu.VMEM((SUB, LANE), jnp.int32),
-            pltpu.SMEM((slots + 1,), jnp.int32),
-        ],
-        compiler_params=limit(*made_rows, sets * AUX * PLANE, lane_rows, patches * FIELDS * SUB),
+        functools.partial(prepare_kernel, group, count, patches),
+        out_shape=[pltpu.VMEM((n, LANE), f32) for n in made_rows],
+        in_specs=[vmem] * (1 + group),
+        out_specs=[vmem] * 4,
+        scratch_shapes=[pltpu.VMEM((sets * AUX * PLANE, LANE), f32)],
+        compiler_params=limit(*made_rows, sets * AUX * PLANE, lanes.shape[0], patches * FIELDS * SUB),
         cost_estimate=pl.CostEstimate(flops=patches * 1024 * 300, bytes_accessed=patches * 40000, transcendentals=0),
         name="prepare",
-    )(sides_first(neighbors), sides_first(new_owner), *raws)
-
-    strips = to_group(strip, made[4])
+    )(lanes, *raws)
+
+    strips = to_group(strip, made[0])
     scratch_rows = [sets * FIELDS * PLANE, sets * AUX * PLANE, sets * FIELDS * DEEP * FACES] + [
         FIELDS * lines,
         4 * patches // LANE * FIELDS * PX,
@@ -570,9 +585,9 @@
         in_specs=[vmem] * (5 + group),
         out_specs=vmem,
         scratch_shapes=[pltpu.VMEM((n, LANE), f32) for n in scratch_rows],
-        compiler_params=limit(*scratch_rows, *made_rows, lane_rows, group * strip_rows, FIELDS * slots * SUB),
+        compiler_params=limit(*scratch_rows, *made_rows, lanes.shape[0], group * strip_rows, FIELDS * slots * SUB),
         name="step",
-    )(*made, *strips)
+    )(*made, lanes, *strips)
     return sides_first(out)
 
 

time: 29.7 us -> 26.7 us (0.90)
  local copies, waits for them, and re-layouts: 2.96 us -> 0.02 us
  waiting for transfers between devices: 7.87 us -> 9.4 us
  Pallas kernels: 7.38 us -> 6.29 us
  starting transfers between devices: 11.1 us -> 10.8 us
    unnamed x12 -> x4, local copies, waits for them, and re-layouts: 2.95 us -> 0.01 us
    ppermute x6, waiting for transfers between devices: 0.89 us -> 2.41 us  [to_group(): blocks[k ^ mask] = lax.ppermute(block, 'gy', perm)]
    pallas_call x2, Pallas kernels: 3.49 us -> 2.39 us  [the longest x1 1.23 us: per_device(): pl.pallas_call(functools.partial(pack_kernel, tiles, rows, group, count,...]
    ppermute x6, starting transfers between devices: 3.97 us -> 3.57 us  [to_group(): blocks[k ^ mask] = lax.ppermute(block, 'gy', perm)]
  transfers between devices with their start and end apart: 10 -> 10, of which waited for: 4 -> 5; matrix products, arithmetic and copies ran while one was open for 0% -> 0% of each run, Pallas kernels for 9% -> 8%
where the time goes in v5:
time: 26.7 us; the launch traced here: 26.6 us
  starting transfers between devices  10.8 us (40%)
  waiting for transfers between devices  9.4 us (35%)
  Pallas kernels  6.29 us (24%)
    ppermute x4, starting transfers between devices, gathered(): lax.ppermute(x, axis, perm)  7.24 us
    ppermute x4, waiting for transfers between devices, gathered(): lax.ppermute(x, axis, perm)  6.98 us
    ppermute x6, starting transfers between devices, to_group(): blocks[k ^ mask] = lax.ppermute(block, 'gy', perm)  3.57 us
    pallas_call x1, Pallas kernels, per_device(): pl.pallas_call(functools.partial(step_kernel, group, count, patches, slot...  3 us
    ppermute x6, waiting for transfers between devices, to_group(): blocks[k ^ mask] = lax.ppermute(block, 'gy', perm)  2.41 us
    pallas_call x1, Pallas kernels, per_device(): pl.pallas_call(functools.partial(pack_kernel, tiles, rows, group, count,...  1.23 us
    pallas_call x1, Pallas kernels, per_device(): pl.pallas_call(functools.partial(prepare_kernel, group, count, patches),...  1.16 us
    pallas_call x1, Pallas kernels, per_device(): pl.pallas_call(functools.partial(strip_kernel, parts, rows, tiles, patche...  0.89 us
  transfers between devices with their start and end apart: 10, of which 5 were waited for; matrix products, arithmetic and copies ran while one was open for 0% of the time, Pallas kernels for 8%

profile of v5, /device:TPU:0, one launch (start us, length us, event | category | flops | bytes accessed | tf_op | source)
XLA Modules:
  0.0 26.6 jit_solution(17579724403879614230)
XLA Ops:
  0.0 1.2 %pack.1 = (f32[48,128]{1,0:T(8,128)S(1)}, f32[1,1,5,8,1024]{4,3,2,1,0:T(8,128)S(1)}, s32[16,128]{1,0:T(8,128)S(1)}, s32[104,128]{1,0:T(8,128)S(1)}) custom-call(s32[1,1,1,32]{3,2,1,0:T(1,128)} %bitcast.12, s32[1,1,4,32]{3,2,1,0:T(4,128)} %bitcast.9, s32[1,1,4,32]{3,2,1,0:T(4,128)} %bitcast.10, s32[1,1,4,32]{3,2,1,0:T(4,128)} %bitcast.11, ...), custom_call_target="tpu_custom_call" | custom-call | tf_op jit(solution)/shard_map/pack/pallas_call | solution.py:504
  1.2 3.1 %collective-permute-start.2 = (f32[48,128]{1,0:T(8,128)S(1)}, f32[48,128]{1,0:T(8,128)S(1)}, u32[]{:S(2)}, u32[]{:S(2)}) collective-permute-start(f32[48,128]{1,0:T(8,128)S(1)} %get-tuple-element.18), channel_id=1, source_target_pairs={{0,8},{8,0},{16,24},{24,16},{1,9},{9,1},{17,25},{25,17},{2,10},{10... | collective-permute-start | bytes 73736 | tf_op jit(solution)/shard_map/ppermute | solution.py:530
  4.3 2.6 %collective-permute-start.3 = (f32[48,128]{1,0:T(8,128)S(1)}, f32[48,128]{1,0:T(8,128)S(1)}, u32[]{:S(2)}, u32[]{:S(2)}) collective-permute-start(f32[48,128]{1,0:T(8,128)S(1)} %get-tuple-element.18), channel_id=1, source_target_pairs={{0,16},{8,24},{16,0},{24,8},{1,17},{9,25},{17,1},{25,9},{2,18},{10... | collective-permute-start | bytes 73736 | tf_op jit(solution)/shard_map/ppermute | solution.py:530
  6.9 0.0 collective-permute-start.4
  6.9 1.7 %collective-permute-start.1 = (f32[1,1,5,8,1024]{4,3,2,1,0:T(8,128)S(1)}, f32[1,1,5,8,1024]{4,3,2,1,0:T(8,128)S(1)}, u32[]{:S(2)}, u32[]{:S(2)}) collective-permute-start(f32[1,1,5,8,1024]{4,3,2,1,0:T(8,128)S(1)} %get-tuple-element.16.refs_0_), channel_id=1, source_target_pairs={{0,4},{2,6},{4,0},{6,2},{1,5},{3,7},{5,1},{7,3},{8,12},{10,14},{12... | collective-permute-start | bytes 491528 | tf_op jit(solution)/shard_map/ppermute | solution.py:552
  8.7 0.0 collective-permute-start
  8.7 0.0 collective-permute-done.2
  8.7 0.7 %collective-permute-done.3 = f32[48,128]{1,0:T(8,128)S(1)} collective-permute-done((f32[48,128]{1,0:T(8,128)S(1)}, f32[48,128]{1,0:T(8,128)S(1)}, u32[]{:S(2)}, u32[]{:S(2)}) %collective-permute-start.3) | collective-permute-done | bytes 24608 | tf_op jit(solution)/shard_map/ppermute | solution.py:530
  9.4 3.1 %collective-permute-done.4 = f32[48,128]{1,0:T(8,128)S(1)} collective-permute-done((f32[48,128]{1,0:T(8,128)S(1)}, f32[48,128]{1,0:T(8,128)S(1)}, u32[]{:S(2)}, u32[]{:S(2)}) %collective-permute-start.4) | collective-permute-done | bytes 24608 | tf_op jit(solution)/shard_map/ppermute | solution.py:530
  12.6 1.6 %collective-permute-start.5 = (f32[192,128]{1,0:T(8,128)S(1)}, f32[192,128]{1,0:T(8,128)S(1)}, u32[]{:S(2)}, u32[]{:S(2)}) collective-permute-start(f32[192,128]{1,0:T(8,128)S(1)} %pad_maximum_fusion), channel_id=1, source_target_pairs={{0,1},{1,0},{2,3},{3,2},{4,5},{5,4},{6,7},{7,6},{8,9},{9,8},{10,11... | collective-permute-start | bytes 294920 | tf_op jit(solution)/shard_map/ppermute | solution.py:530
  14.1 3.1 %collective-permute-done.5 = f32[192,128]{1,0:T(8,128)S(1)} collective-permute-done((f32[192,128]{1,0:T(8,128)S(1)}, f32[192,128]{1,0:T(8,128)S(1)}, u32[]{:S(2)}, u32[]{:S(2)}) %collective-permute-start.5) | collective-permute-done | bytes 98336 | tf_op jit(solution)/shard_map/ppermute | solution.py:530
  17.2 0.9 %strips.1.refs_5_ = f32[88,128]{1,0:T(8,128)S(1)} custom-call(s32[16,128]{1,0:T(8,128)S(1)} %get-tuple-element.17.meta_ref, f32[384,128]{1,0:T(8,128)S(1)} %constant_dynamic-update-slice_fusion.pay_ref), custom_call_target="tpu_custom_call" | custom-call | tf_op jit(solution)/shard_map/strips/pallas_call | solution.py:534
  18.1 0.0 collective-permute-done.1.refs_2_
  18.2 0.1 collective-permute-start.6
  18.2 1.6 %collective-permute-start.8 = (f32[88,128]{1,0:T(8,128)S(1)}, f32[88,128]{1,0:T(8,128)S(1)}, u32[]{:S(2)}, u32[]{:S(2)}) collective-permute-start(f32[88,128]{1,0:T(8,128)S(1)} %strips.1.refs_5_), channel_id=1, source_target_pairs={{0,4},{2,6},{4,0},{6,2},{1,5},{3,7},{5,1},{7,3},{8,12},{10,14},{12... | collective-permute-start | bytes 135176 | tf_op jit(solution)/shard_map/ppermute | solution.py:552
  19.8 0.2 collective-permute-start.7
  20.0 0.0 collective-permute-done.refs_1_
  20.0 0.0 collective-permute-done.6.refs_3_
  20.0 1.2 %prepare.1 = (f32[2400,128]{1,0:T(8,128)S(1)}, f32[480,128]{1,0:T(8,128)S(1)}, f32[1600,128]{1,0:T(8,128)S(1)}, f32[1440,128]{1,0:T(8,128)S(1)}) custom-call(s32[104,128]{1,0:T(8,128)S(1)} %get-tuple-element.15.lanes_ref.refs_4_, f32[1,1,5,8,1024]{4,3,2,1,0:T(8,128)S(1)} %get-tuple-element.16.refs_0_, ...), custom_call_target="tpu_custom_call" | custom-call | flops 9830400 | bytes 1280000 | tf_op jit(solution)/shard_map/prepare/pallas_call | solution.py:564
  21.2 1.2 %collective-permute-done.8.refs_7_ = f32[88,128]{1,0:T(8,128)S(1)} collective-permute-done((f32[88,128]{1,0:T(8,128)S(1)}, f32[88,128]{1,0:T(8,128)S(1)}, u32[]{:S(2)}, u32[]{:S(2)}) %collective-permute-start.8) | collective-permute-done | bytes 45088 | tf_op jit(solution)/shard_map/ppermute | solution.py:552
  22.3 0.0 collective-permute-start.9
  22.4 0.0 collective-permute-done.7.refs_6_
  22.4 1.2 %collective-permute-done.9.refs_8_ = f32[88,128]{1,0:T(8,128)S(1)} collective-permute-done((f32[88,128]{1,0:T(8,128)S(1)}, f32[88,128]{1,0:T(8,128)S(1)}, u32[]{:S(2)}, u32[]{:S(2)}) %collective-permute-start.9) | collective-permute-done | bytes 45088 | tf_op jit(solution)/shard_map/ppermute | solution.py:552
  23.6 3.0 %step.1 = f32[1,1,5,16,1024]{4,3,2,1,0:T(8,128)} custom-call(f32[2400,128]{1,0:T(8,128)S(1)} %get-tuple-element.20.refs_0_, f32[480,128]{1,0:T(8,128)S(1)} %get-tuple-element.21.refs_1_, f32[1600,128]{1,0:T(8,128)S(1)} %get-tuple-element.22.refs_2_, f32[1440,128]{1,0:T(8,128)S(1)} %get-tuple-element.23.refs_3_, ...), custom_call_target="tpu_custom_call" | custom-call | tf_op jit(solution)/shard_map/step/pallas_call | solution.py:582
  (6 shorter events, 0.0 us)
Async XLA Ops:
  1.2 7.4 %collective-permute-start.2 = (f32[48,128]{1,0:T(8,128)S(1)}, f32[48,128]{1,0:T(8,128)S(1)}, u32[]{:S(2)}, u32[]{:S(2)}) collective-permute-start(f32[48,128]{1,0:T(8,128)S(1)} %get-tuple-element.18), channel_id=1, source_target_pairs={{0,8},{8,0},{16,24},{24,16},{1,9},{9,1},{17,25},{25,17},{2,10},{10... | collective-permute-start | bytes 73736 | tf_op jit(solution)/shard_map/ppermute | solution.py:530
  4.3 5.1 %collective-permute-start.3 = (f32[48,128]{1,0:T(8,128)S(1)}, f32[48,128]{1,0:T(8,128)S(1)}, u32[]{:S(2)}, u32[]{:S(2)}) collective-permute-start(f32[48,128]{1,0:T(8,128)S(1)} %get-tuple-element.18), channel_id=1, source_target_pairs={{0,16},{8,24},{16,0},{24,8},{1,17},{9,25},{17,1},{25,9},{2,18},{10... | collective-permute-start | bytes 73736 | tf_op jit(solution)/shard_map/ppermute | solution.py:530
  6.9 5.6 %collective-permute-start.4 = (f32[48,128]{1,0:T(8,128)S(1)}, f32[48,128]{1,0:T(8,128)S(1)}, u32[]{:S(2)}, u32[]{:S(2)}) collective-permute-start(f32[48,128]{1,0:T(8,128)S(1)} %get-tuple-element.18), channel_id=1, source_target_pairs={{0,24},{8,16},{16,8},{24,0},{1,25},{9,17},{17,9},{25,1},{2,26},{10... | collective-permute-start | bytes 73736 | tf_op jit(solution)/shard_map/ppermute | solution.py:530
  6.9 11.2 %collective-permute-start.1 = (f32[1,1,5,8,1024]{4,3,2,1,0:T(8,128)S(1)}, f32[1,1,5,8,1024]{4,3,2,1,0:T(8,128)S(1)}, u32[]{:S(2)}, u32[]{:S(2)}) collective-permute-start(f32[1,1,5,8,1024]{4,3,2,1,0:T(8,128)S(1)} %get-tuple-element.16.refs_0_), channel_id=1, source_target_pairs={{0,4},{2,6},{4,0},{6,2},{1,5},{3,7},{5,1},{7,3},{8,12},{10,14},{12... | collective-permute-start | bytes 491528 | tf_op jit(solution)/shard_map/ppermute | solution.py:552
  8.7 11.3 %collective-permute-start = (f32[1,1,5,8,1024]{4,3,2,1,0:T(8,128)S(1)}, f32[1,1,5,8,1024]{4,3,2,1,0:T(8,128)S(1)}, u32[]{:S(2)}, u32[]{:S(2)}) collective-permute-start(f32[1,1,5,8,1024]{4,3,2,1,0:T(8,128)S(1)} %get-tuple-element.16.refs_0_), channel_id=1, source_target_pairs={{0,2},{2,0},{4,6},{6,4},{1,3},{3,1},{5,7},{7,5},{8,10},{10,8},{12,... | collective-permute-start | bytes 491528 | tf_op jit(solution)/shard_map/ppermute | solution.py:552
  12.6 4.7 %collective-permute-start.5 = (f32[192,128]{1,0:T(8,128)S(1)}, f32[192,128]{1,0:T(8,128)S(1)}, u32[]{:S(2)}, u32[]{:S(2)}) collective-permute-start(f32[192,128]{1,0:T(8,128)S(1)} %pad_maximum_fusion), channel_id=1, source_target_pairs={{0,1},{1,0},{2,3},{3,2},{4,5},{5,4},{6,7},{7,6},{8,9},{9,8},{10,11... | collective-permute-start | bytes 294920 | tf_op jit(solution)/shard_map/ppermute | solution.py:530
  18.2 1.8 %collective-permute-start.6 = (f32[1,1,5,8,1024]{4,3,2,1,0:T(8,128)S(1)}, f32[1,1,5,8,1024]{4,3,2,1,0:T(8,128)S(1)}, u32[]{:S(2)}, u32[]{:S(2)}) collective-permute-start(f32[1,1,5,8,1024]{4,3,2,1,0:T(8,128)S(1)} %collective-permute-done.1.refs_2_), channel_id=1, source_target_pairs={{0,2},{2,0},{4,6},{6,4},{1,3},{3,1},{5,7},{7,5},{8,10},{10,8},{12,... | collective-permute-start | bytes 491528 | tf_op jit(solution)/shard_map/ppermute | solution.py:552
  18.2 4.1 %collective-permute-start.8 = (f32[88,128]{1,0:T(8,128)S(1)}, f32[88,128]{1,0:T(8,128)S(1)}, u32[]{:S(2)}, u32[]{:S(2)}) collective-permute-start(f32[88,128]{1,0:T(8,128)S(1)} %strips.1.refs_5_), channel_id=1, source_target_pairs={{0,4},{2,6},{4,0},{6,2},{1,5},{3,7},{5,1},{7,3},{8,12},{10,14},{12... | collective-permute-start | bytes 135176 | tf_op jit(solution)/shard_map/ppermute | solution.py:552
  19.8 2.5 %collective-permute-start.7 = (f32[88,128]{1,0:T(8,128)S(1)}, f32[88,128]{1,0:T(8,128)S(1)}, u32[]{:S(2)}, u32[]{:S(2)}) collective-permute-start(f32[88,128]{1,0:T(8,128)S(1)} %strips.1.refs_5_), channel_id=1, source_target_pairs={{0,2},{2,0},{4,6},{6,4},{1,3},{3,1},{5,7},{7,5},{8,10},{10,8},{12,... | collective-permute-start | bytes 135176 | tf_op jit(solution)/shard_map/ppermute | solution.py:552
  22.3 1.2 %collective-permute-start.9 = (f32[88,128]{1,0:T(8,128)S(1)}, f32[88,128]{1,0:T(8,128)S(1)}, u32[]{:S(2)}, u32[]{:S(2)}) collective-permute-start(f32[88,128]{1,0:T(8,128)S(1)} %collective-permute-done.8.refs_7_), channel_id=1, source_target_pairs={{0,2},{2,0},{4,6},{6,4},{1,3},{3,1},{5,7},{7,5},{8,10},{10,8},{12,... | collective-permute-start | bytes 135176 | tf_op jit(solution)/shard_map/ppermute | solution.py:552

commit v6 on v5

--- a/solution.py
+++ b/solution.py
@@ -133,8 +133,9 @@
 
 def pack_kernel(tiles, rows, group, count, patches, slots, mesh_sizes, *refs):
     owner_ref, around_ref, which_ref, start_ref, patch_ref, box_ref = refs[:6]
-    pay_ref, raw_ref, meta_ref, lanes_ref, table, slot_ref = refs[6:]
     n_gx, n_gz = mesh_sizes
+    pay_ref, raw_ref, lanes_ref = refs[6:9]
+    cut_refs, (table, slot_ref) = refs[9 : 9 + n_gz], refs[9 + n_gz :]
     raw_ref[...] = patch_ref[...]
     me = lax.axis_index("gy")
     top = None
@@ -145,41 +146,37 @@
         pay_ref[f * tiles : (f + 1) * tiles, :] = box_ref[pl.ds(f * BOX_ROWS + me * tiles, tiles), :]
     pay_ref[rows - SUB : rows, :] = top
 
-    start = start_ref[0, 0]
+    start, which = start_ref[0, 0], which_ref[0, 0]
     row = lax.shift_right_logical(start * 2675, 17)
     offset = BOX * (row & 1) + start - row * STRIDE
     near = lax.shift_right_logical(row, 1) - me * tiles
-    mine = (near >= 0) & (near < tiles)
+    place = place_of(lax.axis_index("gx"), lax.shift_right_logical(which, n_gz.bit_length() - 1), n_gx)
+    apart = (which & (n_gz - 1)) ^ lax.axis_index("gz")
     patch = lax.broadcasted_iota(jnp.int32, start.shape, 1)
-    which = which_ref[0, 0]
-    gz_bits = n_gz.bit_length() - 1
-    place = place_of(lax.axis_index("gx"), lax.shift_right_logical(which, gz_bits), n_gx) + n_gx * place_of(
-        lax.axis_index("gz"), which & (n_gz - 1), n_gz
-    )
-    meta_ref[0:4, 0:patches] = place * rows + jnp.where(mine, near, 0)
-    meta_ref[4:8, 0:patches] = (HALF * (patch & (SUB - 1)) - offset) & (LANE - 1)
-    meta_ref[8:12, 0:patches] = jnp.where(mine, patch & (SUB - 1), -1)
+    for k in range(n_gz):
+        mine = (near >= 0) & (near < tiles) & (apart == k)
+        cut_refs[k][0:4, 0:patches] = jnp.where(mine, place * rows + near, n_gx * rows)
+        cut_refs[k][4:8, 0:patches] = (HALF * (patch & (SUB - 1)) - offset) & (LANE - 1)
     make_lanes(group, count, patches, slots, around_ref, owner_ref, lanes_ref, table, slot_ref)
 
 
-def strip_kernel(parts, rows, tiles, patches, meta_ref, pay_ref, out_ref):
+def strip_kernel(parts, groups, rows, tiles, patches, *refs):
+    cut_refs, pay_ref, out_refs = refs[:groups], refs[groups], refs[groups + 1 :]
     top = pay_ref[rows - SUB : rows, :]
     for k in range(1, parts):
         top = jnp.maximum(top, pay_ref[(k + 1) * rows - SUB : (k + 1) * rows, :])
     block = lane_of() // HALF
     lines = 4 * patches // SUB
-    out_ref[FIELDS * lines :, :] = top
-
-    for v in range(lines):
-        side, first = v // (patches // SUB), v % (patches // SUB) * SUB
-        acc = jnp.zeros((SUB, LANE), jnp.float32)
-        for m in range(SUB):
-            p = first + m
-            at, shift, fills = meta_ref[side, p], meta_ref[4 + side, p], meta_ref[8 + side, p]
-            strip = pay_ref[pl.ds(at, FIELDS, stride=tiles), :]
-            strip = jnp.concatenate([strip, jnp.zeros((SUB - FIELDS, LANE), jnp.float32)], axis=0)
-            acc = jnp.where(block == fills, pltpu.roll(strip, shift, 1), acc)
-        out_ref[pl.ds(v, FIELDS, stride=lines), :] = acc[:FIELDS, :]
+    for cut_ref, out_ref in zip(cut_refs, out_refs):
+        out_ref[FIELDS * lines :, :] = top
+        for v in range(lines):
+            side, first = v // (patches // SUB), v % (patches // SUB) * SUB
+            acc = None
+            for m in range(SUB):
+                strip = pay_ref[pl.ds(cut_ref[side, first + m], SUB, stride=tiles), :]
+                strip = pltpu.roll(strip, cut_ref[4 + side, first + m], 1)
+                acc = strip if acc is None else jnp.where(block == m, strip, acc)
+            out_ref[pl.ds(v, FIELDS, stride=lines), :] = acc[:FIELDS, :]
 
 
 def lanes_at(lanes_ref, g, side, kind):
@@ -331,10 +328,10 @@
     return ((g * 10 + kept) * (FIELDS + 1) + n) * SUB
 
 
-def step_kernel(group, count, patches, slots, *refs):
+def step_kernel(count, patches, slots, *refs):
     u_ref, edge_ref, dx_ref, dy_ref, lanes_ref = refs[:5]
-    strip_refs, out_ref = refs[5 : 5 + group], refs[5 + group]
-    next_u, next_aux, next_dx, strips, doubled, coarse_ref, border_ref = refs[6 + group :]
+    strip_refs, out_ref = refs[5:7], refs[7]
+    next_u, next_aux, next_dx, strips, doubled, coarse_ref, border_ref = refs[8:]
     lines = 4 * patches // SUB
     sets = patches // PX
     lane, sub = lane_of(), sub_of()
@@ -501,16 +498,16 @@
         return jnp.swapaxes(x, 2, 3)
 
     sets = patches // PX
-    payload, raw, meta, lanes = pl.pallas_call(
+    payload, raw, lanes, *cuts = pl.pallas_call(
         functools.partial(pack_kernel, tiles, rows, group, count, patches, slots, (n_gx, n_gz)),
         out_shape=(
             pltpu.VMEM((rows, LANE), f32),
             pltpu.VMEM((1, 1, FIELDS, count, SUB * LANE), f32),
-            pltpu.VMEM((16, max(LANE, patches)), jnp.int32),
             pltpu.VMEM(((sets * 4 * 3 + 1) * SUB, LANE), jnp.int32),
-        ),
+        )
+        + (pltpu.VMEM((SUB, max(LANE, patches)), jnp.int32),) * n_gz,
         in_specs=[smem] + [vmem] * 5,
-        out_specs=(vmem,) * 4,
+        out_specs=(vmem,) * (3 + n_gz),
         scratch_shapes=[pltpu.VMEM((SUB, LANE), jnp.int32), pltpu.SMEM((slots + 1,), jnp.int32)],
         name="pack",
     )(
@@ -522,23 +519,22 @@
         coarse_boxes.reshape(FIELDS * BOX_ROWS, LANE),
     )
 
-    def gathered(x, axis, n):
-        if power_of_two(n):
-            perms = [[(i, i ^ k) for i in range(n)] for k in range(1, n)]
-        else:
-            perms = [[(i, (i + k) % n) for i in range(n)] for k in range(1, n)]
-        return jnp.concatenate([x] + [lax.ppermute(x, axis, perm) for perm in perms], axis=0)
-
-    payload = gathered(gathered(payload, "gx", n_gx), "gz", n_gz)
-
-    strip = pl.pallas_call(
-        functools.partial(strip_kernel, parts, rows, tiles, patches),
-        out_shape=pltpu.VMEM((strip_rows, LANE), f32),
-        in_specs=[smem, vmem],
-        out_specs=vmem,
-        compiler_params=limit(parts * rows, strip_rows),
+    if power_of_two(n_gx):
+        perms = [[(i, i ^ k) for i in range(n_gx)] for k in range(1, n_gx)]
+    else:
+        perms = [[(i, (i + k) % n_gx) for i in range(n_gx)] for k in range(1, n_gx)]
+    boxes = [payload] + [lax.ppermute(payload, "gx", perm) for perm in perms]
+    boxes = jnp.concatenate(boxes + [jnp.zeros((SUB * tiles, LANE), f32)], axis=0)
+    cuts = cuts[:1] + [lax.ppermute(cuts[k], "gz", [(i, i ^ k) for i in range(n_gz)]) for k in range(1, n_gz)]
+
+    strips = pl.pallas_call(
+        functools.partial(strip_kernel, n_gx, n_gz, rows, tiles, patches),
+        out_shape=[pltpu.VMEM((strip_rows, LANE), f32)] * n_gz,
+        in_specs=[smem] * n_gz + [vmem],
+        out_specs=[vmem] * n_gz,
+        compiler_params=limit(n_gx * rows + SUB * tiles, n_gz * strip_rows),
         name="strips",
-    )(meta, payload)
+    )(*cuts, boxes)
 
     def to_group(x, after=None):
         blocks, have = [x] + [None] * (group - 1), [0]
@@ -553,7 +549,13 @@
             have = have + [k ^ mask for k in have]
         return blocks
 
-    raws = to_group(raw, strip)
+    raws = to_group(raw, strips[0])
+
+    shares = [strips[0]]
+    for k in range(1, n_gz * group):
+        if k // n_gz % 2 == 0:
+            perm = [(i, i ^ k) for i in range(n_gz * group)]
+            shares.append(lax.ppermute(strips[k % n_gz], ("gy", "gz"), perm))
 
     made_rows = [
         sets * FIELDS * PLANE,
@@ -572,7 +574,11 @@
         name="prepare",
     )(lanes, *raws)
 
-    strips = to_group(strip, made[0])
+    shares = lax.optimization_barrier(shares + [made[0]])[:-1]
+    row = lax.broadcasted_iota(jnp.int32, (strip_rows, LANE), 0)
+    joined = jnp.where(row < FIELDS * lines, functools.reduce(jnp.add, shares), functools.reduce(jnp.maximum, shares))
+
+    strips = [joined, lax.ppermute(joined, "gy", [(i, i ^ 1) for i in range(group)])]
     scratch_rows = [sets * FIELDS * PLANE, sets * AUX * PLANE, sets * FIELDS * DEEP * FACES] + [
         FIELDS * lines,
         4 * patches // LANE * FIELDS * PX,
@@ -580,12 +586,12 @@
         sets * FIELDS * 8 * SUB,
     ]
     out = pl.pallas_call(
-        functools.partial(step_kernel, group, count, patches, slots),
+        functools.partial(step_kernel, count, patches, slots),
         out_shape=jax.ShapeDtypeStruct((1, 1, FIELDS, slots, SUB * LANE), f32),
-        in_specs=[vmem] * (5 + group),
+        in_specs=[vmem] * 7,
         out_specs=vmem,
         scratch_shapes=[pltpu.VMEM((n, LANE), f32) for n in scratch_rows],
-        compiler_params=limit(*scratch_rows, *made_rows, lanes.shape[0], group * strip_rows, FIELDS * slots * SUB),
+        compiler_params=limit(*scratch_rows, *made_rows, lanes.shape[0], 2 * strip_rows, FIELDS * slots * SUB),
         name="step",
     )(*made, lanes, *strips)
     return sides_first(out)

time: 26.7 us -> 26.2 us (0.981)
  waiting for transfers between devices: 9.4 us -> 6.81 us
  starting transfers between devices: 10.8 us -> 12.7 us
    ppermute x4 -> x8, starting transfers between devices: 7.24 us -> 10.9 us  [the longest x3 5.68 us: per_device(): boxes = [payload] + [lax.ppermute(payload, 'gx', perm) for perm in perms]]
    ppermute x6 -> x3, waiting for transfers between devices: 2.41 us -> 0.01 us  [to_group(): blocks[k ^ mask] = lax.ppermute(block, 'gy', perm)]
    ppermute x6 -> x3, starting transfers between devices: 3.57 us -> 1.81 us  [to_group(): blocks[k ^ mask] = lax.ppermute(block, 'gy', perm)]
    ppermute x4 -> x8, waiting for transfers between devices: 6.98 us -> 6.8 us  [the longest x3 3.28 us: per_device(): shares.append(lax.ppermute(strips[k % n_gz], ('gy', 'gz'), perm))]
  transfers between devices with their start and end apart: 10 -> 11, of which waited for: 5 -> 4; matrix products, arithmetic and copies ran while one was open for 0% -> 0% of each run, Pallas kernels for 8% -> 8%
where the time goes in v6:
time: 26.2 us; the launch traced here: 26.1 us
  starting transfers between devices  12.7 us (48%)
  waiting for transfers between devices  6.81 us (26%)
  Pallas kernels  6.39 us (24%)
    ppermute x3, starting transfers between devices, per_device(): boxes = [payload] + [lax.ppermute(payload, 'gx', perm) for perm in perms]  5.68 us
    ppermute x3, starting transfers between devices, per_device(): shares.append(lax.ppermute(strips[k % n_gz], ('gy', 'gz'), perm))  3.55 us
    ppermute x3, waiting for transfers between devices, per_device(): shares.append(lax.ppermute(strips[k % n_gz], ('gy', 'gz'), perm))  3.28 us
    pallas_call x1, Pallas kernels, per_device(): pl.pallas_call(functools.partial(step_kernel, count, patches, slots), out...  2.98 us
    ppermute x3, waiting for transfers between devices, per_device(): boxes = [payload] + [lax.ppermute(payload, 'gx', perm) for perm in perms]  2.31 us
    ppermute x3, starting transfers between devices, to_group(): blocks[k ^ mask] = lax.ppermute(block, 'gy', perm)  1.81 us
    ppermute x1, starting transfers between devices, per_device(): lax.ppermute(cuts[k], 'gz', [(i, i ^ k) for i in range(n_gz)])  1.56 us
    pallas_call x1, Pallas kernels, per_device(): pl.pallas_call(functools.partial(pack_kernel, tiles, rows, group, count,...  1.23 us
  transfers between devices with their start and end apart: 11, of which 4 were waited for; matrix products, arithmetic and copies ran while one was open for 0% of the time, Pallas kernels for 8%

profile of v6, /device:TPU:0, one launch (start us, length us, event | category | flops | bytes accessed | tf_op | source)
XLA Modules:
  0.0 26.1 jit_solution(11929188602244434993)
XLA Ops:
  0.0 1.2 %pack.1 = (f32[48,128]{1,0:T(8,128)S(1)}, f32[1,1,5,8,1024]{4,3,2,1,0:T(8,128)S(1)}, s32[104,128]{1,0:T(8,128)S(1)}, s32[8,128]{1,0:T(8,128)S(1)}, s32[8,128]{1,0:T(8,128)S(1)}) custom-call(s32[1,1,1,32]{3,2,1,0:T(1,128)} %bitcast.12, s32[1,1,4,32]{3,2,1,0:T(4,128)} %bitcast.9, s32[1,1,4,32]{3,2,1,0:T(4,128)} %bitcast.10, s32[1,1,4,32]{3,2,1,0:T(4,128)} %bitcast.11, ...), custom_call_target="tpu_custom_call" | custom-call | tf_op jit(solution)/shard_map/pack/pallas_call | solution.py:501
  1.2 3.1 %collective-permute-start.3 = (f32[48,128]{1,0:T(8,128)S(1)}, f32[48,128]{1,0:T(8,128)S(1)}, u32[]{:S(2)}, u32[]{:S(2)}) collective-permute-start(f32[48,128]{1,0:T(8,128)S(1)} %get-tuple-element.25), channel_id=1, source_target_pairs={{0,8},{8,0},{16,24},{24,16},{1,9},{9,1},{17,25},{25,17},{2,10},{10... | collective-permute-start | bytes 73736 | tf_op jit(solution)/shard_map/ppermute | solution.py:526
  4.3 2.6 %collective-permute-start.4 = (f32[48,128]{1,0:T(8,128)S(1)}, f32[48,128]{1,0:T(8,128)S(1)}, u32[]{:S(2)}, u32[]{:S(2)}) collective-permute-start(f32[48,128]{1,0:T(8,128)S(1)} %get-tuple-element.25), channel_id=1, source_target_pairs={{0,16},{8,24},{16,0},{24,8},{1,17},{9,25},{17,1},{25,9},{2,18},{10... | collective-permute-start | bytes 73736 | tf_op jit(solution)/shard_map/ppermute | solution.py:526
  6.9 0.0 collective-permute-start.5
  6.9 1.7 %collective-permute-start.1 = (f32[1,1,5,8,1024]{4,3,2,1,0:T(8,128)S(1)}, f32[1,1,5,8,1024]{4,3,2,1,0:T(8,128)S(1)}, u32[]{:S(2)}, u32[]{:S(2)}) collective-permute-start(f32[1,1,5,8,1024]{4,3,2,1,0:T(8,128)S(1)} %get-tuple-element.22.refs_0_), channel_id=1, source_target_pairs={{0,4},{2,6},{4,0},{6,2},{1,5},{3,7},{5,1},{7,3},{8,12},{10,14},{12... | collective-permute-start | bytes 491528 | tf_op jit(solution)/shard_map/ppermute | solution.py:548
  8.7 0.0 collective-permute-start
  8.7 0.0 collective-permute-done.3
  8.7 1.6 %collective-permute-start.2 = (s32[8,128]{1,0:T(8,128)S(1)}, s32[8,128]{1,0:T(8,128)S(1)}, u32[]{:S(2)}, u32[]{:S(2)}) collective-permute-start(s32[8,128]{1,0:T(8,128)S(1)} %get-tuple-element.24), channel_id=1, source_target_pairs={{0,1},{1,0},{2,3},{3,2},{4,5},{5,4},{6,7},{7,6},{8,9},{9,8},{10,11... | collective-permute-start | bytes 12296 | tf_op jit(solution)/shard_map/ppermute | solution.py:528
  10.2 0.0 collective-permute-done.4
  10.2 2.3 %collective-permute-done.5 = f32[48,128]{1,0:T(8,128)S(1)} collective-permute-done((f32[48,128]{1,0:T(8,128)S(1)}, f32[48,128]{1,0:T(8,128)S(1)}, u32[]{:S(2)}, u32[]{:S(2)}) %collective-permute-start.5) | collective-permute-done | bytes 24608 | tf_op jit(solution)/shard_map/ppermute | solution.py:526
  12.5 0.0 collective-permute-done.2.refs_1_
  12.6 1.0 %strips.1 = (f32[88,128]{1,0:T(8,128)S(1)}, f32[88,128]{1,0:T(8,128)S(1)}) custom-call(s32[8,128]{1,0:T(8,128)S(1)} %get-tuple-element.23.refs_0_, s32[8,128]{1,0:T(8,128)S(1)} %collective-permute-done.2.refs_1_, f32[256,128]{1,0:T(8,128)S(1)} %broadcast_dynamic-update-slice_fusion.refs_2_), custom_call_target="tpu_custom_call" | custom-call | tf_op jit(solution)/shard_map/strips/pallas_call | solution.py:530
  13.6 0.0 collective-permute-done.1.refs_2_
  13.6 0.1 collective-permute-start.6
  13.7 1.6 %collective-permute-start.8 = (f32[88,128]{1,0:T(8,128)S(1)}, f32[88,128]{1,0:T(8,128)S(1)}, u32[]{:S(2)}, u32[]{:S(2)}) collective-permute-start(f32[88,128]{1,0:T(8,128)S(1)} %get-tuple-element.33), channel_id=1, source_target_pairs={{0,4},{1,5},{2,6},{3,7},{4,0},{5,1},{6,2},{7,3},{8,12},{9,13},{10,... | collective-permute-start | bytes 135176 | tf_op jit(solution)/shard_map/ppermute | solution.py:558
  15.3 1.5 %collective-permute-start.7 = (f32[88,128]{1,0:T(8,128)S(1)}, f32[88,128]{1,0:T(8,128)S(1)}, u32[]{:S(2)}, u32[]{:S(2)}) collective-permute-start(f32[88,128]{1,0:T(8,128)S(1)} %get-tuple-element.32), channel_id=1, source_target_pairs={{0,1},{1,0},{2,3},{3,2},{4,5},{5,4},{6,7},{7,6},{8,9},{9,8},{10,11... | collective-permute-start | bytes 135176 | tf_op jit(solution)/shard_map/ppermute | solution.py:558
  16.7 0.5 %collective-permute-start.9 = (f32[88,128]{1,0:T(8,128)S(1)}, f32[88,128]{1,0:T(8,128)S(1)}, u32[]{:S(2)}, u32[]{:S(2)}) collective-permute-start(f32[88,128]{1,0:T(8,128)S(1)} %get-tuple-element.32), channel_id=1, source_target_pairs={{0,5},{1,4},{2,7},{3,6},{4,1},{5,0},{6,3},{7,2},{8,13},{9,12},{10,... | collective-permute-start | bytes 135176 | tf_op jit(solution)/shard_map/ppermute | solution.py:558
  17.2 0.0 collective-permute-done.refs_1_
  17.2 0.0 collective-permute-done.6.refs_3_
  17.2 1.2 %prepare.1 = (f32[2400,128]{1,0:T(8,128)S(1)}, f32[480,128]{1,0:T(8,128)S(1)}, f32[1600,128]{1,0:T(8,128)S(1)}, f32[1440,128]{1,0:T(8,128)S(1)}) custom-call(s32[104,128]{1,0:T(8,128)S(1)} %get-tuple-element.21.lanes_ref.refs_4_, f32[1,1,5,8,1024]{4,3,2,1,0:T(8,128)S(1)} %get-tuple-element.22.refs_0_, ...), custom_call_target="tpu_custom_call" | custom-call | flops 9830400 | bytes 1280000 | tf_op jit(solution)/shard_map/prepare/pallas_call | solution.py:566
  18.4 0.0 collective-permute-done.8
  18.4 1.1 %collective-permute-done.7 = f32[88,128]{1,0:T(8,128)S(1)} collective-permute-done((f32[88,128]{1,0:T(8,128)S(1)}, f32[88,128]{1,0:T(8,128)S(1)}, u32[]{:S(2)}, u32[]{:S(2)}) %collective-permute-start.7) | collective-permute-done | bytes 45088 | tf_op jit(solution)/shard_map/ppermute | solution.py:558
  19.5 2.2 %collective-permute-done.9 = f32[88,128]{1,0:T(8,128)S(1)} collective-permute-done((f32[88,128]{1,0:T(8,128)S(1)}, f32[88,128]{1,0:T(8,128)S(1)}, u32[]{:S(2)}, u32[]{:S(2)}) %collective-permute-start.9) | collective-permute-done | bytes 45088 | tf_op jit(solution)/shard_map/ppermute | solution.py:558
  21.7 0.1 maximum_select_fusion.refs_5_
  21.8 0.1 collective-permute-start.10
  21.9 1.2 %collective-permute-done.10.refs_6_ = f32[88,128]{1,0:T(8,128)S(1)} collective-permute-done((f32[88,128]{1,0:T(8,128)S(1)}, f32[88,128]{1,0:T(8,128)S(1)}, u32[]{:S(2)}, u32[]{:S(2)}) %collective-permute-start.10) | collective-permute-done | bytes 45088 | tf_op jit(solution)/shard_map/ppermute | solution.py:581
  23.1 3.0 %step.1 = f32[1,1,5,16,1024]{4,3,2,1,0:T(8,128)} custom-call(f32[2400,128]{1,0:T(8,128)S(1)} %get-tuple-element.28.refs_0_, f32[480,128]{1,0:T(8,128)S(1)} %get-tuple-element.29.refs_1_, f32[1600,128]{1,0:T(8,128)S(1)} %get-tuple-element.30.refs_2_, f32[1440,128]{1,0:T(8,128)S(1)} %get-tuple-element.31.refs_3_, ...), custom_call_target="tpu_custom_call" | custom-call | tf_op jit(solution)/shard_map/step/pallas_call | solution.py:588
  (6 shorter events, 0.0 us)
Async XLA Ops:
  1.2 7.4 %collective-permute-start.3 = (f32[48,128]{1,0:T(8,128)S(1)}, f32[48,128]{1,0:T(8,128)S(1)}, u32[]{:S(2)}, u32[]{:S(2)}) collective-permute-start(f32[48,128]{1,0:T(8,128)S(1)} %get-tuple-element.25), channel_id=1, source_target_pairs={{0,8},{8,0},{16,24},{24,16},{1,9},{9,1},{17,25},{25,17},{2,10},{10... | collective-permute-start | bytes 73736 | tf_op jit(solution)/shard_map/ppermute | solution.py:526
  4.3 5.9 %collective-permute-start.4 = (f32[48,128]{1,0:T(8,128)S(1)}, f32[48,128]{1,0:T(8,128)S(1)}, u32[]{:S(2)}, u32[]{:S(2)}) collective-permute-start(f32[48,128]{1,0:T(8,128)S(1)} %get-tuple-element.25), channel_id=1, source_target_pairs={{0,16},{8,24},{16,0},{24,8},{1,17},{9,25},{17,1},{25,9},{2,18},{10... | collective-permute-start | bytes 73736 | tf_op jit(solution)/shard_map/ppermute | solution.py:526
  6.9 5.6 %collective-permute-start.5 = (f32[48,128]{1,0:T(8,128)S(1)}, f32[48,128]{1,0:T(8,128)S(1)}, u32[]{:S(2)}, u32[]{:S(2)}) collective-permute-start(f32[48,128]{1,0:T(8,128)S(1)} %get-tuple-element.25), channel_id=1, source_target_pairs={{0,24},{8,16},{16,8},{24,0},{1,25},{9,17},{17,9},{25,1},{2,26},{10... | collective-permute-start | bytes 73736 | tf_op jit(solution)/shard_map/ppermute | solution.py:526
  6.9 6.7 %collective-permute-start.1 = (f32[1,1,5,8,1024]{4,3,2,1,0:T(8,128)S(1)}, f32[1,1,5,8,1024]{4,3,2,1,0:T(8,128)S(1)}, u32[]{:S(2)}, u32[]{:S(2)}) collective-permute-start(f32[1,1,5,8,1024]{4,3,2,1,0:T(8,128)S(1)} %get-tuple-element.22.refs_0_), channel_id=1, source_target_pairs={{0,4},{2,6},{4,0},{6,2},{1,5},{3,7},{5,1},{7,3},{8,12},{10,14},{12... | collective-permute-start | bytes 491528 | tf_op jit(solution)/shard_map/ppermute | solution.py:548
  8.7 8.6 %collective-permute-start = (f32[1,1,5,8,1024]{4,3,2,1,0:T(8,128)S(1)}, f32[1,1,5,8,1024]{4,3,2,1,0:T(8,128)S(1)}, u32[]{:S(2)}, u32[]{:S(2)}) collective-permute-start(f32[1,1,5,8,1024]{4,3,2,1,0:T(8,128)S(1)} %get-tuple-element.22.refs_0_), channel_id=1, source_target_pairs={{0,2},{2,0},{4,6},{6,4},{1,3},{3,1},{5,7},{7,5},{8,10},{10,8},{12,... | collective-permute-start | bytes 491528 | tf_op jit(solution)/shard_map/ppermute | solution.py:548
  8.7 3.9 %collective-permute-start.2 = (s32[8,128]{1,0:T(8,128)S(1)}, s32[8,128]{1,0:T(8,128)S(1)}, u32[]{:S(2)}, u32[]{:S(2)}) collective-permute-start(s32[8,128]{1,0:T(8,128)S(1)} %get-tuple-element.24), channel_id=1, source_target_pairs={{0,1},{1,0},{2,3},{3,2},{4,5},{5,4},{6,7},{7,6},{8,9},{9,8},{10,11... | collective-permute-start | bytes 12296 | tf_op jit(solution)/shard_map/ppermute | solution.py:528
  13.6 3.6 %collective-permute-start.6 = (f32[1,1,5,8,1024]{4,3,2,1,0:T(8,128)S(1)}, f32[1,1,5,8,1024]{4,3,2,1,0:T(8,128)S(1)}, u32[]{:S(2)}, u32[]{:S(2)}) collective-permute-start(f32[1,1,5,8,1024]{4,3,2,1,0:T(8,128)S(1)} %collective-permute-done.1.refs_2_), channel_id=1, source_target_pairs={{0,2},{2,0},{4,6},{6,4},{1,3},{3,1},{5,7},{7,5},{8,10},{10,8},{12,... | collective-permute-start | bytes 491528 | tf_op jit(solution)/shard_map/ppermute | solution.py:548
  13.7 4.7 %collective-permute-start.8 = (f32[88,128]{1,0:T(8,128)S(1)}, f32[88,128]{1,0:T(8,128)S(1)}, u32[]{:S(2)}, u32[]{:S(2)}) collective-permute-start(f32[88,128]{1,0:T(8,128)S(1)} %get-tuple-element.33), channel_id=1, source_target_pairs={{0,4},{1,5},{2,6},{3,7},{4,0},{5,1},{6,2},{7,3},{8,12},{9,13},{10,... | collective-permute-start | bytes 135176 | tf_op jit(solution)/shard_map/ppermute | solution.py:558
  15.3 4.3 %collective-permute-start.7 = (f32[88,128]{1,0:T(8,128)S(1)}, f32[88,128]{1,0:T(8,128)S(1)}, u32[]{:S(2)}, u32[]{:S(2)}) collective-permute-start(f32[88,128]{1,0:T(8,128)S(1)} %get-tuple-element.32), channel_id=1, source_target_pairs={{0,1},{1,0},{2,3},{3,2},{4,5},{5,4},{6,7},{7,6},{8,9},{9,8},{10,11... | collective-permute-start | bytes 135176 | tf_op jit(solution)/shard_map/ppermute | solution.py:558
  16.7 4.9 %collective-permute-start.9 = (f32[88,128]{1,0:T(8,128)S(1)}, f32[88,128]{1,0:T(8,128)S(1)}, u32[]{:S(2)}, u32[]{:S(2)}) collective-permute-start(f32[88,128]{1,0:T(8,128)S(1)} %get-tuple-element.32), channel_id=1, source_target_pairs={{0,5},{1,4},{2,7},{3,6},{4,1},{5,0},{6,3},{7,2},{8,13},{9,12},{10,... | collective-permute-start | bytes 135176 | tf_op jit(solution)/shard_map/ppermute | solution.py:558
  21.8 1.3 %collective-permute-start.10 = (f32[88,128]{1,0:T(8,128)S(1)}, f32[88,128]{1,0:T(8,128)S(1)}, u32[]{:S(2)}, u32[]{:S(2)}) collective-permute-start(f32[88,128]{1,0:T(8,128)S(1)} %maximum_select_fusion.refs_5_), channel_id=1, source_target_pairs={{0,2},{2,0},{4,6},{6,4},{1,3},{3,1},{5,7},{7,5},{8,10},{10,8},{12,... | collective-permute-start | bytes 135176 | tf_op jit(solution)/shard_map/ppermute | solution.py:581

commit v7 on v6

--- a/solution.py
+++ b/solution.py
@@ -527,14 +527,19 @@
     boxes = jnp.concatenate(boxes + [jnp.zeros((SUB * tiles, LANE), f32)], axis=0)
     cuts = cuts[:1] + [lax.ppermute(cuts[k], "gz", [(i, i ^ k) for i in range(n_gz)]) for k in range(1, n_gz)]
 
-    strips = pl.pallas_call(
-        functools.partial(strip_kernel, n_gx, n_gz, rows, tiles, patches),
-        out_shape=[pltpu.VMEM((strip_rows, LANE), f32)] * n_gz,
-        in_specs=[smem] * n_gz + [vmem],
-        out_specs=[vmem] * n_gz,
-        compiler_params=limit(n_gx * rows + SUB * tiles, n_gz * strip_rows),
-        name="strips",
-    )(*cuts, boxes)
+    def cut_strips(cuts, boxes, name):
+        return pl.pallas_call(
+            functools.partial(strip_kernel, n_gx, len(cuts), rows, tiles, patches),
+            out_shape=[pltpu.VMEM((strip_rows, LANE), f32)] * len(cuts),
+            in_specs=[smem] * len(cuts) + [vmem],
+            out_specs=[vmem] * len(cuts),
+            compiler_params=limit(n_gx * rows + SUB * tiles, len(cuts) * strip_rows),
+            name=name,
+        )(*cuts, boxes)
+
+    strips = cut_strips(cuts[:1], boxes, "own_strips")
+    boxes, _ = lax.optimization_barrier((boxes, strips[0]))
+    strips = strips + cut_strips(cuts[1:], boxes, "other_strips")
 
     def to_group(x, after=None):
         blocks, have = [x] + [None] * (group - 1), [0]

time: 26.2 us -> 29.5 us (1.13)
  waiting for transfers between devices: 6.81 us -> 9.54 us
  Pallas kernels: 6.39 us -> 7 us
    ppermute x1, waiting for transfers between devices: 0.01 us -> 2.12 us  [per_device(): lax.ppermute(cuts[k], 'gz', [(i, i ^ k) for i in range(n_gz)])]
    ppermute x3, waiting for transfers between devices: 2.31 us -> 3.86 us  [per_device(): boxes = [payload] + [lax.ppermute(payload, 'gx', perm) for perm in perms]]
    ppermute x3, waiting for transfers between devices: 3.28 us -> 2.35 us  [per_device(): shares.append(lax.ppermute(strips[k % n_gz], ('gy', 'gz'), perm))]
    pallas_call x1 -> x2, Pallas kernels: 1.02 us -> 1.62 us  [cut_strips(): pl.pallas_call(functools.partial(strip_kernel, n_gx, len(cuts), rows, til...]
  transfers between devices with their start and end apart: 11 -> 11, of which waited for: 4 -> 6; matrix products, arithmetic and copies ran while one was open for 0% -> 0% of each run, Pallas kernels for 8% -> 9%
where the time goes in v7:
time: 29.5 us; the launch traced here: 29.4 us
  starting transfers between devices  12.7 us (43%)
  waiting for transfers between devices  9.54 us (32%)
  Pallas kernels  7 us (24%)
    ppermute x3, starting transfers between devices, per_device(): boxes = [payload] + [lax.ppermute(payload, 'gx', perm) for perm in perms]  5.68 us
    ppermute x3, waiting for transfers between devices, per_device(): boxes = [payload] + [lax.ppermute(payload, 'gx', perm) for perm in perms]  3.86 us
    ppermute x3, starting transfers between devices, per_device(): shares.append(lax.ppermute(strips[k % n_gz], ('gy', 'gz'), perm))  3.55 us
    pallas_call x1, Pallas kernels, per_device(): pl.pallas_call(functools.partial(step_kernel, count, patches, slots), out...  2.98 us
    ppermute x3, waiting for transfers between devices, per_device(): shares.append(lax.ppermute(strips[k % n_gz], ('gy', 'gz'), perm))  2.35 us
    ppermute x1, waiting for transfers between devices, per_device(): lax.ppermute(cuts[k], 'gz', [(i, i ^ k) for i in range(n_gz)])  2.12 us
    ppermute x3, starting transfers between devices, to_group(): blocks[k ^ mask] = lax.ppermute(block, 'gy', perm)  1.81 us
    pallas_call x2, Pallas kernels, cut_strips(): pl.pallas_call(functools.partial(strip_kernel, n_gx, len(cuts), rows, til...  1.62 us
  transfers between devices with their start and end apart: 11, of which 6 were waited for; matrix products, arithmetic and copies ran while one was open for 0% of the time, Pallas kernels for 9%

profile of v7, /device:TPU:0, one launch (start us, length us, event | category | flops | bytes accessed | tf_op | source)
XLA Modules:
  0.0 29.4 jit_solution(10731425797799883583)
XLA Ops:
  0.0 1.2 %pack.1 = (f32[48,128]{1,0:T(8,128)S(1)}, f32[1,1,5,8,1024]{4,3,2,1,0:T(8,128)S(1)}, s32[104,128]{1,0:T(8,128)S(1)}, s32[8,128]{1,0:T(8,128)S(1)}, s32[8,128]{1,0:T(8,128)S(1)}) custom-call(s32[1,1,1,32]{3,2,1,0:T(1,128)} %bitcast.12, s32[1,1,4,32]{3,2,1,0:T(4,128)} %bitcast.9, s32[1,1,4,32]{3,2,1,0:T(4,128)} %bitcast.10, s32[1,1,4,32]{3,2,1,0:T(4,128)} %bitcast.11, ...), custom_call_target="tpu_custom_call" | custom-call | tf_op jit(solution)/shard_map/pack/pallas_call | solution.py:501
  1.2 3.1 %collective-permute-start.2 = (f32[48,128]{1,0:T(8,128)S(1)}, f32[48,128]{1,0:T(8,128)S(1)}, u32[]{:S(2)}, u32[]{:S(2)}) collective-permute-start(f32[48,128]{1,0:T(8,128)S(1)} %get-tuple-element.23), channel_id=1, source_target_pairs={{0,8},{8,0},{16,24},{24,16},{1,9},{9,1},{17,25},{25,17},{2,10},{10... | collective-permute-start | bytes 73736 | tf_op jit(solution)/shard_map/ppermute | solution.py:526
  4.3 2.6 %collective-permute-start.3 = (f32[48,128]{1,0:T(8,128)S(1)}, f32[48,128]{1,0:T(8,128)S(1)}, u32[]{:S(2)}, u32[]{:S(2)}) collective-permute-start(f32[48,128]{1,0:T(8,128)S(1)} %get-tuple-element.23), channel_id=1, source_target_pairs={{0,16},{8,24},{16,0},{24,8},{1,17},{9,25},{17,1},{25,9},{2,18},{10... | collective-permute-start | bytes 73736 | tf_op jit(solution)/shard_map/ppermute | solution.py:526
  6.9 0.0 collective-permute-start.4
  6.9 1.7 %collective-permute-start.1 = (f32[1,1,5,8,1024]{4,3,2,1,0:T(8,128)S(1)}, f32[1,1,5,8,1024]{4,3,2,1,0:T(8,128)S(1)}, u32[]{:S(2)}, u32[]{:S(2)}) collective-permute-start(f32[1,1,5,8,1024]{4,3,2,1,0:T(8,128)S(1)} %get-tuple-element.21.refs_0_), channel_id=1, source_target_pairs={{0,4},{2,6},{4,0},{6,2},{1,5},{3,7},{5,1},{7,3},{8,12},{10,14},{12... | collective-permute-start | bytes 491528 | tf_op jit(solution)/shard_map/ppermute | solution.py:553
  8.7 0.0 collective-permute-start
  8.7 0.0 collective-permute-done.2
  8.7 0.7 %collective-permute-done.3 = f32[48,128]{1,0:T(8,128)S(1)} collective-permute-done((f32[48,128]{1,0:T(8,128)S(1)}, f32[48,128]{1,0:T(8,128)S(1)}, u32[]{:S(2)}, u32[]{:S(2)}) %collective-permute-start.3) | collective-permute-done | bytes 24608 | tf_op jit(solution)/shard_map/ppermute | solution.py:526
  9.4 3.1 %collective-permute-done.4 = f32[48,128]{1,0:T(8,128)S(1)} collective-permute-done((f32[48,128]{1,0:T(8,128)S(1)}, f32[48,128]{1,0:T(8,128)S(1)}, u32[]{:S(2)}, u32[]{:S(2)}) %collective-permute-start.4) | collective-permute-done | bytes 24608 | tf_op jit(solution)/shard_map/ppermute | solution.py:526
  12.5 0.8 %own_strips.1 = f32[88,128]{1,0:T(8,128)S(1)} custom-call(s32[8,128]{1,0:T(8,128)S(1)} %get-tuple-element.22.refs_0_, f32[256,128]{1,0:T(8,128)S(1)} %broadcast_dynamic-update-slice_fusion.refs_1_), custom_call_target="tpu_custom_call" | custom-call | tf_op jit(solution)/shard_map/own_strips/pallas_call | solution.py:531
  13.4 0.0 collective-permute-done.1.refs_2_
  13.4 0.1 collective-permute-start.5
  13.5 1.6 %collective-permute-start.6 = (s32[8,128]{1,0:T(8,128)S(1)}, s32[8,128]{1,0:T(8,128)S(1)}, u32[]{:S(2)}, u32[]{:S(2)}) collective-permute-start(s32[8,128]{1,0:T(8,128)S(1)} %get-tuple-element.29), channel_id=1, source_target_pairs={{0,1},{1,0},{2,3},{3,2},{4,5},{5,4},{6,7},{7,6},{8,9},{9,8},{10,11... | collective-permute-start | bytes 12296 | tf_op jit(solution)/shard_map/ppermute | solution.py:528
  15.0 2.1 %collective-permute-done.6.refs_0_ = s32[8,128]{1,0:T(8,128)S(1)} collective-permute-done((s32[8,128]{1,0:T(8,128)S(1)}, s32[8,128]{1,0:T(8,128)S(1)}, u32[]{:S(2)}, u32[]{:S(2)}) %collective-permute-start.6) | collective-permute-done | bytes 4128 | tf_op jit(solution)/shard_map/ppermute | solution.py:528
  17.1 0.8 %other_strips.1 = f32[88,128]{1,0:T(8,128)S(1)} custom-call(s32[8,128]{1,0:T(8,128)S(1)} %collective-permute-done.6.refs_0_, f32[256,128]{1,0:T(8,128)S(1)} %broadcast_dynamic-update-slice_fusion.refs_1_), custom_call_target="tpu_custom_call" | custom-call | tf_op jit(solution)/shard_map/other_strips/pallas_call | solution.py:531
  17.9 1.6 %collective-permute-start.7 = (f32[88,128]{1,0:T(8,128)S(1)}, f32[88,128]{1,0:T(8,128)S(1)}, u32[]{:S(2)}, u32[]{:S(2)}) collective-permute-start(f32[88,128]{1,0:T(8,128)S(1)} %other_strips.1), channel_id=1, source_target_pairs={{0,1},{1,0},{2,3},{3,2},{4,5},{5,4},{6,7},{7,6},{8,9},{9,8},{10,11... | collective-permute-start | bytes 135176 | tf_op jit(solution)/shard_map/ppermute | solution.py:563
  19.5 1.5 %collective-permute-start.9 = (f32[88,128]{1,0:T(8,128)S(1)}, f32[88,128]{1,0:T(8,128)S(1)}, u32[]{:S(2)}, u32[]{:S(2)}) collective-permute-start(f32[88,128]{1,0:T(8,128)S(1)} %other_strips.1), channel_id=1, source_target_pairs={{0,5},{1,4},{2,7},{3,6},{4,1},{5,0},{6,3},{7,2},{8,13},{9,12},{10,... | collective-permute-start | bytes 135176 | tf_op jit(solution)/shard_map/ppermute | solution.py:563
  21.0 0.5 %collective-permute-start.8 = (f32[88,128]{1,0:T(8,128)S(1)}, f32[88,128]{1,0:T(8,128)S(1)}, u32[]{:S(2)}, u32[]{:S(2)}) collective-permute-start(f32[88,128]{1,0:T(8,128)S(1)} %own_strips.1), channel_id=1, source_target_pairs={{0,4},{1,5},{2,6},{3,7},{4,0},{5,1},{6,2},{7,3},{8,12},{9,13},{10,... | collective-permute-start | bytes 135176 | tf_op jit(solution)/shard_map/ppermute | solution.py:563
  21.5 0.0 collective-permute-done.refs_1_
  21.5 0.0 collective-permute-done.5.refs_3_
  21.5 1.2 %prepare.1 = (f32[2400,128]{1,0:T(8,128)S(1)}, f32[480,128]{1,0:T(8,128)S(1)}, f32[1600,128]{1,0:T(8,128)S(1)}, f32[1440,128]{1,0:T(8,128)S(1)}) custom-call(s32[104,128]{1,0:T(8,128)S(1)} %get-tuple-element.20.lanes_ref.refs_4_, f32[1,1,5,8,1024]{4,3,2,1,0:T(8,128)S(1)} %get-tuple-element.21.refs_0_, ...), custom_call_target="tpu_custom_call" | custom-call | flops 9830400 | bytes 1280000 | tf_op jit(solution)/shard_map/prepare/pallas_call | solution.py:571
  22.7 0.0 collective-permute-done.7
  22.7 1.8 %collective-permute-done.9 = f32[88,128]{1,0:T(8,128)S(1)} collective-permute-done((f32[88,128]{1,0:T(8,128)S(1)}, f32[88,128]{1,0:T(8,128)S(1)}, u32[]{:S(2)}, u32[]{:S(2)}) %collective-permute-start.9) | collective-permute-done | bytes 45088 | tf_op jit(solution)/shard_map/ppermute | solution.py:563
  24.4 0.6 %collective-permute-done.8 = f32[88,128]{1,0:T(8,128)S(1)} collective-permute-done((f32[88,128]{1,0:T(8,128)S(1)}, f32[88,128]{1,0:T(8,128)S(1)}, u32[]{:S(2)}, u32[]{:S(2)}) %collective-permute-start.8) | collective-permute-done | bytes 45088 | tf_op jit(solution)/shard_map/ppermute | solution.py:563
  25.0 0.1 maximum_select_fusion.refs_5_
  25.1 0.1 collective-permute-start.10
  25.2 1.2 %collective-permute-done.10.refs_6_ = f32[88,128]{1,0:T(8,128)S(1)} collective-permute-done((f32[88,128]{1,0:T(8,128)S(1)}, f32[88,128]{1,0:T(8,128)S(1)}, u32[]{:S(2)}, u32[]{:S(2)}) %collective-permute-start.10) | collective-permute-done | bytes 45088 | tf_op jit(solution)/shard_map/ppermute | solution.py:586
  26.4 3.0 %step.1 = f32[1,1,5,16,1024]{4,3,2,1,0:T(8,128)} custom-call(f32[2400,128]{1,0:T(8,128)S(1)} %get-tuple-element.25.refs_0_, f32[480,128]{1,0:T(8,128)S(1)} %get-tuple-element.26.refs_1_, f32[1600,128]{1,0:T(8,128)S(1)} %get-tuple-element.27.refs_2_, f32[1440,128]{1,0:T(8,128)S(1)} %get-tuple-element.28.refs_3_, ...), custom_call_target="tpu_custom_call" | custom-call | tf_op jit(solution)/shard_map/step/pallas_call | solution.py:593
  (6 shorter events, 0.0 us)
Async XLA Ops:
  1.2 7.4 %collective-permute-start.2 = (f32[48,128]{1,0:T(8,128)S(1)}, f32[48,128]{1,0:T(8,128)S(1)}, u32[]{:S(2)}, u32[]{:S(2)}) collective-permute-start(f32[48,128]{1,0:T(8,128)S(1)} %get-tuple-element.23), channel_id=1, source_target_pairs={{0,8},{8,0},{16,24},{24,16},{1,9},{9,1},{17,25},{25,17},{2,10},{10... | collective-permute-start | bytes 73736 | tf_op jit(solution)/shard_map/ppermute | solution.py:526
  4.3 5.1 %collective-permute-start.3 = (f32[48,128]{1,0:T(8,128)S(1)}, f32[48,128]{1,0:T(8,128)S(1)}, u32[]{:S(2)}, u32[]{:S(2)}) collective-permute-start(f32[48,128]{1,0:T(8,128)S(1)} %get-tuple-element.23), channel_id=1, source_target_pairs={{0,16},{8,24},{16,0},{24,8},{1,17},{9,25},{17,1},{25,9},{2,18},{10... | collective-permute-start | bytes 73736 | tf_op jit(solution)/shard_map/ppermute | solution.py:526
  6.9 5.6 %collective-permute-start.4 = (f32[48,128]{1,0:T(8,128)S(1)}, f32[48,128]{1,0:T(8,128)S(1)}, u32[]{:S(2)}, u32[]{:S(2)}) collective-permute-start(f32[48,128]{1,0:T(8,128)S(1)} %get-tuple-element.23), channel_id=1, source_target_pairs={{0,24},{8,16},{16,8},{24,0},{1,25},{9,17},{17,9},{25,1},{2,26},{10... | collective-permute-start | bytes 73736 | tf_op jit(solution)/shard_map/ppermute | solution.py:526
  6.9 6.4 %collective-permute-start.1 = (f32[1,1,5,8,1024]{4,3,2,1,0:T(8,128)S(1)}, f32[1,1,5,8,1024]{4,3,2,1,0:T(8,128)S(1)}, u32[]{:S(2)}, u32[]{:S(2)}) collective-permute-start(f32[1,1,5,8,1024]{4,3,2,1,0:T(8,128)S(1)} %get-tuple-element.21.refs_0_), channel_id=1, source_target_pairs={{0,4},{2,6},{4,0},{6,2},{1,5},{3,7},{5,1},{7,3},{8,12},{10,14},{12... | collective-permute-start | bytes 491528 | tf_op jit(solution)/shard_map/ppermute | solution.py:553
  8.7 12.8 %collective-permute-start = (f32[1,1,5,8,1024]{4,3,2,1,0:T(8,128)S(1)}, f32[1,1,5,8,1024]{4,3,2,1,0:T(8,128)S(1)}, u32[]{:S(2)}, u32[]{:S(2)}) collective-permute-start(f32[1,1,5,8,1024]{4,3,2,1,0:T(8,128)S(1)} %get-tuple-element.21.refs_0_), channel_id=1, source_target_pairs={{0,2},{2,0},{4,6},{6,4},{1,3},{3,1},{5,7},{7,5},{8,10},{10,8},{12,... | collective-permute-start | bytes 491528 | tf_op jit(solution)/shard_map/ppermute | solution.py:553
  13.4 8.1 %collective-permute-start.5 = (f32[1,1,5,8,1024]{4,3,2,1,0:T(8,128)S(1)}, f32[1,1,5,8,1024]{4,3,2,1,0:T(8,128)S(1)}, u32[]{:S(2)}, u32[]{:S(2)}) collective-permute-start(f32[1,1,5,8,1024]{4,3,2,1,0:T(8,128)S(1)} %collective-permute-done.1.refs_2_), channel_id=1, source_target_pairs={{0,2},{2,0},{4,6},{6,4},{1,3},{3,1},{5,7},{7,5},{8,10},{10,8},{12,... | collective-permute-start | bytes 491528 | tf_op jit(solution)/shard_map/ppermute | solution.py:553
  13.5 3.7 %collective-permute-start.6 = (s32[8,128]{1,0:T(8,128)S(1)}, s32[8,128]{1,0:T(8,128)S(1)}, u32[]{:S(2)}, u32[]{:S(2)}) collective-permute-start(s32[8,128]{1,0:T(8,128)S(1)} %get-tuple-element.29), channel_id=1, source_target_pairs={{0,1},{1,0},{2,3},{3,2},{4,5},{5,4},{6,7},{7,6},{8,9},{9,8},{10,11... | collective-permute-start | bytes 12296 | tf_op jit(solution)/shard_map/ppermute | solution.py:528
  17.9 4.7 %collective-permute-start.7 = (f32[88,128]{1,0:T(8,128)S(1)}, f32[88,128]{1,0:T(8,128)S(1)}, u32[]{:S(2)}, u32[]{:S(2)}) collective-permute-start(f32[88,128]{1,0:T(8,128)S(1)} %other_strips.1), channel_id=1, source_target_pairs={{0,1},{1,0},{2,3},{3,2},{4,5},{5,4},{6,7},{7,6},{8,9},{9,8},{10,11... | collective-permute-start | bytes 135176 | tf_op jit(solution)/shard_map/ppermute | solution.py:563
  19.5 4.9 %collective-permute-start.9 = (f32[88,128]{1,0:T(8,128)S(1)}, f32[88,128]{1,0:T(8,128)S(1)}, u32[]{:S(2)}, u32[]{:S(2)}) collective-permute-start(f32[88,128]{1,0:T(8,128)S(1)} %other_strips.1), channel_id=1, source_target_pairs={{0,5},{1,4},{2,7},{3,6},{4,1},{5,0},{6,3},{7,2},{8,13},{9,12},{10,... | collective-permute-start | bytes 135176 | tf_op jit(solution)/shard_map/ppermute | solution.py:563
  21.0 4.0 %collective-permute-start.8 = (f32[88,128]{1,0:T(8,128)S(1)}, f32[88,128]{1,0:T(8,128)S(1)}, u32[]{:S(2)}, u32[]{:S(2)}) collective-permute-start(f32[88,128]{1,0:T(8,128)S(1)} %own_strips.1), channel_id=1, source_target_pairs={{0,4},{1,5},{2,6},{3,7},{4,0},{5,1},{6,2},{7,3},{8,12},{9,13},{10,... | collective-permute-start | bytes 135176 | tf_op jit(solution)/shard_map/ppermute | solution.py:563
  25.1 1.3 %collective-permute-start.10 = (f32[88,128]{1,0:T(8,128)S(1)}, f32[88,128]{1,0:T(8,128)S(1)}, u32[]{:S(2)}, u32[]{:S(2)}) collective-permute-start(f32[88,128]{1,0:T(8,128)S(1)} %maximum_select_fusion.refs_5_), channel_id=1, source_target_pairs={{0,2},{2,0},{4,6},{6,4},{1,3},{3,1},{5,7},{7,5},{8,10},{10,8},{12,... | collective-permute-start | bytes 135176 | tf_op jit(solution)/shard_map/ppermute | solution.py:586

commit v8 on v6

--- a/solution.py
+++ b/solution.py
@@ -229,13 +229,13 @@
     for g in range(sets):
 
         def cells(r, carry):
-            for half in range(2):
+            for part in range(BLOCKS):
                 for i in range(BLOCKS):
-                    at = spot(2 * r + half, SUB * i)
+                    at = spot(BLOCKS * r + part, SUB * i)
                     fill(g, lambda b, at=at: pl.ds(pl.multiple_of(b + at, SUB), SUB), (0, 1))
             return carry
 
-        lax.fori_loop(0, DEEP // 2, cells, 0)
+        lax.fori_loop(0, DEEP // BLOCKS, cells, 0)
         for r in (-1, DEEP):
             for i in range(BLOCKS):
                 fill(g, lambda b, at=spot(r, SUB * i): pl.ds(b + at, SUB), (1,))
@@ -255,8 +255,8 @@
 
 def fill_x_faces(u_ref, aux_ref, dx_ref, g, base):
     def across(r, carry):
-        for half in range(2):
-            row = 2 * r + half
+        for part in range(BLOCKS):
+            row = BLOCKS * r + part
             for i in range(BLOCKS + 1):
                 at = pl.multiple_of(spot(row, SUB * i), SUB)
                 low = load_cells(u_ref, aux_ref, g, 0, at_row(at - 1))
@@ -266,7 +266,7 @@
                     dx_ref[pl.ds(to, SUB), :] = faces[f]
         return carry
 
-    lax.fori_loop(0, DEEP // 2, across, 0)
+    lax.fori_loop(0, DEEP // BLOCKS, across, 0)
 
 
 def x_change(dx_ref, base, f, row, i):
@@ -414,7 +414,7 @@
                     to = ((g * FIELDS + f) * 8 + kept) * SUB
                     border_ref[to : to + SUB, :] = jnp.where(lacking, faces[f], dy_ref[fine : fine + SUB, :])
 
-        def update(f, carry):
+        for f in range(FIELDS):
             for i in range(BLOCKS):
                 for r in range(DEEP):
                     faces = []
@@ -428,9 +428,6 @@
                     change = x_change(next_dx, g * size, f, r, i) + (faces[0] - faces[1])
                     at = pl.ds(pl.multiple_of((g * FIELDS + f) * PLANE + spot(r, SUB * i), SUB), SUB)
                     next_u[at, :] = u_ref[at, :] + time_step * change
-            return carry
-
-        lax.fori_loop(0, FIELDS, update, 0)
 
     fill_ghosts(next_u, lanes_ref, coarse_ref, sets)
     fill_halves(next_u, next_aux, sets)
@@ -552,7 +549,7 @@
     raws = to_group(raw, strips[0])
 
     shares = [strips[0]]
-    for k in range(1, n_gz * group):
+    for k in reversed(range(1, n_gz * group)):
         if k // n_gz % 2 == 0:
             perm = [(i, i ^ k) for i in range(n_gz * group)]
             shares.append(lax.ppermute(strips[k % n_gz], ("gy", "gz"), perm))

time: 26.2 us -> 25 us (0.954)
  waiting for transfers between devices: 6.81 us -> 5.89 us
    ppermute x3, waiting for transfers between devices: 3.28 us -> 2.36 us  [per_device(): shares.append(lax.ppermute(strips[k % n_gz], ('gy', 'gz'), perm))]
  transfers between devices with their start and end apart: 11 -> 11, of which waited for: 4 -> 4; matrix products, arithmetic and copies ran while one was open for 0% -> 0% of each run, Pallas kernels for 8% -> 9%
where the time goes in v8:
time: 25 us; the launch traced here: 24.9 us
  starting transfers between devices  12.7 us (51%)
  Pallas kernels  6.16 us (25%)
  waiting for transfers between devices  5.89 us (24%)
    ppermute x3, starting transfers between devices, per_device(): boxes = [payload] + [lax.ppermute(payload, 'gx', perm) for perm in perms]  5.68 us
    ppermute x3, starting transfers between devices, per_device(): shares.append(lax.ppermute(strips[k % n_gz], ('gy', 'gz'), perm))  3.55 us
    pallas_call x1, Pallas kernels, per_device(): pl.pallas_call(functools.partial(step_kernel, count, patches, slots), out...  2.78 us
    ppermute x3, waiting for transfers between devices, per_device(): shares.append(lax.ppermute(strips[k % n_gz], ('gy', 'gz'), perm))  2.36 us
    ppermute x3, waiting for transfers between devices, per_device(): boxes = [payload] + [lax.ppermute(payload, 'gx', perm) for perm in perms]  2.31 us
    ppermute x3, starting transfers between devices, to_group(): blocks[k ^ mask] = lax.ppermute(block, 'gy', perm)  1.81 us
    ppermute x1, starting transfers between devices, per_device(): lax.ppermute(cuts[k], 'gz', [(i, i ^ k) for i in range(n_gz)])  1.56 us
    pallas_call x1, Pallas kernels, per_device(): pl.pallas_call(functools.partial(pack_kernel, tiles, rows, group, count,...  1.23 us
  transfers between devices with their start and end apart: 11, of which 4 were waited for; matrix products, arithmetic and copies ran while one was open for 0% of the time, Pallas kernels for 9%

profile of v8, /device:TPU:0, one launch (start us, length us, event | category | flops | bytes accessed | tf_op | source)
XLA Modules:
  0.0 24.9 jit_solution(6701830802375371940)
XLA Ops:
  0.0 1.2 %pack.1 = (f32[48,128]{1,0:T(8,128)S(1)}, f32[1,1,5,8,1024]{4,3,2,1,0:T(8,128)S(1)}, s32[104,128]{1,0:T(8,128)S(1)}, s32[8,128]{1,0:T(8,128)S(1)}, s32[8,128]{1,0:T(8,128)S(1)}) custom-call(s32[1,1,1,32]{3,2,1,0:T(1,128)} %bitcast.12, s32[1,1,4,32]{3,2,1,0:T(4,128)} %bitcast.9, s32[1,1,4,32]{3,2,1,0:T(4,128)} %bitcast.10, s32[1,1,4,32]{3,2,1,0:T(4,128)} %bitcast.11, ...), custom_call_target="tpu_custom_call" | custom-call | tf_op jit(solution)/shard_map/pack/pallas_call | solution.py:498
  1.2 3.1 %collective-permute-start.3 = (f32[48,128]{1,0:T(8,128)S(1)}, f32[48,128]{1,0:T(8,128)S(1)}, u32[]{:S(2)}, u32[]{:S(2)}) collective-permute-start(f32[48,128]{1,0:T(8,128)S(1)} %get-tuple-element.25), channel_id=1, source_target_pairs={{0,8},{8,0},{16,24},{24,16},{1,9},{9,1},{17,25},{25,17},{2,10},{10... | collective-permute-start | bytes 73736 | tf_op jit(solution)/shard_map/ppermute | solution.py:523
  4.3 2.6 %collective-permute-start.4 = (f32[48,128]{1,0:T(8,128)S(1)}, f32[48,128]{1,0:T(8,128)S(1)}, u32[]{:S(2)}, u32[]{:S(2)}) collective-permute-start(f32[48,128]{1,0:T(8,128)S(1)} %get-tuple-element.25), channel_id=1, source_target_pairs={{0,16},{8,24},{16,0},{24,8},{1,17},{9,25},{17,1},{25,9},{2,18},{10... | collective-permute-start | bytes 73736 | tf_op jit(solution)/shard_map/ppermute | solution.py:523
  6.9 0.0 collective-permute-start.5
  6.9 1.7 %collective-permute-start.1 = (f32[1,1,5,8,1024]{4,3,2,1,0:T(8,128)S(1)}, f32[1,1,5,8,1024]{4,3,2,1,0:T(8,128)S(1)}, u32[]{:S(2)}, u32[]{:S(2)}) collective-permute-start(f32[1,1,5,8,1024]{4,3,2,1,0:T(8,128)S(1)} %get-tuple-element.22.refs_0_), channel_id=1, source_target_pairs={{0,4},{2,6},{4,0},{6,2},{1,5},{3,7},{5,1},{7,3},{8,12},{10,14},{12... | collective-permute-start | bytes 491528 | tf_op jit(solution)/shard_map/ppermute | solution.py:545
  8.7 0.0 collective-permute-start
  8.7 0.0 collective-permute-done.3
  8.7 1.6 %collective-permute-start.2 = (s32[8,128]{1,0:T(8,128)S(1)}, s32[8,128]{1,0:T(8,128)S(1)}, u32[]{:S(2)}, u32[]{:S(2)}) collective-permute-start(s32[8,128]{1,0:T(8,128)S(1)} %get-tuple-element.24), channel_id=1, source_target_pairs={{0,1},{1,0},{2,3},{3,2},{4,5},{5,4},{6,7},{7,6},{8,9},{9,8},{10,11... | collective-permute-start | bytes 12296 | tf_op jit(solution)/shard_map/ppermute | solution.py:525
  10.2 0.0 collective-permute-done.4
  10.2 2.3 %collective-permute-done.5 = f32[48,128]{1,0:T(8,128)S(1)} collective-permute-done((f32[48,128]{1,0:T(8,128)S(1)}, f32[48,128]{1,0:T(8,128)S(1)}, u32[]{:S(2)}, u32[]{:S(2)}) %collective-permute-start.5) | collective-permute-done | bytes 24608 | tf_op jit(solution)/shard_map/ppermute | solution.py:523
  12.5 0.0 collective-permute-done.2.refs_1_
  12.6 1.0 %strips.1 = (f32[88,128]{1,0:T(8,128)S(1)}, f32[88,128]{1,0:T(8,128)S(1)}) custom-call(s32[8,128]{1,0:T(8,128)S(1)} %get-tuple-element.23.refs_0_, s32[8,128]{1,0:T(8,128)S(1)} %collective-permute-done.2.refs_1_, f32[256,128]{1,0:T(8,128)S(1)} %broadcast_dynamic-update-slice_fusion.refs_2_), custom_call_target="tpu_custom_call" | custom-call | tf_op jit(solution)/shard_map/strips/pallas_call | solution.py:527
  13.6 0.0 collective-permute-done.1.refs_2_
  13.6 0.1 collective-permute-start.6
  13.7 1.6 %collective-permute-start.8 = (f32[88,128]{1,0:T(8,128)S(1)}, f32[88,128]{1,0:T(8,128)S(1)}, u32[]{:S(2)}, u32[]{:S(2)}) collective-permute-start(f32[88,128]{1,0:T(8,128)S(1)} %get-tuple-element.33), channel_id=1, source_target_pairs={{0,4},{1,5},{2,6},{3,7},{4,0},{5,1},{6,2},{7,3},{8,12},{9,13},{10,... | collective-permute-start | bytes 135176 | tf_op jit(solution)/shard_map/ppermute | solution.py:555
  15.3 1.4 %collective-permute-start.7 = (f32[88,128]{1,0:T(8,128)S(1)}, f32[88,128]{1,0:T(8,128)S(1)}, u32[]{:S(2)}, u32[]{:S(2)}) collective-permute-start(f32[88,128]{1,0:T(8,128)S(1)} %get-tuple-element.32), channel_id=1, source_target_pairs={{0,5},{1,4},{2,7},{3,6},{4,1},{5,0},{6,3},{7,2},{8,13},{9,12},{10,... | collective-permute-start | bytes 135176 | tf_op jit(solution)/shard_map/ppermute | solution.py:555
  16.7 0.5 %collective-permute-start.9 = (f32[88,128]{1,0:T(8,128)S(1)}, f32[88,128]{1,0:T(8,128)S(1)}, u32[]{:S(2)}, u32[]{:S(2)}) collective-permute-start(f32[88,128]{1,0:T(8,128)S(1)} %get-tuple-element.32), channel_id=1, source_target_pairs={{0,1},{1,0},{2,3},{3,2},{4,5},{5,4},{6,7},{7,6},{8,9},{9,8},{10,11... | collective-permute-start | bytes 135176 | tf_op jit(solution)/shard_map/ppermute | solution.py:555
  17.2 0.0 collective-permute-done.refs_1_
  17.2 0.0 collective-permute-done.6.refs_3_
  17.2 1.1 %prepare.1 = (f32[2400,128]{1,0:T(8,128)S(1)}, f32[480,128]{1,0:T(8,128)S(1)}, f32[1600,128]{1,0:T(8,128)S(1)}, f32[1440,128]{1,0:T(8,128)S(1)}) custom-call(s32[104,128]{1,0:T(8,128)S(1)} %get-tuple-element.21.lanes_ref.refs_4_, f32[1,1,5,8,1024]{4,3,2,1,0:T(8,128)S(1)} %get-tuple-element.22.refs_0_, ...), custom_call_target="tpu_custom_call" | custom-call | flops 9830400 | bytes 1280000 | tf_op jit(solution)/shard_map/prepare/pallas_call | solution.py:563
  18.4 0.0 collective-permute-done.8
  18.4 2.0 %collective-permute-done.7 = f32[88,128]{1,0:T(8,128)S(1)} collective-permute-done((f32[88,128]{1,0:T(8,128)S(1)}, f32[88,128]{1,0:T(8,128)S(1)}, u32[]{:S(2)}, u32[]{:S(2)}) %collective-permute-start.7) | collective-permute-done | bytes 45088 | tf_op jit(solution)/shard_map/ppermute | solution.py:555
  20.4 0.4 %collective-permute-done.9 = f32[88,128]{1,0:T(8,128)S(1)} collective-permute-done((f32[88,128]{1,0:T(8,128)S(1)}, f32[88,128]{1,0:T(8,128)S(1)}, u32[]{:S(2)}, u32[]{:S(2)}) %collective-permute-start.9) | collective-permute-done | bytes 45088 | tf_op jit(solution)/shard_map/ppermute | solution.py:555
  20.7 0.1 maximum_select_fusion.refs_5_
  20.8 0.1 collective-permute-start.10
  20.9 1.2 %collective-permute-done.10.refs_6_ = f32[88,128]{1,0:T(8,128)S(1)} collective-permute-done((f32[88,128]{1,0:T(8,128)S(1)}, f32[88,128]{1,0:T(8,128)S(1)}, u32[]{:S(2)}, u32[]{:S(2)}) %collective-permute-start.10) | collective-permute-done | bytes 45088 | tf_op jit(solution)/shard_map/ppermute | solution.py:578
  22.1 2.8 %step.1 = f32[1,1,5,16,1024]{4,3,2,1,0:T(8,128)} custom-call(f32[2400,128]{1,0:T(8,128)S(1)} %get-tuple-element.28.refs_0_, f32[480,128]{1,0:T(8,128)S(1)} %get-tuple-element.29.refs_1_, f32[1600,128]{1,0:T(8,128)S(1)} %get-tuple-element.30.refs_2_, f32[1440,128]{1,0:T(8,128)S(1)} %get-tuple-element.31.refs_3_, ...), custom_call_target="tpu_custom_call" | custom-call | tf_op jit(solution)/shard_map/step/pallas_call | solution.py:585
  (6 shorter events, 0.0 us)
Async XLA Ops:
  1.2 7.4 %collective-permute-start.3 = (f32[48,128]{1,0:T(8,128)S(1)}, f32[48,128]{1,0:T(8,128)S(1)}, u32[]{:S(2)}, u32[]{:S(2)}) collective-permute-start(f32[48,128]{1,0:T(8,128)S(1)} %get-tuple-element.25), channel_id=1, source_target_pairs={{0,8},{8,0},{16,24},{24,16},{1,9},{9,1},{17,25},{25,17},{2,10},{10... | collective-permute-start | bytes 73736 | tf_op jit(solution)/shard_map/ppermute | solution.py:523
  4.3 5.9 %collective-permute-start.4 = (f32[48,128]{1,0:T(8,128)S(1)}, f32[48,128]{1,0:T(8,128)S(1)}, u32[]{:S(2)}, u32[]{:S(2)}) collective-permute-start(f32[48,128]{1,0:T(8,128)S(1)} %get-tuple-element.25), channel_id=1, source_target_pairs={{0,16},{8,24},{16,0},{24,8},{1,17},{9,25},{17,1},{25,9},{2,18},{10... | collective-permute-start | bytes 73736 | tf_op jit(solution)/shard_map/ppermute | solution.py:523
  6.9 5.6 %collective-permute-start.5 = (f32[48,128]{1,0:T(8,128)S(1)}, f32[48,128]{1,0:T(8,128)S(1)}, u32[]{:S(2)}, u32[]{:S(2)}) collective-permute-start(f32[48,128]{1,0:T(8,128)S(1)} %get-tuple-element.25), channel_id=1, source_target_pairs={{0,24},{8,16},{16,8},{24,0},{1,25},{9,17},{17,9},{25,1},{2,26},{10... | collective-permute-start | bytes 73736 | tf_op jit(solution)/shard_map/ppermute | solution.py:523
  6.9 6.7 %collective-permute-start.1 = (f32[1,1,5,8,1024]{4,3,2,1,0:T(8,128)S(1)}, f32[1,1,5,8,1024]{4,3,2,1,0:T(8,128)S(1)}, u32[]{:S(2)}, u32[]{:S(2)}) collective-permute-start(f32[1,1,5,8,1024]{4,3,2,1,0:T(8,128)S(1)} %get-tuple-element.22.refs_0_), channel_id=1, source_target_pairs={{0,4},{2,6},{4,0},{6,2},{1,5},{3,7},{5,1},{7,3},{8,12},{10,14},{12... | collective-permute-start | bytes 491528 | tf_op jit(solution)/shard_map/ppermute | solution.py:545
  8.7 8.6 %collective-permute-start = (f32[1,1,5,8,1024]{4,3,2,1,0:T(8,128)S(1)}, f32[1,1,5,8,1024]{4,3,2,1,0:T(8,128)S(1)}, u32[]{:S(2)}, u32[]{:S(2)}) collective-permute-start(f32[1,1,5,8,1024]{4,3,2,1,0:T(8,128)S(1)} %get-tuple-element.22.refs_0_), channel_id=1, source_target_pairs={{0,2},{2,0},{4,6},{6,4},{1,3},{3,1},{5,7},{7,5},{8,10},{10,8},{12,... | collective-permute-start | bytes 491528 | tf_op jit(solution)/shard_map/ppermute | solution.py:545
  8.7 3.9 %collective-permute-start.2 = (s32[8,128]{1,0:T(8,128)S(1)}, s32[8,128]{1,0:T(8,128)S(1)}, u32[]{:S(2)}, u32[]{:S(2)}) collective-permute-start(s32[8,128]{1,0:T(8,128)S(1)} %get-tuple-element.24), channel_id=1, source_target_pairs={{0,1},{1,0},{2,3},{3,2},{4,5},{5,4},{6,7},{7,6},{8,9},{9,8},{10,11... | collective-permute-start | bytes 12296 | tf_op jit(solution)/shard_map/ppermute | solution.py:525
  13.6 3.6 %collective-permute-start.6 = (f32[1,1,5,8,1024]{4,3,2,1,0:T(8,128)S(1)}, f32[1,1,5,8,1024]{4,3,2,1,0:T(8,128)S(1)}, u32[]{:S(2)}, u32[]{:S(2)}) collective-permute-start(f32[1,1,5,8,1024]{4,3,2,1,0:T(8,128)S(1)} %collective-permute-done.1.refs_2_), channel_id=1, source_target_pairs={{0,2},{2,0},{4,6},{6,4},{1,3},{3,1},{5,7},{7,5},{8,10},{10,8},{12,... | collective-permute-start | bytes 491528 | tf_op jit(solution)/shard_map/ppermute | solution.py:545
  13.7 4.7 %collective-permute-start.8 = (f32[88,128]{1,0:T(8,128)S(1)}, f32[88,128]{1,0:T(8,128)S(1)}, u32[]{:S(2)}, u32[]{:S(2)}) collective-permute-start(f32[88,128]{1,0:T(8,128)S(1)} %get-tuple-element.33), channel_id=1, source_target_pairs={{0,4},{1,5},{2,6},{3,7},{4,0},{5,1},{6,2},{7,3},{8,12},{9,13},{10,... | collective-permute-start | bytes 135176 | tf_op jit(solution)/shard_map/ppermute | solution.py:555
  15.3 5.1 %collective-permute-start.7 = (f32[88,128]{1,0:T(8,128)S(1)}, f32[88,128]{1,0:T(8,128)S(1)}, u32[]{:S(2)}, u32[]{:S(2)}) collective-permute-start(f32[88,128]{1,0:T(8,128)S(1)} %get-tuple-element.32), channel_id=1, source_target_pairs={{0,5},{1,4},{2,7},{3,6},{4,1},{5,0},{6,3},{7,2},{8,13},{9,12},{10,... | collective-permute-start | bytes 135176 | tf_op jit(solution)/shard_map/ppermute | solution.py:555
  16.7 4.0 %collective-permute-start.9 = (f32[88,128]{1,0:T(8,128)S(1)}, f32[88,128]{1,0:T(8,128)S(1)}, u32[]{:S(2)}, u32[]{:S(2)}) collective-permute-start(f32[88,128]{1,0:T(8,128)S(1)} %get-tuple-element.32), channel_id=1, source_target_pairs={{0,1},{1,0},{2,3},{3,2},{4,5},{5,4},{6,7},{7,6},{8,9},{9,8},{10,11... | collective-permute-start | bytes 135176 | tf_op jit(solution)/shard_map/ppermute | solution.py:555
  20.8 1.3 %collective-permute-start.10 = (f32[88,128]{1,0:T(8,128)S(1)}, f32[88,128]{1,0:T(8,128)S(1)}, u32[]{:S(2)}, u32[]{:S(2)}) collective-permute-start(f32[88,128]{1,0:T(8,128)S(1)} %maximum_select_fusion.refs_5_), channel_id=1, source_target_pairs={{0,2},{2,0},{4,6},{6,4},{1,3},{3,1},{5,7},{7,5},{8,10},{10,8},{12,... | collective-permute-start | bytes 135176 | tf_op jit(solution)/shard_map/ppermute | solution.py:578

commit v9 on v8

--- a/solution.py
+++ b/solution.py
@@ -126,9 +126,10 @@
 
 def place_of(me, other, n):
     if power_of_two(n):
-        return me ^ other
-    behind = me - other
-    return jnp.where(behind < 0, behind + n, behind)
+        apart = me ^ other
+        return jnp.where(apart == 0, 0, n - apart)
+    ahead = other - me
+    return jnp.where(ahead < 0, ahead + n, ahead)
 
 
 def pack_kernel(tiles, rows, group, count, patches, slots, mesh_sizes, *refs):
@@ -520,9 +521,11 @@
         perms = [[(i, i ^ k) for i in range(n_gx)] for k in range(1, n_gx)]
     else:
         perms = [[(i, (i + k) % n_gx) for i in range(n_gx)] for k in range(1, n_gx)]
-    boxes = [payload] + [lax.ppermute(payload, "gx", perm) for perm in perms]
+    boxes = [payload] + [lax.ppermute(payload, "gx", perm) for perm in perms[::-1]]
+    cuts = cuts[:1] + [lax.ppermute(cuts[k], "gz", [(i, i ^ k) for i in range(n_gz)]) for k in range(1, n_gz)]
+    *boxes, last = lax.optimization_barrier(boxes + cuts[1:2])
+    cuts = cuts[:1] + [last] + cuts[2:]
     boxes = jnp.concatenate(boxes + [jnp.zeros((SUB * tiles, LANE), f32)], axis=0)
-    cuts = cuts[:1] + [lax.ppermute(cuts[k], "gz", [(i, i ^ k) for i in range(n_gz)]) for k in range(1, n_gz)]
 
     strips = pl.pallas_call(
         functools.partial(strip_kernel, n_gx, n_gz, rows, tiles, patches),

time: 25 us -> 24.9 us (level)
    ppermute x3, waiting for transfers between devices: 2.31 us -> 0.47 us  [per_device(): lax.ppermute(payload, 'gx', perm)]
    ppermute x3, waiting for transfers between devices: 0.01 us -> 1.8 us  [to_group(): blocks[k ^ mask] = lax.ppermute(block, 'gy', perm)]
    ppermute x1, waiting for transfers between devices: 0.01 us -> 0.45 us  [per_device(): lax.ppermute(cuts[k], 'gz', [(i, i ^ k) for i in range(n_gz)])]
    ppermute x3, waiting for transfers between devices: 2.36 us -> 2.06 us  [per_device(): shares.append(lax.ppermute(strips[k % n_gz], ('gy', 'gz'), perm))]
    ppermute x3, starting transfers between devices: 1.81 us -> 1.52 us  [to_group(): blocks[k ^ mask] = lax.ppermute(block, 'gy', perm)]
  transfers between devices with their start and end apart: 11 -> 11, of which waited for: 4 -> 5; matrix products, arithmetic and copies ran while one was open for 0% -> 0% of each run, Pallas kernels for 9% -> 9%
where the time goes in v9:
time: 24.9 us; the launch traced here: 24.8 us
  starting transfers between devices  12.5 us (50%)
  Pallas kernels  6.16 us (25%)
  waiting for transfers between devices  5.99 us (24%)
    ppermute x3, starting transfers between devices, per_device(): lax.ppermute(payload, 'gx', perm)  5.76 us
    ppermute x3, starting transfers between devices, per_device(): shares.append(lax.ppermute(strips[k % n_gz], ('gy', 'gz'), perm))  3.49 us
    pallas_call x1, Pallas kernels, per_device(): pl.pallas_call(functools.partial(step_kernel, count, patches, slots), out...  2.78 us
    ppermute x3, waiting for transfers between devices, per_device(): shares.append(lax.ppermute(strips[k % n_gz], ('gy', 'gz'), perm))  2.06 us
    ppermute x3, waiting for transfers between devices, to_group(): blocks[k ^ mask] = lax.ppermute(block, 'gy', perm)  1.8 us
    ppermute x1, starting transfers between devices, per_device(): lax.ppermute(cuts[k], 'gz', [(i, i ^ k) for i in range(n_gz)])  1.63 us
    ppermute x3, starting transfers between devices, to_group(): blocks[k ^ mask] = lax.ppermute(block, 'gy', perm)  1.52 us
    pallas_call x1, Pallas kernels, per_device(): pl.pallas_call(functools.partial(pack_kernel, tiles, rows, group, count,...  1.23 us
  transfers between devices with their start and end apart: 11, of which 5 were waited for; matrix products, arithmetic and copies ran while one was open for 0% of the time, Pallas kernels for 9%

profile of v9, /device:TPU:0, one launch (start us, length us, event | category | flops | bytes accessed | tf_op | source)
XLA Modules:
  0.0 24.8 jit_solution(7385102799933986223)
XLA Ops:
  0.0 1.2 %pack.1 = (f32[48,128]{1,0:T(8,128)S(1)}, f32[1,1,5,8,1024]{4,3,2,1,0:T(8,128)S(1)}, s32[104,128]{1,0:T(8,128)S(1)}, s32[8,128]{1,0:T(8,128)S(1)}, s32[8,128]{1,0:T(8,128)S(1)}) custom-call(s32[1,1,1,32]{3,2,1,0:T(1,128)} %bitcast.12, s32[1,1,4,32]{3,2,1,0:T(4,128)} %bitcast.9, s32[1,1,4,32]{3,2,1,0:T(4,128)} %bitcast.10, s32[1,1,4,32]{3,2,1,0:T(4,128)} %bitcast.11, ...), custom_call_target="tpu_custom_call" | custom-call | tf_op jit(solution)/shard_map/pack/pallas_call | solution.py:499
  1.2 5.1 %collective-permute-start.2 = (f32[48,128]{1,0:T(8,128)S(1)}, f32[48,128]{1,0:T(8,128)S(1)}, u32[]{:S(2)}, u32[]{:S(2)}) collective-permute-start(f32[48,128]{1,0:T(8,128)S(1)} %get-tuple-element.32), channel_id=1, source_target_pairs={{0,24},{8,16},{16,8},{24,0},{1,25},{9,17},{17,9},{25,1},{2,26},{10... | collective-permute-start | bytes 73736 | tf_op jit(solution)/shard_map/ppermute | solution.py:524
  6.4 0.0 collective-permute-start.3
  6.4 0.6 %collective-permute-start.4 = (f32[48,128]{1,0:T(8,128)S(1)}, f32[48,128]{1,0:T(8,128)S(1)}, u32[]{:S(2)}, u32[]{:S(2)}) collective-permute-start(f32[48,128]{1,0:T(8,128)S(1)} %get-tuple-element.32), channel_id=1, source_target_pairs={{0,8},{8,0},{16,24},{24,16},{1,9},{9,1},{17,25},{25,17},{2,10},{10... | collective-permute-start | bytes 73736 | tf_op jit(solution)/shard_map/ppermute | solution.py:524
  7.0 1.6 %collective-permute-start.5 = (s32[8,128]{1,0:T(8,128)S(1)}, s32[8,128]{1,0:T(8,128)S(1)}, u32[]{:S(2)}, u32[]{:S(2)}) collective-permute-start(s32[8,128]{1,0:T(8,128)S(1)} %get-tuple-element.30), channel_id=1, source_target_pairs={{0,1},{1,0},{2,3},{3,2},{4,5},{5,4},{6,7},{7,6},{8,9},{9,8},{10,11... | collective-permute-start | bytes 12296 | tf_op jit(solution)/shard_map/ppermute | solution.py:525
  8.6 1.5 %collective-permute-start.1 = (f32[1,1,5,8,1024]{4,3,2,1,0:T(8,128)S(1)}, f32[1,1,5,8,1024]{4,3,2,1,0:T(8,128)S(1)}, u32[]{:S(2)}, u32[]{:S(2)}) collective-permute-start(f32[1,1,5,8,1024]{4,3,2,1,0:T(8,128)S(1)} %get-tuple-element.27.refs_0_), channel_id=1, source_target_pairs={{0,4},{2,6},{4,0},{6,2},{1,5},{3,7},{5,1},{7,3},{8,12},{10,14},{12... | collective-permute-start | bytes 491528 | tf_op jit(solution)/shard_map/ppermute | solution.py:548
  10.2 0.5 %collective-permute-done.5.refs_1_ = s32[8,128]{1,0:T(8,128)S(1)} collective-permute-done((s32[8,128]{1,0:T(8,128)S(1)}, s32[8,128]{1,0:T(8,128)S(1)}, u32[]{:S(2)}, u32[]{:S(2)}) %collective-permute-start.5) | collective-permute-done | bytes 4128 | tf_op jit(solution)/shard_map/ppermute | solution.py:525
  10.6 0.0 collective-permute-start
  10.6 0.0 collective-permute-done.2
  10.6 0.5 %collective-permute-done.3 = f32[48,128]{1,0:T(8,128)S(1)} collective-permute-done((f32[48,128]{1,0:T(8,128)S(1)}, f32[48,128]{1,0:T(8,128)S(1)}, u32[]{:S(2)}, u32[]{:S(2)}) %collective-permute-start.3) | collective-permute-done | bytes 24608 | tf_op jit(solution)/shard_map/ppermute | solution.py:524
  11.1 0.0 collective-permute-done.4
  11.1 1.0 %strips.1 = (f32[88,128]{1,0:T(8,128)S(1)}, f32[88,128]{1,0:T(8,128)S(1)}) custom-call(s32[8,128]{1,0:T(8,128)S(1)} %get-tuple-element.28.refs_0_, s32[8,128]{1,0:T(8,128)S(1)} %collective-permute-done.5.refs_1_, f32[256,128]{1,0:T(8,128)S(1)} %broadcast_dynamic-update-slice_fusion.refs_2_), custom_call_target="tpu_custom_call" | custom-call | tf_op jit(solution)/shard_map/strips/pallas_call | solution.py:530
  12.2 1.8 %collective-permute-done.1.refs_2_ = f32[1,1,5,8,1024]{4,3,2,1,0:T(8,128)S(1)} collective-permute-done((f32[1,1,5,8,1024]{4,3,2,1,0:T(8,128)S(1)}, f32[1,1,5,8,1024]{4,3,2,1,0:T(8,128)S(1)}, u32[]{:S(2)}, u32[]{:S(2)}) %collective-permute-start.1) | collective-permute-done | bytes 163872 | tf_op jit(solution)/shard_map/ppermute | solution.py:548
  13.9 0.0 collective-permute-start.6
  14.0 1.5 %collective-permute-start.8 = (f32[88,128]{1,0:T(8,128)S(1)}, f32[88,128]{1,0:T(8,128)S(1)}, u32[]{:S(2)}, u32[]{:S(2)}) collective-permute-start(f32[88,128]{1,0:T(8,128)S(1)} %get-tuple-element.43), channel_id=1, source_target_pairs={{0,4},{1,5},{2,6},{3,7},{4,0},{5,1},{6,2},{7,3},{8,12},{9,13},{10,... | collective-permute-start | bytes 135176 | tf_op jit(solution)/shard_map/ppermute | solution.py:558
  15.5 0.3 %collective-permute-start.7 = (f32[88,128]{1,0:T(8,128)S(1)}, f32[88,128]{1,0:T(8,128)S(1)}, u32[]{:S(2)}, u32[]{:S(2)}) collective-permute-start(f32[88,128]{1,0:T(8,128)S(1)} %get-tuple-element.42), channel_id=1, source_target_pairs={{0,5},{1,4},{2,7},{3,6},{4,1},{5,0},{6,3},{7,2},{8,13},{9,12},{10,... | collective-permute-start | bytes 135176 | tf_op jit(solution)/shard_map/ppermute | solution.py:558
  15.8 1.6 %collective-permute-start.9 = (f32[88,128]{1,0:T(8,128)S(1)}, f32[88,128]{1,0:T(8,128)S(1)}, u32[]{:S(2)}, u32[]{:S(2)}) collective-permute-start(f32[88,128]{1,0:T(8,128)S(1)} %get-tuple-element.42), channel_id=1, source_target_pairs={{0,1},{1,0},{2,3},{3,2},{4,5},{5,4},{6,7},{7,6},{8,9},{9,8},{10,11... | collective-permute-start | bytes 135176 | tf_op jit(solution)/shard_map/ppermute | solution.py:558
  17.4 0.0 collective-permute-done.refs_1_
  17.5 0.0 collective-permute-done.6.refs_3_
  17.5 1.1 %prepare.1 = (f32[2400,128]{1,0:T(8,128)S(1)}, f32[480,128]{1,0:T(8,128)S(1)}, f32[1600,128]{1,0:T(8,128)S(1)}, f32[1440,128]{1,0:T(8,128)S(1)}) custom-call(s32[104,128]{1,0:T(8,128)S(1)} %get-tuple-element.26.lanes_ref.refs_4_, f32[1,1,5,8,1024]{4,3,2,1,0:T(8,128)S(1)} %get-tuple-element.27.refs_0_, ...), custom_call_target="tpu_custom_call" | custom-call | flops 9830400 | bytes 1280000 | tf_op jit(solution)/shard_map/prepare/pallas_call | solution.py:566
  18.6 2.1 %collective-permute-done.7 = f32[88,128]{1,0:T(8,128)S(1)} collective-permute-done((f32[88,128]{1,0:T(8,128)S(1)}, f32[88,128]{1,0:T(8,128)S(1)}, u32[]{:S(2)}, u32[]{:S(2)}) %collective-permute-start.7) | collective-permute-done | bytes 45088 | tf_op jit(solution)/shard_map/ppermute | solution.py:558
  20.6 0.0 collective-permute-done.8
  20.6 0.0 collective-permute-done.9
  20.6 0.1 maximum_select_fusion.refs_5_
  20.7 0.1 collective-permute-start.10
  20.8 1.2 %collective-permute-done.10.refs_6_ = f32[88,128]{1,0:T(8,128)S(1)} collective-permute-done((f32[88,128]{1,0:T(8,128)S(1)}, f32[88,128]{1,0:T(8,128)S(1)}, u32[]{:S(2)}, u32[]{:S(2)}) %collective-permute-start.10) | collective-permute-done | bytes 45088 | tf_op jit(solution)/shard_map/ppermute | solution.py:581
  22.0 2.8 %step.1 = f32[1,1,5,16,1024]{4,3,2,1,0:T(8,128)} custom-call(f32[2400,128]{1,0:T(8,128)S(1)} %get-tuple-element.38.refs_0_, f32[480,128]{1,0:T(8,128)S(1)} %get-tuple-element.39.refs_1_, f32[1600,128]{1,0:T(8,128)S(1)} %get-tuple-element.40.refs_2_, f32[1440,128]{1,0:T(8,128)S(1)} %get-tuple-element.41.refs_3_, ...), custom_call_target="tpu_custom_call" | custom-call | tf_op jit(solution)/shard_map/step/pallas_call | solution.py:588
  (6 shorter events, 0.0 us)
Async XLA Ops:
  1.2 9.4 %collective-permute-start.2 = (f32[48,128]{1,0:T(8,128)S(1)}, f32[48,128]{1,0:T(8,128)S(1)}, u32[]{:S(2)}, u32[]{:S(2)}) collective-permute-start(f32[48,128]{1,0:T(8,128)S(1)} %get-tuple-element.32), channel_id=1, source_target_pairs={{0,24},{8,16},{16,8},{24,0},{1,25},{9,17},{17,9},{25,1},{2,26},{10... | collective-permute-start | bytes 73736 | tf_op jit(solution)/shard_map/ppermute | solution.py:524
  6.4 4.7 %collective-permute-start.3 = (f32[48,128]{1,0:T(8,128)S(1)}, f32[48,128]{1,0:T(8,128)S(1)}, u32[]{:S(2)}, u32[]{:S(2)}) collective-permute-start(f32[48,128]{1,0:T(8,128)S(1)} %get-tuple-element.32), channel_id=1, source_target_pairs={{0,16},{8,24},{16,0},{24,8},{1,17},{9,25},{17,1},{25,9},{2,18},{10... | collective-permute-start | bytes 73736 | tf_op jit(solution)/shard_map/ppermute | solution.py:524
  6.4 4.7 %collective-permute-start.4 = (f32[48,128]{1,0:T(8,128)S(1)}, f32[48,128]{1,0:T(8,128)S(1)}, u32[]{:S(2)}, u32[]{:S(2)}) collective-permute-start(f32[48,128]{1,0:T(8,128)S(1)} %get-tuple-element.32), channel_id=1, source_target_pairs={{0,8},{8,0},{16,24},{24,16},{1,9},{9,1},{17,25},{25,17},{2,10},{10... | collective-permute-start | bytes 73736 | tf_op jit(solution)/shard_map/ppermute | solution.py:524
  7.0 3.6 %collective-permute-start.5 = (s32[8,128]{1,0:T(8,128)S(1)}, s32[8,128]{1,0:T(8,128)S(1)}, u32[]{:S(2)}, u32[]{:S(2)}) collective-permute-start(s32[8,128]{1,0:T(8,128)S(1)} %get-tuple-element.30), channel_id=1, source_target_pairs={{0,1},{1,0},{2,3},{3,2},{4,5},{5,4},{6,7},{7,6},{8,9},{9,8},{10,11... | collective-permute-start | bytes 12296 | tf_op jit(solution)/shard_map/ppermute | solution.py:525
  8.6 5.3 %collective-permute-start.1 = (f32[1,1,5,8,1024]{4,3,2,1,0:T(8,128)S(1)}, f32[1,1,5,8,1024]{4,3,2,1,0:T(8,128)S(1)}, u32[]{:S(2)}, u32[]{:S(2)}) collective-permute-start(f32[1,1,5,8,1024]{4,3,2,1,0:T(8,128)S(1)} %get-tuple-element.27.refs_0_), channel_id=1, source_target_pairs={{0,4},{2,6},{4,0},{6,2},{1,5},{3,7},{5,1},{7,3},{8,12},{10,14},{12... | collective-permute-start | bytes 491528 | tf_op jit(solution)/shard_map/ppermute | solution.py:548
  10.6 6.8 %collective-permute-start = (f32[1,1,5,8,1024]{4,3,2,1,0:T(8,128)S(1)}, f32[1,1,5,8,1024]{4,3,2,1,0:T(8,128)S(1)}, u32[]{:S(2)}, u32[]{:S(2)}) collective-permute-start(f32[1,1,5,8,1024]{4,3,2,1,0:T(8,128)S(1)} %get-tuple-element.27.refs_0_), channel_id=1, source_target_pairs={{0,2},{2,0},{4,6},{6,4},{1,3},{3,1},{5,7},{7,5},{8,10},{10,8},{12,... | collective-permute-start | bytes 491528 | tf_op jit(solution)/shard_map/ppermute | solution.py:548
  13.9 3.5 %collective-permute-start.6 = (f32[1,1,5,8,1024]{4,3,2,1,0:T(8,128)S(1)}, f32[1,1,5,8,1024]{4,3,2,1,0:T(8,128)S(1)}, u32[]{:S(2)}, u32[]{:S(2)}) collective-permute-start(f32[1,1,5,8,1024]{4,3,2,1,0:T(8,128)S(1)} %collective-permute-done.1.refs_2_), channel_id=1, source_target_pairs={{0,2},{2,0},{4,6},{6,4},{1,3},{3,1},{5,7},{7,5},{8,10},{10,8},{12,... | collective-permute-start | bytes 491528 | tf_op jit(solution)/shard_map/ppermute | solution.py:548
  14.0 6.7 %collective-permute-start.8 = (f32[88,128]{1,0:T(8,128)S(1)}, f32[88,128]{1,0:T(8,128)S(1)}, u32[]{:S(2)}, u32[]{:S(2)}) collective-permute-start(f32[88,128]{1,0:T(8,128)S(1)} %get-tuple-element.43), channel_id=1, source_target_pairs={{0,4},{1,5},{2,6},{3,7},{4,0},{5,1},{6,2},{7,3},{8,12},{9,13},{10,... | collective-permute-start | bytes 135176 | tf_op jit(solution)/shard_map/ppermute | solution.py:558
  15.5 5.2 %collective-permute-start.7 = (f32[88,128]{1,0:T(8,128)S(1)}, f32[88,128]{1,0:T(8,128)S(1)}, u32[]{:S(2)}, u32[]{:S(2)}) collective-permute-start(f32[88,128]{1,0:T(8,128)S(1)} %get-tuple-element.42), channel_id=1, source_target_pairs={{0,5},{1,4},{2,7},{3,6},{4,1},{5,0},{6,3},{7,2},{8,13},{9,12},{10,... | collective-permute-start | bytes 135176 | tf_op jit(solution)/shard_map/ppermute | solution.py:558
  15.8 4.8 %collective-permute-start.9 = (f32[88,128]{1,0:T(8,128)S(1)}, f32[88,128]{1,0:T(8,128)S(1)}, u32[]{:S(2)}, u32[]{:S(2)}) collective-permute-start(f32[88,128]{1,0:T(8,128)S(1)} %get-tuple-element.42), channel_id=1, source_target_pairs={{0,1},{1,0},{2,3},{3,2},{4,5},{5,4},{6,7},{7,6},{8,9},{9,8},{10,11... | collective-permute-start | bytes 135176 | tf_op jit(solution)/shard_map/ppermute | solution.py:558
  20.7 1.3 %collective-permute-start.10 = (f32[88,128]{1,0:T(8,128)S(1)}, f32[88,128]{1,0:T(8,128)S(1)}, u32[]{:S(2)}, u32[]{:S(2)}) collective-permute-start(f32[88,128]{1,0:T(8,128)S(1)} %maximum_select_fusion.refs_5_), channel_id=1, source_target_pairs={{0,2},{2,0},{4,6},{6,4},{1,3},{3,1},{5,7},{7,5},{8,10},{10,8},{12,... | collective-permute-start | bytes 135176 | tf_op jit(solution)/shard_map/ppermute | solution.py:581

commit v10 on v9

--- a/solution.py
+++ b/solution.py
@@ -523,7 +523,9 @@
         perms = [[(i, (i + k) % n_gx) for i in range(n_gx)] for k in range(1, n_gx)]
     boxes = [payload] + [lax.ppermute(payload, "gx", perm) for perm in perms[::-1]]
     cuts = cuts[:1] + [lax.ppermute(cuts[k], "gz", [(i, i ^ k) for i in range(n_gz)]) for k in range(1, n_gz)]
-    *boxes, last = lax.optimization_barrier(boxes + cuts[1:2])
+    far = masks_of(group)[0]
+    raw_far = lax.ppermute(raw, "gy", [(i, i ^ far) for i in range(group)])
+    raw_far, *boxes, last = lax.optimization_barrier([raw_far] + boxes + cuts[1:2])
     cuts = cuts[:1] + [last] + cuts[2:]
     boxes = jnp.concatenate(boxes + [jnp.zeros((SUB * tiles, LANE), f32)], axis=0)
 
@@ -536,20 +538,17 @@
         name="strips",
     )(*cuts, boxes)
 
-    def to_group(x, after=None):
-        blocks, have = [x] + [None] * (group - 1), [0]
-        masks = masks_of(group)
-        for mask in masks:
-            perm = [(i, i ^ mask) for i in range(group)]
-            for k in have:
-                block = blocks[k]
-                if after is not None and mask == masks[-1] and k:
-                    block, _ = lax.optimization_barrier((block, after))
-                blocks[k ^ mask] = lax.ppermute(block, "gy", perm)
-            have = have + [k ^ mask for k in have]
-        return blocks
-
-    raws = to_group(raw, strips[0])
+    raws, have = [raw] + [None] * (group - 1), [0]
+    raws[far] = raw_far
+    for mask in masks_of(group):
+        perm = [(i, i ^ mask) for i in range(group)]
+        for k in have:
+            block = raws[k]
+            if mask == 1 and k:
+                block, _ = lax.optimization_barrier((block, strips[0]))
+            if raws[k ^ mask] is None:
+                raws[k ^ mask] = lax.ppermute(block, "gy", perm)
+        have = have + [k ^ mask for k in have]
 
     shares = [strips[0]]
     for k in reversed(range(1, n_gz * group)):

time: 24.9 us -> 25.3 us (1.016)
    ppermute x3, waiting for transfers between devices: 1.8 us -> 0.01 us  [the longest x2 0.01 us: per_device(): raws[k ^ mask] = lax.ppermute(block, 'gy', perm)]
    ppermute x3, starting transfers between devices: 1.52 us -> 3.3 us  [the longest x1 3.03 us: per_device(): raw_far = lax.ppermute(raw, 'gy', [(i, i ^ far) for i in range(group)])]
    ppermute x1, waiting for transfers between devices: 0.45 us -> 2.12 us  [per_device(): lax.ppermute(cuts[k], 'gz', [(i, i ^ k) for i in range(n_gz)])]
    ppermute x3, starting transfers between devices: 5.76 us -> 4.39 us  [per_device(): lax.ppermute(payload, 'gx', perm)]
    ppermute x3, waiting for transfers between devices: 2.06 us -> 2.36 us  [per_device(): shares.append(lax.ppermute(strips[k % n_gz], ('gy', 'gz'), perm))]
where the time goes in v10:
time: 25.3 us; the launch traced here: 25.1 us
  starting transfers between devices  12.7 us (50%)
  Pallas kernels  6.16 us (24%)
  waiting for transfers between devices  6.03 us (24%)
    ppermute x3, starting transfers between devices, per_device(): lax.ppermute(payload, 'gx', perm)  4.39 us
    ppermute x3, starting transfers between devices, per_device(): shares.append(lax.ppermute(strips[k % n_gz], ('gy', 'gz'), perm))  3.49 us
    ppermute x1, starting transfers between devices, per_device(): raw_far = lax.ppermute(raw, 'gy', [(i, i ^ far) for i in range(group)])  3.03 us
    pallas_call x1, Pallas kernels, per_device(): pl.pallas_call(functools.partial(step_kernel, count, patches, slots), out...  2.78 us
    ppermute x3, waiting for transfers between devices, per_device(): shares.append(lax.ppermute(strips[k % n_gz], ('gy', 'gz'), perm))  2.36 us
    ppermute x1, waiting for transfers between devices, per_device(): lax.ppermute(cuts[k], 'gz', [(i, i ^ k) for i in range(n_gz)])  2.12 us
    ppermute x1, starting transfers between devices, per_device(): lax.ppermute(cuts[k], 'gz', [(i, i ^ k) for i in range(n_gz)])  1.49 us
    pallas_call x1, Pallas kernels, per_device(): pl.pallas_call(functools.partial(pack_kernel, tiles, rows, group, count,...  1.23 us
  transfers between devices with their start and end apart: 11, of which 5 were waited for; matrix products, arithmetic and copies ran while one was open for 0% of the time, Pallas kernels for 9%

profile of v10, /device:TPU:0, one launch (start us, length us, event | category | flops | bytes accessed | tf_op | source)
XLA Modules:
  0.0 25.1 jit_solution(37458482369273984)
XLA Ops:
  0.0 1.2 %pack.1 = (f32[48,128]{1,0:T(8,128)S(1)}, f32[1,1,5,8,1024]{4,3,2,1,0:T(8,128)S(1)}, s32[104,128]{1,0:T(8,128)S(1)}, s32[8,128]{1,0:T(8,128)S(1)}, s32[8,128]{1,0:T(8,128)S(1)}) custom-call(s32[1,1,1,32]{3,2,1,0:T(1,128)} %bitcast.12, s32[1,1,4,32]{3,2,1,0:T(4,128)} %bitcast.9, s32[1,1,4,32]{3,2,1,0:T(4,128)} %bitcast.10, s32[1,1,4,32]{3,2,1,0:T(4,128)} %bitcast.11, ...), custom_call_target="tpu_custom_call" | custom-call | tf_op jit(solution)/shard_map/pack/pallas_call | solution.py:499
  1.2 3.0 %collective-permute-start.1 = (f32[1,1,5,8,1024]{4,3,2,1,0:T(8,128)S(1)}, f32[1,1,5,8,1024]{4,3,2,1,0:T(8,128)S(1)}, u32[]{:S(2)}, u32[]{:S(2)}) collective-permute-start(f32[1,1,5,8,1024]{4,3,2,1,0:T(8,128)S(1)} %get-tuple-element.28.refs_0_), channel_id=1, source_target_pairs={{0,4},{2,6},{4,0},{6,2},{1,5},{3,7},{5,1},{7,3},{8,12},{10,14},{12... | collective-permute-start | bytes 491528 | tf_op jit(solution)/shard_map/ppermute | solution.py:527
  4.3 3.6 %collective-permute-start.2 = (f32[48,128]{1,0:T(8,128)S(1)}, f32[48,128]{1,0:T(8,128)S(1)}, u32[]{:S(2)}, u32[]{:S(2)}) collective-permute-start(f32[48,128]{1,0:T(8,128)S(1)} %get-tuple-element.34), channel_id=1, source_target_pairs={{0,24},{8,16},{16,8},{24,0},{1,25},{9,17},{17,9},{25,1},{2,26},{10... | collective-permute-start | bytes 73736 | tf_op jit(solution)/shard_map/ppermute | solution.py:524
  7.9 0.0 collective-permute-start.3
  7.9 0.8 %collective-permute-start.4 = (f32[48,128]{1,0:T(8,128)S(1)}, f32[48,128]{1,0:T(8,128)S(1)}, u32[]{:S(2)}, u32[]{:S(2)}) collective-permute-start(f32[48,128]{1,0:T(8,128)S(1)} %get-tuple-element.34), channel_id=1, source_target_pairs={{0,8},{8,0},{16,24},{24,16},{1,9},{9,1},{17,25},{25,17},{2,10},{10... | collective-permute-start | bytes 73736 | tf_op jit(solution)/shard_map/ppermute | solution.py:524
  8.7 1.5 %collective-permute-start.5 = (s32[8,128]{1,0:T(8,128)S(1)}, s32[8,128]{1,0:T(8,128)S(1)}, u32[]{:S(2)}, u32[]{:S(2)}) collective-permute-start(s32[8,128]{1,0:T(8,128)S(1)} %get-tuple-element.30), channel_id=1, source_target_pairs={{0,1},{1,0},{2,3},{3,2},{4,5},{5,4},{6,7},{7,6},{8,9},{9,8},{10,11... | collective-permute-start | bytes 12296 | tf_op jit(solution)/shard_map/ppermute | solution.py:525
  10.2 2.1 %collective-permute-done.5.refs_1_ = s32[8,128]{1,0:T(8,128)S(1)} collective-permute-done((s32[8,128]{1,0:T(8,128)S(1)}, s32[8,128]{1,0:T(8,128)S(1)}, u32[]{:S(2)}, u32[]{:S(2)}) %collective-permute-start.5) | collective-permute-done | bytes 4128 | tf_op jit(solution)/shard_map/ppermute | solution.py:525
  12.3 0.0 collective-permute-start
  12.3 0.0 collective-permute-done.2
  12.3 0.3 %collective-permute-done.3 = f32[48,128]{1,0:T(8,128)S(1)} collective-permute-done((f32[48,128]{1,0:T(8,128)S(1)}, f32[48,128]{1,0:T(8,128)S(1)}, u32[]{:S(2)}, u32[]{:S(2)}) %collective-permute-start.3) | collective-permute-done | bytes 24608 | tf_op jit(solution)/shard_map/ppermute | solution.py:524
  12.6 0.0 collective-permute-done.4
  12.6 0.0 collective-permute-done.1.refs_2_
  12.7 1.0 %strips.1 = (f32[88,128]{1,0:T(8,128)S(1)}, f32[88,128]{1,0:T(8,128)S(1)}) custom-call(s32[8,128]{1,0:T(8,128)S(1)} %get-tuple-element.32.refs_0_, s32[8,128]{1,0:T(8,128)S(1)} %collective-permute-done.5.refs_1_, f32[256,128]{1,0:T(8,128)S(1)} %broadcast_dynamic-update-slice_fusion.refs_2_), custom_call_target="tpu_custom_call" | custom-call | tf_op jit(solution)/shard_map/strips/pallas_call | solution.py:532
  13.7 0.3 %collective-permute-start.6 = (f32[1,1,5,8,1024]{4,3,2,1,0:T(8,128)S(1)}, f32[1,1,5,8,1024]{4,3,2,1,0:T(8,128)S(1)}, u32[]{:S(2)}, u32[]{:S(2)}) collective-permute-start(f32[1,1,5,8,1024]{4,3,2,1,0:T(8,128)S(1)} %collective-permute-done.1.refs_2_), channel_id=1, source_target_pairs={{0,2},{2,0},{4,6},{6,4},{1,3},{3,1},{5,7},{7,5},{8,10},{10,8},{12,... | collective-permute-start | bytes 491528 | tf_op jit(solution)/shard_map/ppermute | solution.py:550
  14.0 0.4 %collective-permute-start.8 = (f32[88,128]{1,0:T(8,128)S(1)}, f32[88,128]{1,0:T(8,128)S(1)}, u32[]{:S(2)}, u32[]{:S(2)}) collective-permute-start(f32[88,128]{1,0:T(8,128)S(1)} %get-tuple-element.45), channel_id=1, source_target_pairs={{0,4},{1,5},{2,6},{3,7},{4,0},{5,1},{6,2},{7,3},{8,12},{9,13},{10,... | collective-permute-start | bytes 135176 | tf_op jit(solution)/shard_map/ppermute | solution.py:557
  14.3 2.6 %collective-permute-start.7 = (f32[88,128]{1,0:T(8,128)S(1)}, f32[88,128]{1,0:T(8,128)S(1)}, u32[]{:S(2)}, u32[]{:S(2)}) collective-permute-start(f32[88,128]{1,0:T(8,128)S(1)} %get-tuple-element.44), channel_id=1, source_target_pairs={{0,5},{1,4},{2,7},{3,6},{4,1},{5,0},{6,3},{7,2},{8,13},{9,12},{10,... | collective-permute-start | bytes 135176 | tf_op jit(solution)/shard_map/ppermute | solution.py:557
  16.9 0.5 %collective-permute-start.9 = (f32[88,128]{1,0:T(8,128)S(1)}, f32[88,128]{1,0:T(8,128)S(1)}, u32[]{:S(2)}, u32[]{:S(2)}) collective-permute-start(f32[88,128]{1,0:T(8,128)S(1)} %get-tuple-element.44), channel_id=1, source_target_pairs={{0,1},{1,0},{2,3},{3,2},{4,5},{5,4},{6,7},{7,6},{8,9},{9,8},{10,11... | collective-permute-start | bytes 135176 | tf_op jit(solution)/shard_map/ppermute | solution.py:557
  17.4 0.0 collective-permute-done.refs_1_
  17.5 0.0 collective-permute-done.6.refs_3_
  17.5 1.1 %prepare.1 = (f32[2400,128]{1,0:T(8,128)S(1)}, f32[480,128]{1,0:T(8,128)S(1)}, f32[1600,128]{1,0:T(8,128)S(1)}, f32[1440,128]{1,0:T(8,128)S(1)}) custom-call(s32[104,128]{1,0:T(8,128)S(1)} %get-tuple-element.27.lanes_ref.refs_4_, f32[1,1,5,8,1024]{4,3,2,1,0:T(8,128)S(1)} %get-tuple-element.28.refs_0_, ...), custom_call_target="tpu_custom_call" | custom-call | flops 9830400 | bytes 1280000 | tf_op jit(solution)/shard_map/prepare/pallas_call | solution.py:565
  18.6 0.9 %collective-permute-done.7 = f32[88,128]{1,0:T(8,128)S(1)} collective-permute-done((f32[88,128]{1,0:T(8,128)S(1)}, f32[88,128]{1,0:T(8,128)S(1)}, u32[]{:S(2)}, u32[]{:S(2)}) %collective-permute-start.7) | collective-permute-done | bytes 45088 | tf_op jit(solution)/shard_map/ppermute | solution.py:557
  19.5 0.0 collective-permute-done.8
  19.5 1.5 %collective-permute-done.9 = f32[88,128]{1,0:T(8,128)S(1)} collective-permute-done((f32[88,128]{1,0:T(8,128)S(1)}, f32[88,128]{1,0:T(8,128)S(1)}, u32[]{:S(2)}, u32[]{:S(2)}) %collective-permute-start.9) | collective-permute-done | bytes 45088 | tf_op jit(solution)/shard_map/ppermute | solution.py:557
  21.0 0.1 maximum_select_fusion.refs_5_
  21.0 0.1 collective-permute-start.10
  21.1 1.2 %collective-permute-done.10.refs_6_ = f32[88,128]{1,0:T(8,128)S(1)} collective-permute-done((f32[88,128]{1,0:T(8,128)S(1)}, f32[88,128]{1,0:T(8,128)S(1)}, u32[]{:S(2)}, u32[]{:S(2)}) %collective-permute-start.10) | collective-permute-done | bytes 45088 | tf_op jit(solution)/shard_map/ppermute | solution.py:580
  22.3 2.8 %step.1 = f32[1,1,5,16,1024]{4,3,2,1,0:T(8,128)} custom-call(f32[2400,128]{1,0:T(8,128)S(1)} %get-tuple-element.40.refs_0_, f32[480,128]{1,0:T(8,128)S(1)} %get-tuple-element.41.refs_1_, f32[1600,128]{1,0:T(8,128)S(1)} %get-tuple-element.42.refs_2_, f32[1440,128]{1,0:T(8,128)S(1)} %get-tuple-element.43.refs_3_, ...), custom_call_target="tpu_custom_call" | custom-call | tf_op jit(solution)/shard_map/step/pallas_call | solution.py:587
  (6 shorter events, 0.0 us)
Async XLA Ops:
  1.2 11.4 %collective-permute-start.1 = (f32[1,1,5,8,1024]{4,3,2,1,0:T(8,128)S(1)}, f32[1,1,5,8,1024]{4,3,2,1,0:T(8,128)S(1)}, u32[]{:S(2)}, u32[]{:S(2)}) collective-permute-start(f32[1,1,5,8,1024]{4,3,2,1,0:T(8,128)S(1)} %get-tuple-element.28.refs_0_), channel_id=1, source_target_pairs={{0,4},{2,6},{4,0},{6,2},{1,5},{3,7},{5,1},{7,3},{8,12},{10,14},{12... | collective-permute-start | bytes 491528 | tf_op jit(solution)/shard_map/ppermute | solution.py:527
  4.3 8.0 %collective-permute-start.2 = (f32[48,128]{1,0:T(8,128)S(1)}, f32[48,128]{1,0:T(8,128)S(1)}, u32[]{:S(2)}, u32[]{:S(2)}) collective-permute-start(f32[48,128]{1,0:T(8,128)S(1)} %get-tuple-element.34), channel_id=1, source_target_pairs={{0,24},{8,16},{16,8},{24,0},{1,25},{9,17},{17,9},{25,1},{2,26},{10... | collective-permute-start | bytes 73736 | tf_op jit(solution)/shard_map/ppermute | solution.py:524
  7.9 4.7 %collective-permute-start.3 = (f32[48,128]{1,0:T(8,128)S(1)}, f32[48,128]{1,0:T(8,128)S(1)}, u32[]{:S(2)}, u32[]{:S(2)}) collective-permute-start(f32[48,128]{1,0:T(8,128)S(1)} %get-tuple-element.34), channel_id=1, source_target_pairs={{0,16},{8,24},{16,0},{24,8},{1,17},{9,25},{17,1},{25,9},{2,18},{10... | collective-permute-start | bytes 73736 | tf_op jit(solution)/shard_map/ppermute | solution.py:524
  7.9 4.7 %collective-permute-start.4 = (f32[48,128]{1,0:T(8,128)S(1)}, f32[48,128]{1,0:T(8,128)S(1)}, u32[]{:S(2)}, u32[]{:S(2)}) collective-permute-start(f32[48,128]{1,0:T(8,128)S(1)} %get-tuple-element.34), channel_id=1, source_target_pairs={{0,8},{8,0},{16,24},{24,16},{1,9},{9,1},{17,25},{25,17},{2,10},{10... | collective-permute-start | bytes 73736 | tf_op jit(solution)/shard_map/ppermute | solution.py:524
  8.7 3.6 %collective-permute-start.5 = (s32[8,128]{1,0:T(8,128)S(1)}, s32[8,128]{1,0:T(8,128)S(1)}, u32[]{:S(2)}, u32[]{:S(2)}) collective-permute-start(s32[8,128]{1,0:T(8,128)S(1)} %get-tuple-element.30), channel_id=1, source_target_pairs={{0,1},{1,0},{2,3},{3,2},{4,5},{5,4},{6,7},{7,6},{8,9},{9,8},{10,11... | collective-permute-start | bytes 12296 | tf_op jit(solution)/shard_map/ppermute | solution.py:525
  12.3 5.2 %collective-permute-start = (f32[1,1,5,8,1024]{4,3,2,1,0:T(8,128)S(1)}, f32[1,1,5,8,1024]{4,3,2,1,0:T(8,128)S(1)}, u32[]{:S(2)}, u32[]{:S(2)}) collective-permute-start(f32[1,1,5,8,1024]{4,3,2,1,0:T(8,128)S(1)} %get-tuple-element.28.refs_0_), channel_id=1, source_target_pairs={{0,2},{2,0},{4,6},{6,4},{1,3},{3,1},{5,7},{7,5},{8,10},{10,8},{12,... | collective-permute-start | bytes 491528 | tf_op jit(solution)/shard_map/ppermute | solution.py:550
  13.7 3.8 %collective-permute-start.6 = (f32[1,1,5,8,1024]{4,3,2,1,0:T(8,128)S(1)}, f32[1,1,5,8,1024]{4,3,2,1,0:T(8,128)S(1)}, u32[]{:S(2)}, u32[]{:S(2)}) collective-permute-start(f32[1,1,5,8,1024]{4,3,2,1,0:T(8,128)S(1)} %collective-permute-done.1.refs_2_), channel_id=1, source_target_pairs={{0,2},{2,0},{4,6},{6,4},{1,3},{3,1},{5,7},{7,5},{8,10},{10,8},{12,... | collective-permute-start | bytes 491528 | tf_op jit(solution)/shard_map/ppermute | solution.py:550
  14.0 5.5 %collective-permute-start.8 = (f32[88,128]{1,0:T(8,128)S(1)}, f32[88,128]{1,0:T(8,128)S(1)}, u32[]{:S(2)}, u32[]{:S(2)}) collective-permute-start(f32[88,128]{1,0:T(8,128)S(1)} %get-tuple-element.45), channel_id=1, source_target_pairs={{0,4},{1,5},{2,6},{3,7},{4,0},{5,1},{6,2},{7,3},{8,12},{9,13},{10,... | collective-permute-start | bytes 135176 | tf_op jit(solution)/shard_map/ppermute | solution.py:557
  14.3 5.1 %collective-permute-start.7 = (f32[88,128]{1,0:T(8,128)S(1)}, f32[88,128]{1,0:T(8,128)S(1)}, u32[]{:S(2)}, u32[]{:S(2)}) collective-permute-start(f32[88,128]{1,0:T(8,128)S(1)} %get-tuple-element.44), channel_id=1, source_target_pairs={{0,5},{1,4},{2,7},{3,6},{4,1},{5,0},{6,3},{7,2},{8,13},{9,12},{10,... | collective-permute-start | bytes 135176 | tf_op jit(solution)/shard_map/ppermute | solution.py:557
  16.9 4.0 %collective-permute-start.9 = (f32[88,128]{1,0:T(8,128)S(1)}, f32[88,128]{1,0:T(8,128)S(1)}, u32[]{:S(2)}, u32[]{:S(2)}) collective-permute-start(f32[88,128]{1,0:T(8,128)S(1)} %get-tuple-element.44), channel_id=1, source_target_pairs={{0,1},{1,0},{2,3},{3,2},{4,5},{5,4},{6,7},{7,6},{8,9},{9,8},{10,11... | collective-permute-start | bytes 135176 | tf_op jit(solution)/shard_map/ppermute | solution.py:557
  21.0 1.3 %collective-permute-start.10 = (f32[88,128]{1,0:T(8,128)S(1)}, f32[88,128]{1,0:T(8,128)S(1)}, u32[]{:S(2)}, u32[]{:S(2)}) collective-permute-start(f32[88,128]{1,0:T(8,128)S(1)} %maximum_select_fusion.refs_5_), channel_id=1, source_target_pairs={{0,2},{2,0},{4,6},{6,4},{1,3},{3,1},{5,7},{7,5},{8,10},{10,8},{12,... | collective-permute-start | bytes 135176 | tf_op jit(solution)/shard_map/ppermute | solution.py:580

commit v11 on v8

--- a/solution.py
+++ b/solution.py
@@ -546,7 +546,7 @@
             have = have + [k ^ mask for k in have]
         return blocks
 
-    raws = to_group(raw, strips[0])
+    raws = to_group(raw, strips[-1])
 
     shares = [strips[0]]
     for k in reversed(range(1, n_gz * group)):

time: 25 us -> 25.1 us (level)
  transfers between devices with their start and end apart: 11 -> 11, of which waited for: 4 -> 5; matrix products, arithmetic and copies ran while one was open for 0% -> 0% of each run, Pallas kernels for 9% -> 9%
where the time goes in v11:
time: 25.1 us; the launch traced here: 24.9 us
  starting transfers between devices  12.7 us (51%)
  Pallas kernels  6.16 us (25%)
  waiting for transfers between devices  5.92 us (24%)
    ppermute x3, starting transfers between devices, per_device(): boxes = [payload] + [lax.ppermute(payload, 'gx', perm) for perm in perms]  5.68 us
    ppermute x3, starting transfers between devices, per_device(): shares.append(lax.ppermute(strips[k % n_gz], ('gy', 'gz'), perm))  3.55 us
    pallas_call x1, Pallas kernels, per_device(): pl.pallas_call(functools.partial(step_kernel, count, patches, slots), out...  2.78 us
    ppermute x3, waiting for transfers between devices, per_device(): shares.append(lax.ppermute(strips[k % n_gz], ('gy', 'gz'), perm))  2.39 us
    ppermute x3, waiting for transfers between devices, per_device(): boxes = [payload] + [lax.ppermute(payload, 'gx', perm) for perm in perms]  2.31 us
    ppermute x3, starting transfers between devices, to_group(): blocks[k ^ mask] = lax.ppermute(block, 'gy', perm)  1.81 us
    ppermute x1, starting transfers between devices, per_device(): lax.ppermute(cuts[k], 'gz', [(i, i ^ k) for i in range(n_gz)])  1.56 us
    pallas_call x1, Pallas kernels, per_device(): pl.pallas_call(functools.partial(pack_kernel, tiles, rows, group, count,...  1.23 us
  transfers between devices with their start and end apart: 11, of which 5 were waited for; matrix products, arithmetic and copies ran while one was open for 0% of the time, Pallas kernels for 9%

profile of v11, /device:TPU:0, one launch (start us, length us, event | category | flops | bytes accessed | tf_op | source)
XLA Modules:
  0.0 24.9 jit_solution(3299521510637944452)
XLA Ops:
  0.0 1.2 %pack.1 = (f32[48,128]{1,0:T(8,128)S(1)}, f32[1,1,5,8,1024]{4,3,2,1,0:T(8,128)S(1)}, s32[104,128]{1,0:T(8,128)S(1)}, s32[8,128]{1,0:T(8,128)S(1)}, s32[8,128]{1,0:T(8,128)S(1)}) custom-call(s32[1,1,1,32]{3,2,1,0:T(1,128)} %bitcast.12, s32[1,1,4,32]{3,2,1,0:T(4,128)} %bitcast.9, s32[1,1,4,32]{3,2,1,0:T(4,128)} %bitcast.10, s32[1,1,4,32]{3,2,1,0:T(4,128)} %bitcast.11, ...), custom_call_target="tpu_custom_call" | custom-call | tf_op jit(solution)/shard_map/pack/pallas_call | solution.py:498
  1.2 3.1 %collective-permute-start.3 = (f32[48,128]{1,0:T(8,128)S(1)}, f32[48,128]{1,0:T(8,128)S(1)}, u32[]{:S(2)}, u32[]{:S(2)}) collective-permute-start(f32[48,128]{1,0:T(8,128)S(1)} %get-tuple-element.25), channel_id=1, source_target_pairs={{0,8},{8,0},{16,24},{24,16},{1,9},{9,1},{17,25},{25,17},{2,10},{10... | collective-permute-start | bytes 73736 | tf_op jit(solution)/shard_map/ppermute | solution.py:523
  4.3 2.6 %collective-permute-start.4 = (f32[48,128]{1,0:T(8,128)S(1)}, f32[48,128]{1,0:T(8,128)S(1)}, u32[]{:S(2)}, u32[]{:S(2)}) collective-permute-start(f32[48,128]{1,0:T(8,128)S(1)} %get-tuple-element.25), channel_id=1, source_target_pairs={{0,16},{8,24},{16,0},{24,8},{1,17},{9,25},{17,1},{25,9},{2,18},{10... | collective-permute-start | bytes 73736 | tf_op jit(solution)/shard_map/ppermute | solution.py:523
  6.9 0.0 collective-permute-start.5
  6.9 1.7 %collective-permute-start.1 = (f32[1,1,5,8,1024]{4,3,2,1,0:T(8,128)S(1)}, f32[1,1,5,8,1024]{4,3,2,1,0:T(8,128)S(1)}, u32[]{:S(2)}, u32[]{:S(2)}) collective-permute-start(f32[1,1,5,8,1024]{4,3,2,1,0:T(8,128)S(1)} %get-tuple-element.22.refs_0_), channel_id=1, source_target_pairs={{0,4},{2,6},{4,0},{6,2},{1,5},{3,7},{5,1},{7,3},{8,12},{10,14},{12... | collective-permute-start | bytes 491528 | tf_op jit(solution)/shard_map/ppermute | solution.py:545
  8.7 0.0 collective-permute-start
  8.7 0.0 collective-permute-done.3
  8.7 1.6 %collective-permute-start.2 = (s32[8,128]{1,0:T(8,128)S(1)}, s32[8,128]{1,0:T(8,128)S(1)}, u32[]{:S(2)}, u32[]{:S(2)}) collective-permute-start(s32[8,128]{1,0:T(8,128)S(1)} %get-tuple-element.24), channel_id=1, source_target_pairs={{0,1},{1,0},{2,3},{3,2},{4,5},{5,4},{6,7},{7,6},{8,9},{9,8},{10,11... | collective-permute-start | bytes 12296 | tf_op jit(solution)/shard_map/ppermute | solution.py:525
  10.2 0.0 collective-permute-done.4
  10.2 2.3 %collective-permute-done.5 = f32[48,128]{1,0:T(8,128)S(1)} collective-permute-done((f32[48,128]{1,0:T(8,128)S(1)}, f32[48,128]{1,0:T(8,128)S(1)}, u32[]{:S(2)}, u32[]{:S(2)}) %collective-permute-start.5) | collective-permute-done | bytes 24608 | tf_op jit(solution)/shard_map/ppermute | solution.py:523
  12.5 0.0 collective-permute-done.2.refs_1_
  12.6 1.0 %strips.1 = (f32[88,128]{1,0:T(8,128)S(1)}, f32[88,128]{1,0:T(8,128)S(1)}) custom-call(s32[8,128]{1,0:T(8,128)S(1)} %get-tuple-element.23.refs_0_, s32[8,128]{1,0:T(8,128)S(1)} %collective-permute-done.2.refs_1_, f32[256,128]{1,0:T(8,128)S(1)} %broadcast_dynamic-update-slice_fusion.refs_2_), custom_call_target="tpu_custom_call" | custom-call | tf_op jit(solution)/shard_map/strips/pallas_call | solution.py:527
  13.6 0.0 collective-permute-done.1.refs_2_
  13.6 0.1 collective-permute-start.6
  13.7 2.5 %collective-permute-start.7 = (f32[88,128]{1,0:T(8,128)S(1)}, f32[88,128]{1,0:T(8,128)S(1)}, u32[]{:S(2)}, u32[]{:S(2)}) collective-permute-start(f32[88,128]{1,0:T(8,128)S(1)} %get-tuple-element.26), channel_id=1, source_target_pairs={{0,5},{1,4},{2,7},{3,6},{4,1},{5,0},{6,3},{7,2},{8,13},{9,12},{10,... | collective-permute-start | bytes 135176 | tf_op jit(solution)/shard_map/ppermute | solution.py:555
  16.2 0.5 %collective-permute-start.9 = (f32[88,128]{1,0:T(8,128)S(1)}, f32[88,128]{1,0:T(8,128)S(1)}, u32[]{:S(2)}, u32[]{:S(2)}) collective-permute-start(f32[88,128]{1,0:T(8,128)S(1)} %get-tuple-element.26), channel_id=1, source_target_pairs={{0,1},{1,0},{2,3},{3,2},{4,5},{5,4},{6,7},{7,6},{8,9},{9,8},{10,11... | collective-permute-start | bytes 135176 | tf_op jit(solution)/shard_map/ppermute | solution.py:555
  16.7 0.5 %collective-permute-start.8 = (f32[88,128]{1,0:T(8,128)S(1)}, f32[88,128]{1,0:T(8,128)S(1)}, u32[]{:S(2)}, u32[]{:S(2)}) collective-permute-start(f32[88,128]{1,0:T(8,128)S(1)} %get-tuple-element.33), channel_id=1, source_target_pairs={{0,4},{1,5},{2,6},{3,7},{4,0},{5,1},{6,2},{7,3},{8,12},{9,13},{10,... | collective-permute-start | bytes 135176 | tf_op jit(solution)/shard_map/ppermute | solution.py:555
  17.2 0.0 collective-permute-done.refs_1_
  17.2 0.0 collective-permute-done.6.refs_3_
  17.2 1.1 %prepare.1 = (f32[2400,128]{1,0:T(8,128)S(1)}, f32[480,128]{1,0:T(8,128)S(1)}, f32[1600,128]{1,0:T(8,128)S(1)}, f32[1440,128]{1,0:T(8,128)S(1)}) custom-call(s32[104,128]{1,0:T(8,128)S(1)} %get-tuple-element.21.lanes_ref.refs_4_, f32[1,1,5,8,1024]{4,3,2,1,0:T(8,128)S(1)} %get-tuple-element.22.refs_0_, ...), custom_call_target="tpu_custom_call" | custom-call | flops 9830400 | bytes 1280000 | tf_op jit(solution)/shard_map/prepare/pallas_call | solution.py:563
  18.4 0.3 %collective-permute-done.7 = f32[88,128]{1,0:T(8,128)S(1)} collective-permute-done((f32[88,128]{1,0:T(8,128)S(1)}, f32[88,128]{1,0:T(8,128)S(1)}, u32[]{:S(2)}, u32[]{:S(2)}) %collective-permute-start.7) | collective-permute-done | bytes 45088 | tf_op jit(solution)/shard_map/ppermute | solution.py:555
  18.7 1.5 %collective-permute-done.9 = f32[88,128]{1,0:T(8,128)S(1)} collective-permute-done((f32[88,128]{1,0:T(8,128)S(1)}, f32[88,128]{1,0:T(8,128)S(1)}, u32[]{:S(2)}, u32[]{:S(2)}) %collective-permute-start.9) | collective-permute-done | bytes 45088 | tf_op jit(solution)/shard_map/ppermute | solution.py:555
  20.2 0.5 %collective-permute-done.8 = f32[88,128]{1,0:T(8,128)S(1)} collective-permute-done((f32[88,128]{1,0:T(8,128)S(1)}, f32[88,128]{1,0:T(8,128)S(1)}, u32[]{:S(2)}, u32[]{:S(2)}) %collective-permute-start.8) | collective-permute-done | bytes 45088 | tf_op jit(solution)/shard_map/ppermute | solution.py:555
  20.8 0.1 maximum_select_fusion.refs_5_
  20.9 0.1 collective-permute-start.10
  20.9 1.2 %collective-permute-done.10.refs_6_ = f32[88,128]{1,0:T(8,128)S(1)} collective-permute-done((f32[88,128]{1,0:T(8,128)S(1)}, f32[88,128]{1,0:T(8,128)S(1)}, u32[]{:S(2)}, u32[]{:S(2)}) %collective-permute-start.10) | collective-permute-done | bytes 45088 | tf_op jit(solution)/shard_map/ppermute | solution.py:578
  22.1 2.8 %step.1 = f32[1,1,5,16,1024]{4,3,2,1,0:T(8,128)} custom-call(f32[2400,128]{1,0:T(8,128)S(1)} %get-tuple-element.28.refs_0_, f32[480,128]{1,0:T(8,128)S(1)} %get-tuple-element.29.refs_1_, f32[1600,128]{1,0:T(8,128)S(1)} %get-tuple-element.30.refs_2_, f32[1440,128]{1,0:T(8,128)S(1)} %get-tuple-element.31.refs_3_, ...), custom_call_target="tpu_custom_call" | custom-call | tf_op jit(solution)/shard_map/step/pallas_call | solution.py:585
  (6 shorter events, 0.0 us)
Async XLA Ops:
  1.2 7.4 %collective-permute-start.3 = (f32[48,128]{1,0:T(8,128)S(1)}, f32[48,128]{1,0:T(8,128)S(1)}, u32[]{:S(2)}, u32[]{:S(2)}) collective-permute-start(f32[48,128]{1,0:T(8,128)S(1)} %get-tuple-element.25), channel_id=1, source_target_pairs={{0,8},{8,0},{16,24},{24,16},{1,9},{9,1},{17,25},{25,17},{2,10},{10... | collective-permute-start | bytes 73736 | tf_op jit(solution)/shard_map/ppermute | solution.py:523
  4.3 5.9 %collective-permute-start.4 = (f32[48,128]{1,0:T(8,128)S(1)}, f32[48,128]{1,0:T(8,128)S(1)}, u32[]{:S(2)}, u32[]{:S(2)}) collective-permute-start(f32[48,128]{1,0:T(8,128)S(1)} %get-tuple-element.25), channel_id=1, source_target_pairs={{0,16},{8,24},{16,0},{24,8},{1,17},{9,25},{17,1},{25,9},{2,18},{10... | collective-permute-start | bytes 73736 | tf_op jit(solution)/shard_map/ppermute | solution.py:523
  6.9 5.6 %collective-permute-start.5 = (f32[48,128]{1,0:T(8,128)S(1)}, f32[48,128]{1,0:T(8,128)S(1)}, u32[]{:S(2)}, u32[]{:S(2)}) collective-permute-start(f32[48,128]{1,0:T(8,128)S(1)} %get-tuple-element.25), channel_id=1, source_target_pairs={{0,24},{8,16},{16,8},{24,0},{1,25},{9,17},{17,9},{25,1},{2,26},{10... | collective-permute-start | bytes 73736 | tf_op jit(solution)/shard_map/ppermute | solution.py:523
  6.9 6.7 %collective-permute-start.1 = (f32[1,1,5,8,1024]{4,3,2,1,0:T(8,128)S(1)}, f32[1,1,5,8,1024]{4,3,2,1,0:T(8,128)S(1)}, u32[]{:S(2)}, u32[]{:S(2)}) collective-permute-start(f32[1,1,5,8,1024]{4,3,2,1,0:T(8,128)S(1)} %get-tuple-element.22.refs_0_), channel_id=1, source_target_pairs={{0,4},{2,6},{4,0},{6,2},{1,5},{3,7},{5,1},{7,3},{8,12},{10,14},{12... | collective-permute-start | bytes 491528 | tf_op jit(solution)/shard_map/ppermute | solution.py:545
  8.7 8.6 %collective-permute-start = (f32[1,1,5,8,1024]{4,3,2,1,0:T(8,128)S(1)}, f32[1,1,5,8,1024]{4,3,2,1,0:T(8,128)S(1)}, u32[]{:S(2)}, u32[]{:S(2)}) collective-permute-start(f32[1,1,5,8,1024]{4,3,2,1,0:T(8,128)S(1)} %get-tuple-element.22.refs_0_), channel_id=1, source_target_pairs={{0,2},{2,0},{4,6},{6,4},{1,3},{3,1},{5,7},{7,5},{8,10},{10,8},{12,... | collective-permute-start | bytes 491528 | tf_op jit(solution)/shard_map/ppermute | solution.py:545
  8.7 3.9 %collective-permute-start.2 = (s32[8,128]{1,0:T(8,128)S(1)}, s32[8,128]{1,0:T(8,128)S(1)}, u32[]{:S(2)}, u32[]{:S(2)}) collective-permute-start(s32[8,128]{1,0:T(8,128)S(1)} %get-tuple-element.24), channel_id=1, source_target_pairs={{0,1},{1,0},{2,3},{3,2},{4,5},{5,4},{6,7},{7,6},{8,9},{9,8},{10,11... | collective-permute-start | bytes 12296 | tf_op jit(solution)/shard_map/ppermute | solution.py:525
  13.6 3.6 %collective-permute-start.6 = (f32[1,1,5,8,1024]{4,3,2,1,0:T(8,128)S(1)}, f32[1,1,5,8,1024]{4,3,2,1,0:T(8,128)S(1)}, u32[]{:S(2)}, u32[]{:S(2)}) collective-permute-start(f32[1,1,5,8,1024]{4,3,2,1,0:T(8,128)S(1)} %collective-permute-done.1.refs_2_), channel_id=1, source_target_pairs={{0,2},{2,0},{4,6},{6,4},{1,3},{3,1},{5,7},{7,5},{8,10},{10,8},{12,... | collective-permute-start | bytes 491528 | tf_op jit(solution)/shard_map/ppermute | solution.py:545
  13.7 5.0 %collective-permute-start.7 = (f32[88,128]{1,0:T(8,128)S(1)}, f32[88,128]{1,0:T(8,128)S(1)}, u32[]{:S(2)}, u32[]{:S(2)}) collective-permute-start(f32[88,128]{1,0:T(8,128)S(1)} %get-tuple-element.26), channel_id=1, source_target_pairs={{0,5},{1,4},{2,7},{3,6},{4,1},{5,0},{6,3},{7,2},{8,13},{9,12},{10,... | collective-permute-start | bytes 135176 | tf_op jit(solution)/shard_map/ppermute | solution.py:555
  16.2 4.0 %collective-permute-start.9 = (f32[88,128]{1,0:T(8,128)S(1)}, f32[88,128]{1,0:T(8,128)S(1)}, u32[]{:S(2)}, u32[]{:S(2)}) collective-permute-start(f32[88,128]{1,0:T(8,128)S(1)} %get-tuple-element.26), channel_id=1, source_target_pairs={{0,1},{1,0},{2,3},{3,2},{4,5},{5,4},{6,7},{7,6},{8,9},{9,8},{10,11... | collective-permute-start | bytes 135176 | tf_op jit(solution)/shard_map/ppermute | solution.py:555
  16.7 4.0 %collective-permute-start.8 = (f32[88,128]{1,0:T(8,128)S(1)}, f32[88,128]{1,0:T(8,128)S(1)}, u32[]{:S(2)}, u32[]{:S(2)}) collective-permute-start(f32[88,128]{1,0:T(8,128)S(1)} %get-tuple-element.33), channel_id=1, source_target_pairs={{0,4},{1,5},{2,6},{3,7},{4,0},{5,1},{6,2},{7,3},{8,12},{9,13},{10,... | collective-permute-start | bytes 135176 | tf_op jit(solution)/shard_map/ppermute | solution.py:555
  20.9 1.3 %collective-permute-start.10 = (f32[88,128]{1,0:T(8,128)S(1)}, f32[88,128]{1,0:T(8,128)S(1)}, u32[]{:S(2)}, u32[]{:S(2)}) collective-permute-start(f32[88,128]{1,0:T(8,128)S(1)} %maximum_select_fusion.refs_5_), channel_id=1, source_target_pairs={{0,2},{2,0},{4,6},{6,4},{1,3},{3,1},{5,7},{7,5},{8,10},{10,8},{12,... | collective-permute-start | bytes 135176 | tf_op jit(solution)/shard_map/ppermute | solution.py:578
